TPU v7x, 512 devices: a whole 4x4x16 slice. The times are simulated.
512 devices in a mesh: pipe: 16 (over z_hi, y, core), expert: 32 (over z_lo, x).
Axes of the slice: x: 4, y: 4, z: 16 (z_hi: 2, z_lo: 8; z = z_hi * 8 + z_lo), core: 2. Of those that a mesh axis runs over, the one named last changes fastest.
Arguments:
- act_down: bfloat16 [16, 512, 3584], P('pipe', 'expert'), may hold values from -6 to 6
- act_up: bfloat16 [16, 512, 3584], P('pipe', 'expert'), may hold values from -6 to 6
- routes_down: int32 [16, 512, 2], P('pipe', 'expert'), may hold values from 0 to 3, all different within a row; in each aligned block of 16 rows (0 to 15, 16 to 31, ..., all dimensions but the last counted through in order) at most 12 rows name the same one
- routes_up: int32 [16, 512, 2], P('pipe', 'expert'), may hold values from 0 to 3, all different within a row; in each aligned block of 16 rows (0 to 15, 16 to 31, ..., all dimensions but the last counted through in order) at most 12 rows name the same one
- norm_gain: float32 [16, 3584], P('pipe'), may hold values from 0.5 to 1.5
- router_w: bfloat16 [16, 3584, 4], P('pipe'), may hold values from -0.09375 to 0.09375
- w_gate: bfloat16 [16, 3584, 4096], P('pipe', None, 'expert'), may hold values from -0.09375 to 0.09375
- w_up: bfloat16 [16, 3584, 4096], P('pipe', None, 'expert'), may hold values from -0.09375 to 0.09375
- w_down: bfloat16 [16, 4096, 3584], P('pipe', 'expert'), may hold values from -0.1875 to 0.1875
Outputs:
- next_down: bfloat16 [16, 512, 3584], P('pipe', 'expert')
- next_up: bfloat16 [16, 512, 3584], P('pipe', 'expert')
Inputs may be any that keep to these rules, and one draw needn't show every extreme that they name: `routes_down`: each token names 2 different experts. In each aligned block of 16 tokens (the tokens of one device) no expert is named by more than 12 tokens, a bound that some block reaches. `routes_up`: as for routes_down.
All inputs are finite; a program needn't handle non-finite values.
Results may differ from a plain program's by a relative error of at most 0.006.
Values may be sent and summed in bfloat16 or wider, within the bound.
No kernel may reach another device: no remote copies, remote signals or barrier semaphores. Data moves between devices by JAX's collectives and lax.ppermute only.
A program may use at most 64 MiB of HBM per device.

v0:
```python
import jax
import jax.numpy as jnp
from jax import lax
from jax.sharding import PartitionSpec as P

CAP = 12


route_scale = 2.5


def shifted(block, axis, distance):
    devices = range(lax.axis_size(axis))
    route = [((i - distance) % len(devices), i) for i in devices]
    return lax.ppermute(block, axis, route)


def prepare(x, routes, gain, router):
    xf = x.astype(jnp.float32)
    mean_sq = jnp.mean(xf * xf, axis=-1, keepdims=True)
    normed = (xf * lax.rsqrt(mean_sq + 1e-06) * gain).astype(jnp.bfloat16)
    logits = jnp.dot(normed, router, preferred_element_type=jnp.float32)
    affinity = jax.nn.sigmoid(logits)
    picked = jnp.take_along_axis(affinity, routes, axis=1)
    weights = picked / jnp.sum(picked, axis=1, keepdims=True) * route_scale
    num_rows, choose = routes.shape
    experts_n = router.shape[1]
    flat_ids = routes.reshape(-1)
    onehot = (flat_ids[:, None] == jnp.arange(experts_n, dtype=jnp.int32)[None, :]).astype(
        jnp.int32
    )
    before = jnp.cumsum(onehot, axis=0) - onehot
    slot = jnp.sum(before * onehot, axis=1)
    column = flat_ids * CAP + slot
    select = column[:, None] == jnp.arange(experts_n * CAP, dtype=jnp.int32)[None, :]
    paired = jnp.repeat(normed, choose, axis=0)
    packed = lax.dot_general(
        select.astype(jnp.bfloat16),
        paired,
        (((0,), (0,)), ((), ())),
        preferred_element_type=jnp.float32,
    ).astype(jnp.bfloat16)
    combine = jnp.sum(
        (select.astype(jnp.float32) * weights.reshape(-1)[:, None]).reshape(
            num_rows, choose, experts_n * CAP
        ),
        axis=1,
    )
    return (xf, packed, combine)


def spread_copies(packed, experts_n, group):
    width = packed.shape[1]
    copies = jnp.broadcast_to(
        packed.reshape(experts_n, 1, CAP, width), (experts_n, group, CAP, width)
    )
    return copies.reshape(experts_n * group, CAP, width)


def expert_piece(received, both_cols, down_rows):
    width = received.shape[2]
    hidden_n = down_rows.shape[0]
    rows = received.reshape(-1, width)
    joined = jnp.dot(rows, both_cols, preferred_element_type=jnp.float32)
    hidden = (jax.nn.silu(joined[:, :hidden_n]) * joined[:, hidden_n:]).astype(jnp.bfloat16)
    piece = jnp.dot(hidden, down_rows, preferred_element_type=jnp.float32).astype(jnp.bfloat16)
    return piece.reshape(received.shape)


def finish(xf, combine, returned, experts_n, group):
    width = returned.shape[2]
    summed = jnp.sum(returned.reshape(experts_n, group, CAP, width), axis=1, dtype=jnp.float32)
    expert_out = summed.reshape(experts_n * CAP, width)
    mixed = jnp.dot(
        combine, expert_out, precision=lax.Precision.HIGHEST, preferred_element_type=jnp.float32
    )
    return (xf + mixed).astype(jnp.bfloat16)


def on_device(act_down, act_up, routes_down, routes_up, norm_gain, router_w, w_gate, w_up, w_down):
    devices_n = lax.axis_size("expert")
    experts_n = router_w.shape[2]
    group = devices_n // experts_n
    gain = norm_gain[0]
    router = router_w[0]
    both_cols = jnp.concatenate([w_gate[0], w_up[0]], axis=1)
    down_rows = w_down[0]
    xf_down, packed_down, combine_down = prepare(act_down[0], routes_down[0], gain, router)
    xf_up, packed_up, combine_up = prepare(act_up[0], routes_up[0], gain, router)
    send_down = spread_copies(packed_down, experts_n, group)
    send_up = spread_copies(packed_up, experts_n, group)

    def one_span(received):
        piece = expert_piece(received, both_cols, down_rows)
        return lax.all_to_all(piece, "expert", split_axis=0, concat_axis=0, tiled=True)

    def dispatch(send):
        return one_span(lax.all_to_all(send, "expert", split_axis=0, concat_axis=0, tiled=True))

    back_down = dispatch(send_down)
    back_up = dispatch(send_up)
    out_down = finish(xf_down, combine_down, back_down, experts_n, group)
    out_up = finish(xf_up, combine_up, back_up, experts_n, group)
    next_down = shifted(out_down[None], "pipe", 1)
    next_up = shifted(out_up[None], "pipe", -1)
    return (next_down, next_up)


def solution(mesh):
    placed = (
        P("pipe", "expert", None),
        P("pipe", "expert", None),
        P("pipe", "expert", None),
        P("pipe", "expert", None),
        P("pipe", None),
        P("pipe", None, None),
        P("pipe", None, "expert"),
        P("pipe", None, "expert"),
        P("pipe", "expert", None),
    )
    return jax.shard_map(
        on_device,
        mesh=mesh,
        in_specs=placed,
        out_specs=(P("pipe", "expert", None), P("pipe", "expert", None)),
        check_vma=False,
    )
```

profile of v0, /device:TPU:6, one launch (start us, length us, event | category | flops | bytes accessed | tf_op | source)
XLA Modules:
  0.0 731.6 jit_solution(621257449381552175)
XLA Ops:
  0.6 1.1 fusion.18
  1.8 1.0 fusion.23
  2.8 0.8 copy.39
  4.0 0.8 reduce
  4.8 1.1 fusion.25
  6.5 2.2 broadcast_in_dim.45
  8.7 15.8 %all-to-all-start.2 = ((bf16[32,12,3584]{2,1,0:T(8,128)(2,1)}), bf16[32,12,3584]{2,1,0:T(8,128)(2,1)}, u32[]{:S(2)}, u32[]{:S(2)}) async-start(bf16[32,12,3584]{2,1,0:T(8,128)(2,1)} %bitcast.94), calls=%async_computation.2 | async-start | bytes 7340032 | tf_op jit(solution)/shard_map/all_to_all | solution.py:98
  25.7 161.8 %all-to-all-done.2 = bf16[32,12,3584]{2,1,0:T(8,128)(2,1)} async-done(((bf16[32,12,3584]{2,1,0:T(8,128)(2,1)}), bf16[32,12,3584]{2,1,0:T(8,128)(2,1)}, u32[]{:S(2)}, u32[]{:S(2)}) %all-to-all-start.2) | async-done | bytes 2752544 | tf_op jit(solution)/shard_map/all_to_all | solution.py:98
  187.6 2.3 broadcast_in_dim.21
  189.9 7.8 %all-to-all-start = ((bf16[32,12,3584]{2,1,0:T(8,128)(2,1)}), bf16[32,12,3584]{2,1,0:T(8,128)(2,1)}, u32[]{:S(2)}, u32[]{:S(2)}) async-start(bf16[32,12,3584]{2,1,0:T(8,128)(2,1)} %bitcast.95), calls=%async_computation | async-start | bytes 7340032 | tf_op jit(solution)/shard_map/all_to_all | solution.py:98
  197.7 5.4 reshape.161
  203.0 3.2 fusion.4
  206.2 2.5 convolution_convert_fusion
  208.7 5.3 reshape.162
  214.0 146.8 %all-to-all-done = bf16[32,12,3584]{2,1,0:T(8,128)(2,1)} async-done(((bf16[32,12,3584]{2,1,0:T(8,128)(2,1)}), bf16[32,12,3584]{2,1,0:T(8,128)(2,1)}, u32[]{:S(2)}, u32[]{:S(2)}) %all-to-all-start) | async-done | bytes 2752544 | tf_op jit(solution)/shard_map/all_to_all | solution.py:98
  360.8 7.8 %all-to-all-start.3 = ((bf16[32,12,3584]{2,1,0:T(8,128)(2,1)}), bf16[32,12,3584]{2,1,0:T(8,128)(2,1)}, u32[]{:S(2)}, u32[]{:S(2)}) async-start(bf16[32,12,3584]{2,1,0:T(8,128)(2,1)} %reshape.162), calls=%async_computation.3 | async-start | bytes 7340032 | tf_op jit(solution)/shard_map/all_to_all | solution.py:95
  368.6 5.4 reshape.156
  374.0 3.2 fusion.5
  377.1 2.5 convolution_convert_fusion.1
  379.7 5.3 reshape.157
  385.0 146.8 %all-to-all-done.3 = bf16[32,12,3584]{2,1,0:T(8,128)(2,1)} async-done(((bf16[32,12,3584]{2,1,0:T(8,128)(2,1)}), bf16[32,12,3584]{2,1,0:T(8,128)(2,1)}, u32[]{:S(2)}, u32[]{:S(2)}) %all-to-all-start.3) | async-done | bytes 2752544 | tf_op jit(solution)/shard_map/all_to_all | solution.py:95
  531.8 7.8 %all-to-all-start.1 = ((bf16[32,12,3584]{2,1,0:T(8,128)(2,1)}), bf16[32,12,3584]{2,1,0:T(8,128)(2,1)}, u32[]{:S(2)}, u32[]{:S(2)}) async-start(bf16[32,12,3584]{2,1,0:T(8,128)(2,1)} %reshape.157), calls=%async_computation.1 | async-start | bytes 7340032 | tf_op jit(solution)/shard_map/all_to_all | solution.py:95
  540.2 0.8 gather_fusion
  541.5 0.8 gather_fusion.1
  542.9 2.7 convert_reduce_fusion
  546.2 9.7 %collective-permute-start.1 = (bf16[1,16,3584]{2,1,0:T(8,128)(2,1)S(1)}, bf16[1,16,3584]{2,1,0:T(8,128)(2,1)S(1)}, u32[]{:S(2)}, u32[]{:S(2)}) collective-permute-start(bf16[1,16,3584]{2,1,0:T(8,128)(2,1)S(1)} %fusion.2), channel_id=1, source_target_pairs={{32,0},{64,32},{96,64},{128,96},{160,128},{192,160},{224,192},{256... | collective-permute-start | bytes 344072 | tf_op jit(solution)/shard_map/ppermute | solution.py:15
  555.9 151.7 %all-to-all-done.1 = bf16[32,12,3584]{2,1,0:T(8,128)(2,1)} async-done(((bf16[32,12,3584]{2,1,0:T(8,128)(2,1)}), bf16[32,12,3584]{2,1,0:T(8,128)(2,1)}, u32[]{:S(2)}, u32[]{:S(2)}) %all-to-all-start.1) | async-done | bytes 2752544 | tf_op jit(solution)/shard_map/all_to_all | solution.py:95
  707.7 2.7 convert_reduce_fusion.1
  711.0 1.9 collective-permute-start
  712.9 17.4 %collective-permute-done = bf16[1,16,3584]{2,1,0:T(8,128)(2,1)S(1)} collective-permute-done((bf16[1,16,3584]{2,1,0:T(8,128)(2,1)S(1)}, bf16[1,16,3584]{2,1,0:T(8,128)(2,1)S(1)}, u32[]{:S(2)}, u32[]{:S(2)}) %collective-permute-start) | collective-permute-done | bytes 114720 | tf_op jit(solution)/shard_map/ppermute | solution.py:15
  730.3 0.6 copy.45
  730.9 0.6 copy.46
  (61 shorter events, 5.0 us)
Async XLA Ops:
  0.6 205.6 %copy-start = (bf16[1,128,3584]{2,1,0:T(8,128)(2,1)S(1)}, bf16[1,128,3584]{2,1,0:T(8,128)(2,1)}, u32[]{:S(2)}) copy-start(bf16[1,128,3584]{2,1,0:T(8,128)(2,1)} %param.19) | copy-start | bytes 2752516
  8.7 15.8 %copy-start.4 = (s32[1,16,2]{1,2,0:T(2,128)S(1)}, s32[1,16,2]{1,2,0:T(2,128)}, u32[]{:S(2)}) copy-start(s32[1,16,2]{1,2,0:T(2,128)} %param.13) | copy-start | bytes 388
  8.7 178.8 %all-to-all-start.2 = ((bf16[32,12,3584]{2,1,0:T(8,128)(2,1)}), bf16[32,12,3584]{2,1,0:T(8,128)(2,1)}, u32[]{:S(2)}, u32[]{:S(2)}) async-start(bf16[32,12,3584]{2,1,0:T(8,128)(2,1)} %bitcast.94), calls=%async_computation.2 | async-start | bytes 7340032 | tf_op jit(solution)/shard_map/all_to_all | solution.py:98
  189.9 171.0 %all-to-all-start = ((bf16[32,12,3584]{2,1,0:T(8,128)(2,1)}), bf16[32,12,3584]{2,1,0:T(8,128)(2,1)}, u32[]{:S(2)}, u32[]{:S(2)}) async-start(bf16[32,12,3584]{2,1,0:T(8,128)(2,1)} %bitcast.95), calls=%async_computation | async-start | bytes 7340032 | tf_op jit(solution)/shard_map/all_to_all | solution.py:98
  360.8 171.0 %all-to-all-start.3 = ((bf16[32,12,3584]{2,1,0:T(8,128)(2,1)}), bf16[32,12,3584]{2,1,0:T(8,128)(2,1)}, u32[]{:S(2)}, u32[]{:S(2)}) async-start(bf16[32,12,3584]{2,1,0:T(8,128)(2,1)} %reshape.162), calls=%async_computation.3 | async-start | bytes 7340032 | tf_op jit(solution)/shard_map/all_to_all | solution.py:95
  385.0 155.0 %copy-start.2 = (bf16[1,16,3584]{2,1,0:T(8,128)(2,1)S(1)}, bf16[1,16,3584]{2,1,0:T(8,128)(2,1)}, u32[]{:S(2)}) copy-start(bf16[1,16,3584]{2,1,0:T(8,128)(2,1)} %param.11) | copy-start | bytes 344068
  385.0 155.0 %copy-start.5 = (bf16[1,3584,4]{1,2,0:T(4,128)(2,1)S(1)}, bf16[1,3584,4]{1,2,0:T(4,128)(2,1)}, u32[]{:S(2)}) copy-start(bf16[1,3584,4]{1,2,0:T(4,128)(2,1)} %param.16) | copy-start | bytes 86020
  531.8 175.9 %all-to-all-start.1 = ((bf16[32,12,3584]{2,1,0:T(8,128)(2,1)}), bf16[32,12,3584]{2,1,0:T(8,128)(2,1)}, u32[]{:S(2)}, u32[]{:S(2)}) async-start(bf16[32,12,3584]{2,1,0:T(8,128)(2,1)} %reshape.157), calls=%async_computation.1 | async-start | bytes 7340032 | tf_op jit(solution)/shard_map/all_to_all | solution.py:95
  540.2 0.9 copy-start.3
  540.2 1.1 copy-start.1
  546.2 166.7 %collective-permute-start.1 = (bf16[1,16,3584]{2,1,0:T(8,128)(2,1)S(1)}, bf16[1,16,3584]{2,1,0:T(8,128)(2,1)S(1)}, u32[]{:S(2)}, u32[]{:S(2)}) collective-permute-start(bf16[1,16,3584]{2,1,0:T(8,128)(2,1)S(1)} %fusion.2), channel_id=1, source_target_pairs={{32,0},{64,32},{96,64},{128,96},{160,128},{192,160},{224,192},{256... | collective-permute-start | bytes 344072 | tf_op jit(solution)/shard_map/ppermute | solution.py:15
  711.0 19.3 %collective-permute-start = (bf16[1,16,3584]{2,1,0:T(8,128)(2,1)S(1)}, bf16[1,16,3584]{2,1,0:T(8,128)(2,1)S(1)}, u32[]{:S(2)}, u32[]{:S(2)}) collective-permute-start(bf16[1,16,3584]{2,1,0:T(8,128)(2,1)S(1)} %fusion.3), channel_id=1, source_target_pairs={{480,0},{0,32},{32,64},{64,96},{96,128},{128,160},{160,192},{192,2... | collective-permute-start | bytes 344072 | tf_op jit(solution)/shard_map/ppermute | solution.py:15
where the time goes:
time: 733 us; the launch traced here: 732 us
  waiting for transfers between devices  625 us (85%)
  starting transfers between devices  50.8 us (7%)
  local copies, waits for them, and re-layouts  31.5 us (4%)
  matrix products  13.4 us (2%)
  other arithmetic  10.4 us (1%)
    all_to_all x2, waiting for transfers between devices, dispatch(): lax.all_to_all(send, 'expert', split_axis=0, concat_axis=0, tiled=True)  309 us
    all_to_all x2, waiting for transfers between devices, one_span(): lax.all_to_all(piece, 'expert', split_axis=0, concat_axis=0, tiled=True)  299 us
    all_to_all x2, starting transfers between devices, dispatch(): lax.all_to_all(send, 'expert', split_axis=0, concat_axis=0, tiled=True)  23.6 us
    ppermute x2, waiting for transfers between devices, shifted(): return lax.ppermute(block, axis, route)  17.4 us
    all_to_all x2, starting transfers between devices, one_span(): lax.all_to_all(piece, 'expert', split_axis=0, concat_axis=0, tiled=True)  15.5 us
  transfers between devices with their start and end apart: 6, of which 5 were waited for; matrix products, arithmetic and copies ran while one was open for 6% of the time, Pallas kernels for 0%

commit v1 on v0

v1 whole, which is shorter than its diff:
```python
import jax
import jax.numpy as jnp
from jax import lax
from jax.sharding import PartitionSpec as P

CAP = 12
ALONG_X = 4
UNITS = 2

route_scale = 2.5


def index_of(z, x):
    return z * ALONG_X + x


def places():
    columns = lax.axis_size("expert") // ALONG_X
    return [(z, x) for z in range(columns) for x in range(ALONG_X)]


def along_x(block, step):
    route = [(index_of(z, x), index_of(z, (x + step) % ALONG_X)) for z, x in places()]
    return lax.ppermute(block, "expert", route)


def along_z(block, step):
    columns = lax.axis_size("expert") // ALONG_X
    route = [(index_of(z, x), index_of((z + step) % columns, x)) for z, x in places()]
    return lax.ppermute(block, "expert", route)


def swapped(block):
    route = [(index_of(z, x), index_of(z ^ 1, x)) for z, x in places()]
    return lax.ppermute(block, "expert", route)


def to_section(block, section_step, z_step):
    sections, devices = lax.axis_size("pipe"), lax.axis_size("expert")
    columns = devices // ALONG_X
    route = [
        (
            s * devices + index_of(z, x),
            (s + section_step) % sections * devices + index_of((z + z_step) % columns, x),
        )
        for s in range(sections)
        for z, x in places()
    ]
    return lax.ppermute(block, ("pipe", "expert"), route)


def gather_x(block):
    half = block.shape[0] // 2
    left = along_x(block, 1)
    right = along_x(block, -1)
    far_top = along_x(left[:half], 1)
    far_bottom = along_x(right[half:], -1)
    return left, right, far_top, far_bottom


def prepare(x, routes, gain, router, group):
    xf = x.astype(jnp.float32)
    mean_sq = jnp.mean(xf * xf, axis=-1, keepdims=True)
    normed = (xf * lax.rsqrt(mean_sq + 1e-06) * gain).astype(jnp.bfloat16)
    logits = jnp.dot(normed, router, preferred_element_type=jnp.float32)
    affinity = jax.nn.sigmoid(logits)
    experts_n = router.shape[1]
    hits = routes[:, :, None] == jnp.arange(experts_n, dtype=jnp.int32)
    picked = jnp.sum(jnp.where(hits, affinity[:, None, :], 0.0), axis=2)
    weights = picked / jnp.sum(picked, axis=1, keepdims=True) * route_scale
    named = jnp.any(hits, axis=1)
    share = jnp.sum(jnp.where(hits, weights[:, :, None], 0.0), axis=1)
    count = named.astype(jnp.int32)
    before = jnp.cumsum(count, axis=0) - count
    turn = jnp.mod(jnp.arange(experts_n, dtype=jnp.int32) + group, experts_n)
    rolled = turn[:, None] == jnp.arange(experts_n, dtype=jnp.int32)
    pick = lambda v: jnp.sum(jnp.where(rolled, v[:, None, :], jnp.zeros((), v.dtype)), axis=2)
    slot = jnp.where(pick(count) > 0, pick(before), -1)
    chosen = slot[:, :, None] == jnp.arange(CAP, dtype=jnp.int32)
    combine = jnp.where(chosen, pick(share)[:, :, None], 0.0)
    return normed, chosen, combine


def on_device(act_down, act_up, routes_down, routes_up, norm_gain, router_w, w_gate, w_up, w_down):
    experts_n = router_w.shape[2]
    width = act_down.shape[2]
    rows_n = act_down.shape[1]
    part = width // UNITS
    piece = part // 2
    gain = norm_gain[0]
    router = router_w[0]
    both_cols = jnp.concatenate([w_gate[0], w_up[0]], axis=1)
    down_rows = w_down[0]
    hidden_n = down_rows.shape[0]
    group = lax.axis_index("expert") // ALONG_X // 2

    cols_all = (both_cols,) + gather_x(both_cols)
    down_all = []
    for unit in range(UNITS):
        mine = down_rows[:, unit * part:(unit + 1) * part]
        down_all.append((mine,) + gather_x(mine))

    normed_d, chosen_d, combine_d = prepare(act_down[0], routes_down[0], gain, router, group)
    normed_u, chosen_u, combine_u = prepare(act_up[0], routes_up[0], gain, router, group)
    select = jnp.stack(
        [jnp.pad(chosen_d, ((0, rows_n), (0, 0), (0, 0))), jnp.pad(chosen_u, ((rows_n, 0), (0, 0), (0, 0)))],
        axis=2,
    ).reshape(2 * rows_n, experts_n * 2 * CAP)
    packed = lax.dot_general(
        select.astype(jnp.bfloat16),
        jnp.concatenate([normed_d, normed_u], axis=0),
        (((0,), (0,)), ((), ())),
        preferred_element_type=jnp.float32,
    ).astype(jnp.bfloat16)
    chunk = 2 * CAP
    near = [packed[:chunk]] + [
        along_z(packed[s * chunk:(s + 1) * chunk], 2 * s) for s in range(1, experts_n)
    ]
    mine = jnp.concatenate(near, axis=0)
    rows = jnp.concatenate([mine, swapped(mine)], axis=0)

    def spread(combine):
        blocks = jnp.zeros((2, rows_n, experts_n, 2, CAP), jnp.float32)
        blocks = blocks.at[0, :, :, 0, :].set(combine).at[1, :, :, 1, :].set(combine)
        return blocks.reshape(2 * rows_n, experts_n * chunk)

    res_down = to_section(act_down[0], 1, 0)
    res_up = to_section(act_up[0], -1, 0)
    mix_down = to_section(spread(combine_d), 1, 0)
    mix_up = to_section(spread(combine_u), -1, 0)

    dot = lambda a, b: jnp.dot(a, b, preferred_element_type=jnp.float32)
    act = lambda joined: (jax.nn.silu(joined[:, :hidden_n]) * joined[:, hidden_n:]).astype(jnp.bfloat16)
    own, left, right, far_top, far_bottom = cols_all
    half = far_top.shape[0]
    hidden = [act(dot(rows, own)), act(dot(rows, left)), act(dot(rows, right))]
    hidden.append(act(dot(rows[:, :half], far_top) + dot(rows[:, half:], far_bottom)))
    hidden = jnp.concatenate(hidden, axis=1)

    back_down, back_up = [], []
    for unit in range(UNITS):
        total = dot(hidden, jnp.concatenate(down_all[unit], axis=0))
        held = rows.shape[0] // 2
        theirs = swapped(total[held:].astype(jnp.bfloat16))
        summed = (total[:held] + theirs.astype(jnp.float32)).astype(jnp.bfloat16)
        summed = summed.reshape(experts_n, 2, CAP, 2, piece).transpose(0, 1, 3, 2, 4)
        summed = summed.reshape(experts_n, 2, chunk, piece)
        back_down.append(jnp.concatenate([to_section(summed[s, 0], 1, -2 * s) for s in range(experts_n)], axis=0))
        back_up.append(jnp.concatenate([to_section(summed[s, 1], -1, -2 * s) for s in range(experts_n)], axis=0))

    def finish(residual, mix, back):
        pieces = []
        for unit in range(UNITS):
            mixed = jnp.dot(
                mix, back[unit].astype(jnp.float32), precision=lax.Precision.HIGHEST, preferred_element_type=jnp.float32
            )
            pieces += [mixed[:rows_n], mixed[rows_n:]]
        mixed = jnp.concatenate(pieces, axis=1)
        return (residual.astype(jnp.float32) + mixed).astype(jnp.bfloat16)[None]

    return finish(res_down, mix_down, back_down), finish(res_up, mix_up, back_up)


def solution(mesh):
    placed = (
        P("pipe", "expert", None),
        P("pipe", "expert", None),
        P("pipe", "expert", None),
        P("pipe", "expert", None),
        P("pipe", None),
        P("pipe", None, None),
        P("pipe", None, "expert"),
        P("pipe", None, "expert"),
        P("pipe", "expert", None),
    )
    return jax.shard_map(
        on_device,
        mesh=mesh,
        in_specs=placed,
        out_specs=(P("pipe", "expert", None), P("pipe", "expert", None)),
        check_vma=False,
    )
```

time: 733 us -> 266 us (0.36)
  the two profiles are of different devices: /device:TPU:6 before, /device:TPU:66 now
where the time goes in v1:
time: 266 us; the launch traced here: 264 us
  starting transfers between devices  170 us (64%)
  waiting for transfers between devices  57.1 us (21%)
  local copies, waits for them, and re-layouts  19.6 us (7%)
  matrix products  8.23 us (3%)
  other arithmetic  6.8 us (3%)
    ppermute x20, starting transfers between devices, to_section(): return lax.ppermute(block, ('pipe', 'expert'), route)  108 us
    ppermute x12, starting transfers between devices, along_x(): return lax.ppermute(block, 'expert', route)  38 us
    ppermute x12, waiting for transfers between devices, along_x(): return lax.ppermute(block, 'expert', route)  27.5 us
    ppermute x20, waiting for transfers between devices, to_section(): return lax.ppermute(block, ('pipe', 'expert'), route)  23.7 us
    ppermute x3, starting transfers between devices, along_z(): return lax.ppermute(block, 'expert', route)  16 us
    ppermute x3, starting transfers between devices, swapped(): return lax.ppermute(block, 'expert', route)  8.77 us
  transfers between devices with their start and end apart: 38, of which 12 were waited for; matrix products, arithmetic and copies ran while one was open for 11% of the time, Pallas kernels for 0%

profile of v1, /device:TPU:66, one launch (start us, length us, event | category | flops | bytes accessed | tf_op | source)
XLA Modules:
  0.0 264.1 jit_solution(6337039158290438738)
XLA Ops:
  0.7 3.0 %pad_maximum_fusion = bf16[3584,256]{1,0:T(8,128)(2,1)} fusion(bf16[3584,128]{1,0:T(8,128)(2,1)} %bitcast.106, bf16[3584,128]{1,0:T(8,128)(2,1)} %bitcast.108), kind=kLoop, calls=%fused_computation.1 | loop fusion | flops 3670016 | bytes 3670016 | tf_op jit(solution)/shard_map/concatenate | solution.py:92
  6.1 3.4 %collective-permute-start.6 = (bf16[3584,256]{1,0:T(8,128)(2,1)}, bf16[3584,256]{1,0:T(8,128)(2,1)}, u32[]{:S(2)}, u32[]{:S(2)}) collective-permute-start(bf16[3584,256]{1,0:T(8,128)(2,1)} %pad_maximum_fusion), channel_id=1, source_target_pairs={{0,1},{1,2},{2,3},{3,0},{4,5},{5,6},{6,7},{7,4},{8,9},{9,10},{10,1... | collective-permute-start | bytes 5505032 | tf_op jit(solution)/shard_map/ppermute | solution.py:24
  13.2 6.5 %collective-permute-start.2 = (bf16[24,3584]{1,0:T(8,128)(2,1)}, bf16[24,3584]{1,0:T(8,128)(2,1)}, u32[]{:S(2)}, u32[]{:S(2)}) collective-permute-start(bf16[24,3584]{1,0:T(8,128)(2,1)} %get-tuple-element.68), channel_id=1, source_target_pairs={{0,8},{1,9},{2,10},{3,11},{4,12},{5,13},{6,14},{7,15},{8,16},{9,17... | collective-permute-start | bytes 516104 | tf_op jit(solution)/shard_map/ppermute | solution.py:30
  19.8 6.3 %collective-permute-start.3 = (bf16[24,3584]{1,0:T(8,128)(2,1)}, bf16[24,3584]{1,0:T(8,128)(2,1)}, u32[]{:S(2)}, u32[]{:S(2)}) collective-permute-start(bf16[24,3584]{1,0:T(8,128)(2,1)} %get-tuple-element.67), channel_id=1, source_target_pairs={{0,16},{1,17},{2,18},{3,19},{4,20},{5,21},{6,22},{7,23},{8,24},{9,... | collective-permute-start | bytes 516104 | tf_op jit(solution)/shard_map/ppermute | solution.py:30
  26.1 3.1 %collective-permute-start.4 = (bf16[24,3584]{1,0:T(8,128)(2,1)}, bf16[24,3584]{1,0:T(8,128)(2,1)}, u32[]{:S(2)}, u32[]{:S(2)}) collective-permute-start(bf16[24,3584]{1,0:T(8,128)(2,1)} %get-tuple-element.66), channel_id=1, source_target_pairs={{0,24},{1,25},{2,26},{3,27},{4,28},{5,29},{6,30},{7,31},{8,0},{9,1... | collective-permute-start | bytes 516104 | tf_op jit(solution)/shard_map/ppermute | solution.py:30
  42.9 3.8 %collective-permute-start.10 = (bf16[128,1792]{1,0:T(8,128)(2,1)}, bf16[128,1792]{1,0:T(8,128)(2,1)S(1)}, u32[]{:S(2)}, u32[]{:S(2)}) collective-permute-start(bf16[128,1792]{1,0:T(8,128)(2,1)} %get-tuple-element.60), channel_id=1, source_target_pairs={{0,1},{1,2},{2,3},{3,0},{4,5},{5,6},{6,7},{7,4},{8,9},{9,10},{10,1... | collective-permute-start | bytes 1376264 | tf_op jit(solution)/shard_map/ppermute | solution.py:24
  52.4 3.4 %collective-permute-start.19 = (bf16[128,1792]{1,0:T(8,128)(2,1)}, bf16[128,1792]{1,0:T(8,128)(2,1)S(1)}, u32[]{:S(2)}, u32[]{:S(2)}) collective-permute-start(bf16[128,1792]{1,0:T(8,128)(2,1)} %get-tuple-element.63), channel_id=1, source_target_pairs={{0,1},{1,2},{2,3},{3,0},{4,5},{5,6},{6,7},{7,4},{8,9},{9,10},{10,1... | collective-permute-start | bytes 1376264 | tf_op jit(solution)/shard_map/ppermute | solution.py:24
  58.9 2.8 %collective-permute-done.10 = bf16[128,1792]{1,0:T(8,128)(2,1)S(1)} collective-permute-done((bf16[128,1792]{1,0:T(8,128)(2,1)}, bf16[128,1792]{1,0:T(8,128)(2,1)S(1)}, u32[]{:S(2)}, u32[]{:S(2)}) %collective-permute-start.10) | collective-permute-done | bytes 458784 | tf_op jit(solution)/shard_map/ppermute | solution.py:24
  61.7 5.2 %collective-permute-start.20 = (bf16[128,1792]{1,0:T(8,128)(2,1)S(1)}, bf16[128,1792]{1,0:T(8,128)(2,1)S(1)}, u32[]{:S(2)}, u32[]{:S(2)}) collective-permute-start(bf16[128,1792]{1,0:T(8,128)(2,1)S(1)} %copy-done.8), channel_id=1, source_target_pairs={{0,3},{1,0},{2,1},{3,2},{4,7},{5,4},{6,5},{7,6},{8,11},{9,8},{10,9... | collective-permute-start | bytes 1376264 | tf_op jit(solution)/shard_map/ppermute | solution.py:24
  66.9 12.9 %collective-permute-start.29 = (f32[32,96]{0,1:T(8,128)}, f32[32,96]{0,1:T(8,128)S(1)}, u32[]{:S(2)}, u32[]{:S(2)}) collective-permute-start(f32[32,96]{0,1:T(8,128)} %reshape.349), channel_id=1, source_target_pairs={{0,480},{1,481},{2,482},{3,483},{4,484},{5,485},{6,486},{7,487},{8... | collective-permute-start | bytes 36872 | tf_op jit(solution)/shard_map/ppermute | solution.py:49
  79.9 2.9 %collective-permute-start.5 = (bf16[96,3584]{1,0:T(8,128)(2,1)S(1)}, bf16[96,3584]{1,0:T(8,128)(2,1)S(1)}, u32[]{:S(2)}, u32[]{:S(2)}) collective-permute-start(bf16[96,3584]{1,0:T(8,128)(2,1)S(1)} %pad_maximum_fusion.1), channel_id=1, source_target_pairs={{0,4},{1,5},{2,6},{3,7},{4,0},{5,1},{6,2},{7,3},{8,12},{9,13},{10,... | collective-permute-start | bytes 2064392 | tf_op jit(solution)/shard_map/ppermute | solution.py:35
  85.0 5.9 %collective-permute-done.12 = bf16[64,1792]{1,0:T(8,128)(2,1)S(1)} collective-permute-done((bf16[64,1792]{1,0:T(8,128)(2,1)S(1)}, bf16[64,1792]{1,0:T(8,128)(2,1)S(1)}, u32[]{:S(2)}, u32[]{:S(2)}) %collective-permute-start.12) | collective-permute-done | bytes 229408 | tf_op jit(solution)/shard_map/ppermute | solution.py:24
  90.9 3.4 %collective-permute-start.13 = (bf16[64,1792]{1,0:T(8,128)(2,1)S(1)}, bf16[64,1792]{1,0:T(8,128)(2,1)S(1)}, u32[]{:S(2)}, u32[]{:S(2)}) collective-permute-start(bf16[64,1792]{1,0:T(8,128)(2,1)S(1)} %slice.346), channel_id=1, source_target_pairs={{0,3},{1,0},{2,1},{3,2},{4,7},{5,4},{6,5},{7,6},{8,11},{9,8},{10,9... | collective-permute-start | bytes 688136 | tf_op jit(solution)/shard_map/ppermute | solution.py:24
  94.3 4.5 %collective-permute-done.13 = bf16[64,1792]{1,0:T(8,128)(2,1)S(1)} collective-permute-done((bf16[64,1792]{1,0:T(8,128)(2,1)S(1)}, bf16[64,1792]{1,0:T(8,128)(2,1)S(1)}, u32[]{:S(2)}, u32[]{:S(2)}) %collective-permute-start.13) | collective-permute-done | bytes 229408 | tf_op jit(solution)/shard_map/ppermute | solution.py:24
  100.7 6.0 %collective-permute-done.21 = bf16[64,1792]{1,0:T(8,128)(2,1)S(1)} collective-permute-done((bf16[64,1792]{1,0:T(8,128)(2,1)S(1)}, bf16[64,1792]{1,0:T(8,128)(2,1)S(1)}, u32[]{:S(2)}, u32[]{:S(2)}) %collective-permute-start.21) | collective-permute-done | bytes 229408 | tf_op jit(solution)/shard_map/ppermute | solution.py:24
  106.7 4.6 %collective-permute-start.22 = (bf16[64,1792]{1,0:T(8,128)(2,1)S(1)}, bf16[64,1792]{1,0:T(8,128)(2,1)S(1)}, u32[]{:S(2)}, u32[]{:S(2)}) collective-permute-start(bf16[64,1792]{1,0:T(8,128)(2,1)S(1)} %slice.357), channel_id=1, source_target_pairs={{0,3},{1,0},{2,1},{3,2},{4,7},{5,4},{6,5},{7,6},{8,11},{9,8},{10,9... | collective-permute-start | bytes 688136 | tf_op jit(solution)/shard_map/ppermute | solution.py:24
  115.2 3.9 %collective-permute-start.8 = (bf16[1792,256]{1,0:T(8,128)(2,1)S(1)}, bf16[1792,256]{1,0:T(8,128)(2,1)S(1)}, u32[]{:S(2)}, u32[]{:S(2)}) collective-permute-start(bf16[1792,256]{1,0:T(8,128)(2,1)S(1)} %slice.339), channel_id=1, source_target_pairs={{0,1},{1,2},{2,3},{3,0},{4,5},{5,6},{6,7},{7,4},{8,9},{9,10},{10,1... | collective-permute-start | bytes 2752520 | tf_op jit(solution)/shard_map/ppermute | solution.py:24
  121.8 5.8 %collective-permute-done.9 = bf16[1792,256]{1,0:T(8,128)(2,1)S(1)} collective-permute-done((bf16[1792,256]{1,0:T(8,128)(2,1)S(1)}, bf16[1792,256]{1,0:T(8,128)(2,1)S(1)}, u32[]{:S(2)}, u32[]{:S(2)}) %collective-permute-start.9) | collective-permute-done | bytes 917536 | tf_op jit(solution)/shard_map/ppermute | solution.py:24
  131.5 2.9 %collective-permute-start.14 = (bf16[96,1792]{1,0:T(8,128)(2,1)S(1)}, bf16[96,1792]{1,0:T(8,128)(2,1)S(1)}, u32[]{:S(2)}, u32[]{:S(2)}) collective-permute-start(bf16[96,1792]{1,0:T(8,128)(2,1)S(1)} %slice.410), channel_id=1, source_target_pairs={{0,4},{1,5},{2,6},{3,7},{4,0},{5,1},{6,2},{7,3},{8,12},{9,13},{10,... | collective-permute-start | bytes 1032200 | tf_op jit(solution)/shard_map/ppermute | solution.py:35
  135.1 2.9 %collective-permute-start.23 = (bf16[96,1792]{1,0:T(8,128)(2,1)S(1)}, bf16[96,1792]{1,0:T(8,128)(2,1)S(1)}, u32[]{:S(2)}, u32[]{:S(2)}) collective-permute-start(bf16[96,1792]{1,0:T(8,128)(2,1)S(1)} %slice.409), channel_id=1, source_target_pairs={{0,4},{1,5},{2,6},{3,7},{4,0},{5,1},{6,2},{7,3},{8,12},{9,13},{10,... | collective-permute-start | bytes 1032200 | tf_op jit(solution)/shard_map/ppermute | solution.py:35
  138.0 2.7 %collective-permute-done.14 = bf16[96,1792]{1,0:T(8,128)(2,1)S(1)} collective-permute-done((bf16[96,1792]{1,0:T(8,128)(2,1)S(1)}, bf16[96,1792]{1,0:T(8,128)(2,1)S(1)}, u32[]{:S(2)}, u32[]{:S(2)}) %collective-permute-start.14) | collective-permute-done | bytes 344096 | tf_op jit(solution)/shard_map/ppermute | solution.py:35
  141.6 7.8 %collective-permute-start.30 = (bf16[24,896]{1,0:T(8,128)(2,1)S(1)}, bf16[24,896]{1,0:T(8,128)(2,1)S(1)}, u32[]{:S(2)}, u32[]{:S(2)}) collective-permute-start(bf16[24,896]{1,0:T(8,128)(2,1)S(1)} %bitcast.127), channel_id=1, source_target_pairs={{0,480},{1,481},{2,482},{3,483},{4,484},{5,485},{6,486},{7,487},{8... | collective-permute-start | bytes 129032 | tf_op jit(solution)/shard_map/ppermute | solution.py:49
  149.4 9.1 %collective-permute-start.31 = (bf16[24,896]{1,0:T(8,128)(2,1)S(1)}, bf16[24,896]{1,0:T(8,128)(2,1)S(1)}, u32[]{:S(2)}, u32[]{:S(2)}) collective-permute-start(bf16[24,896]{1,0:T(8,128)(2,1)S(1)} %bitcast.125), channel_id=1, source_target_pairs={{0,504},{1,505},{2,506},{3,507},{4,508},{5,509},{6,510},{7,511},{8... | collective-permute-start | bytes 129032 | tf_op jit(solution)/shard_map/ppermute | solution.py:49
  160.5 7.4 %collective-permute-start.33 = (bf16[24,896]{1,0:T(8,128)(2,1)S(1)}, bf16[24,896]{1,0:T(8,128)(2,1)S(1)}, u32[]{:S(2)}, u32[]{:S(2)}) collective-permute-start(bf16[24,896]{1,0:T(8,128)(2,1)S(1)} %bitcast.123), channel_id=1, source_target_pairs={{0,488},{1,489},{2,490},{3,491},{4,492},{5,493},{6,494},{7,495},{8... | collective-permute-start | bytes 129032 | tf_op jit(solution)/shard_map/ppermute | solution.py:49
  171.0 14.5 %collective-permute-start.34 = (bf16[24,896]{1,0:T(8,128)(2,1)S(1)}, bf16[24,896]{1,0:T(8,128)(2,1)S(1)}, u32[]{:S(2)}, u32[]{:S(2)}) collective-permute-start(bf16[24,896]{1,0:T(8,128)(2,1)S(1)} %bitcast.128), channel_id=1, source_target_pairs={{0,480},{1,481},{2,482},{3,483},{4,484},{5,485},{6,486},{7,487},{8... | collective-permute-start | bytes 129032 | tf_op jit(solution)/shard_map/ppermute | solution.py:49
  191.6 2.9 %collective-permute-start.15 = (bf16[24,896]{1,0:T(8,128)(2,1)S(1)}, bf16[24,896]{1,0:T(8,128)(2,1)S(1)}, u32[]{:S(2)}, u32[]{:S(2)}) collective-permute-start(bf16[24,896]{1,0:T(8,128)(2,1)S(1)} %bitcast.120), channel_id=1, source_target_pairs={{0,32},{1,33},{2,34},{3,35},{4,36},{5,37},{6,38},{7,39},{8,40},{9,... | collective-permute-start | bytes 129032 | tf_op jit(solution)/shard_map/ppermute | solution.py:49
  194.5 8.3 %collective-permute-start.16 = (bf16[24,896]{1,0:T(8,128)(2,1)S(1)}, bf16[24,896]{1,0:T(8,128)(2,1)S(1)}, u32[]{:S(2)}, u32[]{:S(2)}) collective-permute-start(bf16[24,896]{1,0:T(8,128)(2,1)S(1)} %bitcast.119), channel_id=1, source_target_pairs={{0,56},{1,57},{2,58},{3,59},{4,60},{5,61},{6,62},{7,63},{8,32},{9,... | collective-permute-start | bytes 129032 | tf_op jit(solution)/shard_map/ppermute | solution.py:49
  202.8 4.0 %collective-permute-start.17 = (bf16[24,896]{1,0:T(8,128)(2,1)S(1)}, bf16[24,896]{1,0:T(8,128)(2,1)S(1)}, u32[]{:S(2)}, u32[]{:S(2)}) collective-permute-start(bf16[24,896]{1,0:T(8,128)(2,1)S(1)} %bitcast.118), channel_id=1, source_target_pairs={{0,48},{1,49},{2,50},{3,51},{4,52},{5,53},{6,54},{7,55},{8,56},{9,... | collective-permute-start | bytes 129032 | tf_op jit(solution)/shard_map/ppermute | solution.py:49
  206.9 10.3 %collective-permute-start.18 = (bf16[24,896]{1,0:T(8,128)(2,1)S(1)}, bf16[24,896]{1,0:T(8,128)(2,1)S(1)}, u32[]{:S(2)}, u32[]{:S(2)}) collective-permute-start(bf16[24,896]{1,0:T(8,128)(2,1)S(1)} %bitcast.117), channel_id=1, source_target_pairs={{0,40},{1,41},{2,42},{3,43},{4,44},{5,45},{6,46},{7,47},{8,48},{9,... | collective-permute-start | bytes 129032 | tf_op jit(solution)/shard_map/ppermute | solution.py:49
  217.4 11.3 %collective-permute-start.28 = (bf16[16,3584]{1,0:T(8,128)(2,1)S(1)}, bf16[16,3584]{1,0:T(8,128)(2,1)S(1)}, u32[]{:S(2)}, u32[]{:S(2)}) collective-permute-start(bf16[16,3584]{1,0:T(8,128)(2,1)S(1)} %bitcast.111), channel_id=1, source_target_pairs={{0,480},{1,481},{2,482},{3,483},{4,484},{5,485},{6,486},{7,487},{8... | collective-permute-start | bytes 344072 | tf_op jit(solution)/shard_map/ppermute | solution.py:49
  236.8 9.7 %collective-permute-done.24 = bf16[24,896]{1,0:T(8,128)(2,1)S(1)} collective-permute-done((bf16[24,896]{1,0:T(8,128)(2,1)S(1)}, bf16[24,896]{1,0:T(8,128)(2,1)S(1)}, u32[]{:S(2)}, u32[]{:S(2)}) %collective-permute-start.24) | collective-permute-done | bytes 43040 | tf_op jit(solution)/shard_map/ppermute | solution.py:49
  251.2 12.2 %collective-permute-done = bf16[16,3584]{1,0:T(8,128)(2,1)S(1)} collective-permute-done((bf16[16,3584]{1,0:T(8,128)(2,1)S(1)}, bf16[16,3584]{1,0:T(8,128)(2,1)S(1)}, u32[]{:S(2)}, u32[]{:S(2)}) %collective-permute-start) | collective-permute-done | bytes 114720 | tf_op jit(solution)/shard_map/ppermute | solution.py:49
  (201 shorter events, 68.8 us)
Async XLA Ops:
  3.7 108.3 %collective-permute-start.7 = (bf16[3584,256]{1,0:T(8,128)(2,1)}, bf16[3584,256]{1,0:T(8,128)(2,1)S(1)}, u32[]{:S(2)}, u32[]{:S(2)}) collective-permute-start(bf16[3584,256]{1,0:T(8,128)(2,1)} %pad_maximum_fusion), channel_id=1, source_target_pairs={{0,3},{1,0},{2,1},{3,2},{4,7},{5,4},{6,5},{7,6},{8,11},{9,8},{10,9... | collective-permute-start | bytes 5505032 | tf_op jit(solution)/shard_map/ppermute | solution.py:24
  6.1 107.9 %collective-permute-start.6 = (bf16[3584,256]{1,0:T(8,128)(2,1)}, bf16[3584,256]{1,0:T(8,128)(2,1)}, u32[]{:S(2)}, u32[]{:S(2)}) collective-permute-start(bf16[3584,256]{1,0:T(8,128)(2,1)} %pad_maximum_fusion), channel_id=1, source_target_pairs={{0,1},{1,2},{2,3},{3,0},{4,5},{5,6},{6,7},{7,4},{8,9},{9,10},{10,1... | collective-permute-start | bytes 5505032 | tf_op jit(solution)/shard_map/ppermute | solution.py:24
  13.2 29.6 %collective-permute-start.2 = (bf16[24,3584]{1,0:T(8,128)(2,1)}, bf16[24,3584]{1,0:T(8,128)(2,1)}, u32[]{:S(2)}, u32[]{:S(2)}) collective-permute-start(bf16[24,3584]{1,0:T(8,128)(2,1)} %get-tuple-element.68), channel_id=1, source_target_pairs={{0,8},{1,9},{2,10},{3,11},{4,12},{5,13},{6,14},{7,15},{8,16},{9,17... | collective-permute-start | bytes 516104 | tf_op jit(solution)/shard_map/ppermute | solution.py:30
  19.8 27.8 %collective-permute-start.3 = (bf16[24,3584]{1,0:T(8,128)(2,1)}, bf16[24,3584]{1,0:T(8,128)(2,1)}, u32[]{:S(2)}, u32[]{:S(2)}) collective-permute-start(bf16[24,3584]{1,0:T(8,128)(2,1)} %get-tuple-element.67), channel_id=1, source_target_pairs={{0,16},{1,17},{2,18},{3,19},{4,20},{5,21},{6,22},{7,23},{8,24},{9,... | collective-permute-start | bytes 516104 | tf_op jit(solution)/shard_map/ppermute | solution.py:30
  26.1 26.3 %collective-permute-start.4 = (bf16[24,3584]{1,0:T(8,128)(2,1)}, bf16[24,3584]{1,0:T(8,128)(2,1)}, u32[]{:S(2)}, u32[]{:S(2)}) collective-permute-start(bf16[24,3584]{1,0:T(8,128)(2,1)} %get-tuple-element.66), channel_id=1, source_target_pairs={{0,24},{1,25},{2,26},{3,27},{4,28},{5,29},{6,30},{7,31},{8,0},{9,1... | collective-permute-start | bytes 516104 | tf_op jit(solution)/shard_map/ppermute | solution.py:30
  42.9 18.8 %collective-permute-start.10 = (bf16[128,1792]{1,0:T(8,128)(2,1)}, bf16[128,1792]{1,0:T(8,128)(2,1)S(1)}, u32[]{:S(2)}, u32[]{:S(2)}) collective-permute-start(bf16[128,1792]{1,0:T(8,128)(2,1)} %get-tuple-element.60), channel_id=1, source_target_pairs={{0,1},{1,2},{2,3},{3,0},{4,5},{5,6},{6,7},{7,4},{8,9},{9,10},{10,1... | collective-permute-start | bytes 1376264 | tf_op jit(solution)/shard_map/ppermute | solution.py:24
  47.6 19.3 %collective-permute-start.11 = (bf16[128,1792]{1,0:T(8,128)(2,1)}, bf16[128,1792]{1,0:T(8,128)(2,1)S(1)}, u32[]{:S(2)}, u32[]{:S(2)}) collective-permute-start(bf16[128,1792]{1,0:T(8,128)(2,1)} %get-tuple-element.60), channel_id=1, source_target_pairs={{0,3},{1,0},{2,1},{3,2},{4,7},{5,4},{6,5},{7,6},{8,11},{9,8},{10,9... | collective-permute-start | bytes 1376264 | tf_op jit(solution)/shard_map/ppermute | solution.py:24
  52.4 27.5 %collective-permute-start.19 = (bf16[128,1792]{1,0:T(8,128)(2,1)}, bf16[128,1792]{1,0:T(8,128)(2,1)S(1)}, u32[]{:S(2)}, u32[]{:S(2)}) collective-permute-start(bf16[128,1792]{1,0:T(8,128)(2,1)} %get-tuple-element.63), channel_id=1, source_target_pairs={{0,1},{1,2},{2,3},{3,0},{4,5},{5,6},{6,7},{7,4},{8,9},{9,10},{10,1... | collective-permute-start | bytes 1376264 | tf_op jit(solution)/shard_map/ppermute | solution.py:24
  61.7 21.2 %collective-permute-start.20 = (bf16[128,1792]{1,0:T(8,128)(2,1)S(1)}, bf16[128,1792]{1,0:T(8,128)(2,1)S(1)}, u32[]{:S(2)}, u32[]{:S(2)}) collective-permute-start(bf16[128,1792]{1,0:T(8,128)(2,1)S(1)} %copy-done.8), channel_id=1, source_target_pairs={{0,3},{1,0},{2,1},{3,2},{4,7},{5,4},{6,5},{7,6},{8,11},{9,8},{10,9... | collective-permute-start | bytes 1376264 | tf_op jit(solution)/shard_map/ppermute | solution.py:24
  66.9 102.1 %collective-permute-start.29 = (f32[32,96]{0,1:T(8,128)}, f32[32,96]{0,1:T(8,128)S(1)}, u32[]{:S(2)}, u32[]{:S(2)}) collective-permute-start(f32[32,96]{0,1:T(8,128)} %reshape.349), channel_id=1, source_target_pairs={{0,480},{1,481},{2,482},{3,483},{4,484},{5,485},{6,486},{7,487},{8... | collective-permute-start | bytes 36872 | tf_op jit(solution)/shard_map/ppermute | solution.py:49
  79.9 31.4 %collective-permute-start.5 = (bf16[96,3584]{1,0:T(8,128)(2,1)S(1)}, bf16[96,3584]{1,0:T(8,128)(2,1)S(1)}, u32[]{:S(2)}, u32[]{:S(2)}) collective-permute-start(bf16[96,3584]{1,0:T(8,128)(2,1)S(1)} %pad_maximum_fusion.1), channel_id=1, source_target_pairs={{0,4},{1,5},{2,6},{3,7},{4,0},{5,1},{6,2},{7,3},{8,12},{9,13},{10,... | collective-permute-start | bytes 2064392 | tf_op jit(solution)/shard_map/ppermute | solution.py:35
  106.7 27.8 %collective-permute-start.22 = (bf16[64,1792]{1,0:T(8,128)(2,1)S(1)}, bf16[64,1792]{1,0:T(8,128)(2,1)S(1)}, u32[]{:S(2)}, u32[]{:S(2)}) collective-permute-start(bf16[64,1792]{1,0:T(8,128)(2,1)S(1)} %slice.357), channel_id=1, source_target_pairs={{0,3},{1,0},{2,1},{3,2},{4,7},{5,4},{6,5},{7,6},{8,11},{9,8},{10,9... | collective-permute-start | bytes 688136 | tf_op jit(solution)/shard_map/ppermute | solution.py:24
  112.1 15.6 %collective-permute-start.9 = (bf16[1792,256]{1,0:T(8,128)(2,1)S(1)}, bf16[1792,256]{1,0:T(8,128)(2,1)S(1)}, u32[]{:S(2)}, u32[]{:S(2)}) collective-permute-start(bf16[1792,256]{1,0:T(8,128)(2,1)S(1)} %slice.341), channel_id=1, source_target_pairs={{0,3},{1,0},{2,1},{3,2},{4,7},{5,4},{6,5},{7,6},{8,11},{9,8},{10,9... | collective-permute-start | bytes 2752520 | tf_op jit(solution)/shard_map/ppermute | solution.py:24
  135.1 25.4 %collective-permute-start.23 = (bf16[96,1792]{1,0:T(8,128)(2,1)S(1)}, bf16[96,1792]{1,0:T(8,128)(2,1)S(1)}, u32[]{:S(2)}, u32[]{:S(2)}) collective-permute-start(bf16[96,1792]{1,0:T(8,128)(2,1)S(1)} %slice.409), channel_id=1, source_target_pairs={{0,4},{1,5},{2,6},{3,7},{4,0},{5,1},{6,2},{7,3},{8,12},{9,13},{10,... | collective-permute-start | bytes 1032200 | tf_op jit(solution)/shard_map/ppermute | solution.py:35
  141.6 29.4 %collective-permute-start.30 = (bf16[24,896]{1,0:T(8,128)(2,1)S(1)}, bf16[24,896]{1,0:T(8,128)(2,1)S(1)}, u32[]{:S(2)}, u32[]{:S(2)}) collective-permute-start(bf16[24,896]{1,0:T(8,128)(2,1)S(1)} %bitcast.127), channel_id=1, source_target_pairs={{0,480},{1,481},{2,482},{3,483},{4,484},{5,485},{6,486},{7,487},{8... | collective-permute-start | bytes 129032 | tf_op jit(solution)/shard_map/ppermute | solution.py:49
  149.4 36.1 %collective-permute-start.31 = (bf16[24,896]{1,0:T(8,128)(2,1)S(1)}, bf16[24,896]{1,0:T(8,128)(2,1)S(1)}, u32[]{:S(2)}, u32[]{:S(2)}) collective-permute-start(bf16[24,896]{1,0:T(8,128)(2,1)S(1)} %bitcast.125), channel_id=1, source_target_pairs={{0,504},{1,505},{2,506},{3,507},{4,508},{5,509},{6,510},{7,511},{8... | collective-permute-start | bytes 129032 | tf_op jit(solution)/shard_map/ppermute | solution.py:49
  158.5 28.9 %collective-permute-start.32 = (bf16[24,896]{1,0:T(8,128)(2,1)S(1)}, bf16[24,896]{1,0:T(8,128)(2,1)S(1)}, u32[]{:S(2)}, u32[]{:S(2)}) collective-permute-start(bf16[24,896]{1,0:T(8,128)(2,1)S(1)} %bitcast.124), channel_id=1, source_target_pairs={{0,496},{1,497},{2,498},{3,499},{4,500},{5,501},{6,502},{7,503},{8... | collective-permute-start | bytes 129032 | tf_op jit(solution)/shard_map/ppermute | solution.py:49
  160.5 28.9 %collective-permute-start.33 = (bf16[24,896]{1,0:T(8,128)(2,1)S(1)}, bf16[24,896]{1,0:T(8,128)(2,1)S(1)}, u32[]{:S(2)}, u32[]{:S(2)}) collective-permute-start(bf16[24,896]{1,0:T(8,128)(2,1)S(1)} %bitcast.123), channel_id=1, source_target_pairs={{0,488},{1,489},{2,490},{3,491},{4,492},{5,493},{6,494},{7,495},{8... | collective-permute-start | bytes 129032 | tf_op jit(solution)/shard_map/ppermute | solution.py:49
  169.1 48.4 %collective-permute-start.1 = (f32[32,96]{0,1:T(8,128)S(1)}, f32[32,96]{0,1:T(8,128)S(1)}, u32[]{:S(2)}, u32[]{:S(2)}) collective-permute-start(f32[32,96]{0,1:T(8,128)S(1)} %copy-done.10), channel_id=1, source_target_pairs={{0,32},{1,33},{2,34},{3,35},{4,36},{5,37},{6,38},{7,39},{8,40},{9,... | collective-permute-start | bytes 36872 | tf_op jit(solution)/shard_map/ppermute | solution.py:49
  171.0 20.6 %collective-permute-start.34 = (bf16[24,896]{1,0:T(8,128)(2,1)S(1)}, bf16[24,896]{1,0:T(8,128)(2,1)S(1)}, u32[]{:S(2)}, u32[]{:S(2)}) collective-permute-start(bf16[24,896]{1,0:T(8,128)(2,1)S(1)} %bitcast.128), channel_id=1, source_target_pairs={{0,480},{1,481},{2,482},{3,483},{4,484},{5,485},{6,486},{7,487},{8... | collective-permute-start | bytes 129032 | tf_op jit(solution)/shard_map/ppermute | solution.py:49
  187.4 15.4 %collective-permute-start.36 = (bf16[24,896]{1,0:T(8,128)(2,1)S(1)}, bf16[24,896]{1,0:T(8,128)(2,1)S(1)}, u32[]{:S(2)}, u32[]{:S(2)}) collective-permute-start(bf16[24,896]{1,0:T(8,128)(2,1)S(1)} %bitcast.122), channel_id=1, source_target_pairs={{0,496},{1,497},{2,498},{3,499},{4,500},{5,501},{6,502},{7,503},{8... | collective-permute-start | bytes 129032 | tf_op jit(solution)/shard_map/ppermute | solution.py:49
  189.4 17.5 %collective-permute-start.37 = (bf16[24,896]{1,0:T(8,128)(2,1)S(1)}, bf16[24,896]{1,0:T(8,128)(2,1)S(1)}, u32[]{:S(2)}, u32[]{:S(2)}) collective-permute-start(bf16[24,896]{1,0:T(8,128)(2,1)S(1)} %bitcast.121), channel_id=1, source_target_pairs={{0,488},{1,489},{2,490},{3,491},{4,492},{5,493},{6,494},{7,495},{8... | collective-permute-start | bytes 129032 | tf_op jit(solution)/shard_map/ppermute | solution.py:49
  191.6 37.1 %collective-permute-start.15 = (bf16[24,896]{1,0:T(8,128)(2,1)S(1)}, bf16[24,896]{1,0:T(8,128)(2,1)S(1)}, u32[]{:S(2)}, u32[]{:S(2)}) collective-permute-start(bf16[24,896]{1,0:T(8,128)(2,1)S(1)} %bitcast.120), channel_id=1, source_target_pairs={{0,32},{1,33},{2,34},{3,35},{4,36},{5,37},{6,38},{7,39},{8,40},{9,... | collective-permute-start | bytes 129032 | tf_op jit(solution)/shard_map/ppermute | solution.py:49
  194.5 36.2 %collective-permute-start.16 = (bf16[24,896]{1,0:T(8,128)(2,1)S(1)}, bf16[24,896]{1,0:T(8,128)(2,1)S(1)}, u32[]{:S(2)}, u32[]{:S(2)}) collective-permute-start(bf16[24,896]{1,0:T(8,128)(2,1)S(1)} %bitcast.119), channel_id=1, source_target_pairs={{0,56},{1,57},{2,58},{3,59},{4,60},{5,61},{6,62},{7,63},{8,32},{9,... | collective-permute-start | bytes 129032 | tf_op jit(solution)/shard_map/ppermute | solution.py:49
  202.8 29.8 %collective-permute-start.17 = (bf16[24,896]{1,0:T(8,128)(2,1)S(1)}, bf16[24,896]{1,0:T(8,128)(2,1)S(1)}, u32[]{:S(2)}, u32[]{:S(2)}) collective-permute-start(bf16[24,896]{1,0:T(8,128)(2,1)S(1)} %bitcast.118), channel_id=1, source_target_pairs={{0,48},{1,49},{2,50},{3,51},{4,52},{5,53},{6,54},{7,55},{8,56},{9,... | collective-permute-start | bytes 129032 | tf_op jit(solution)/shard_map/ppermute | solution.py:49
  206.9 27.7 %collective-permute-start.18 = (bf16[24,896]{1,0:T(8,128)(2,1)S(1)}, bf16[24,896]{1,0:T(8,128)(2,1)S(1)}, u32[]{:S(2)}, u32[]{:S(2)}) collective-permute-start(bf16[24,896]{1,0:T(8,128)(2,1)S(1)} %bitcast.117), channel_id=1, source_target_pairs={{0,40},{1,41},{2,42},{3,43},{4,44},{5,45},{6,46},{7,47},{8,48},{9,... | collective-permute-start | bytes 129032 | tf_op jit(solution)/shard_map/ppermute | solution.py:49
  217.4 33.0 %collective-permute-start.28 = (bf16[16,3584]{1,0:T(8,128)(2,1)S(1)}, bf16[16,3584]{1,0:T(8,128)(2,1)S(1)}, u32[]{:S(2)}, u32[]{:S(2)}) collective-permute-start(bf16[16,3584]{1,0:T(8,128)(2,1)S(1)} %bitcast.111), channel_id=1, source_target_pairs={{0,480},{1,481},{2,482},{3,483},{4,484},{5,485},{6,486},{7,487},{8... | collective-permute-start | bytes 344072 | tf_op jit(solution)/shard_map/ppermute | solution.py:49
  228.8 17.7 %collective-permute-start.24 = (bf16[24,896]{1,0:T(8,128)(2,1)S(1)}, bf16[24,896]{1,0:T(8,128)(2,1)S(1)}, u32[]{:S(2)}, u32[]{:S(2)}) collective-permute-start(bf16[24,896]{1,0:T(8,128)(2,1)S(1)} %bitcast.116), channel_id=1, source_target_pairs={{0,32},{1,33},{2,34},{3,35},{4,36},{5,37},{6,38},{7,39},{8,40},{9,... | collective-permute-start | bytes 129032 | tf_op jit(solution)/shard_map/ppermute | solution.py:49
  230.7 17.7 %collective-permute-start.25 = (bf16[24,896]{1,0:T(8,128)(2,1)S(1)}, bf16[24,896]{1,0:T(8,128)(2,1)S(1)}, u32[]{:S(2)}, u32[]{:S(2)}) collective-permute-start(bf16[24,896]{1,0:T(8,128)(2,1)S(1)} %bitcast.115), channel_id=1, source_target_pairs={{0,56},{1,57},{2,58},{3,59},{4,60},{5,61},{6,62},{7,63},{8,32},{9,... | collective-permute-start | bytes 129032 | tf_op jit(solution)/shard_map/ppermute | solution.py:49
  232.6 15.8 %collective-permute-start.26 = (bf16[24,896]{1,0:T(8,128)(2,1)S(1)}, bf16[24,896]{1,0:T(8,128)(2,1)S(1)}, u32[]{:S(2)}, u32[]{:S(2)}) collective-permute-start(bf16[24,896]{1,0:T(8,128)(2,1)S(1)} %bitcast.114), channel_id=1, source_target_pairs={{0,48},{1,49},{2,50},{3,51},{4,52},{5,53},{6,54},{7,55},{8,56},{9,... | collective-permute-start | bytes 129032 | tf_op jit(solution)/shard_map/ppermute | solution.py:49
  234.6 15.6 %collective-permute-start.27 = (bf16[24,896]{1,0:T(8,128)(2,1)S(1)}, bf16[24,896]{1,0:T(8,128)(2,1)S(1)}, u32[]{:S(2)}, u32[]{:S(2)}) collective-permute-start(bf16[24,896]{1,0:T(8,128)(2,1)S(1)} %bitcast.113), channel_id=1, source_target_pairs={{0,40},{1,41},{2,42},{3,43},{4,44},{5,45},{6,46},{7,47},{8,48},{9,... | collective-permute-start | bytes 129032 | tf_op jit(solution)/shard_map/ppermute | solution.py:49
  246.5 16.9 %collective-permute-start = (bf16[16,3584]{1,0:T(8,128)(2,1)S(1)}, bf16[16,3584]{1,0:T(8,128)(2,1)S(1)}, u32[]{:S(2)}, u32[]{:S(2)}) collective-permute-start(bf16[16,3584]{1,0:T(8,128)(2,1)S(1)} %bitcast.112), channel_id=1, source_target_pairs={{0,32},{1,33},{2,34},{3,35},{4,36},{5,37},{6,38},{7,39},{8,40},{9,... | collective-permute-start | bytes 344072 | tf_op jit(solution)/shard_map/ppermute | solution.py:49
  (26 other events, 394.6 us)

commit v2 on v1

v2 whole, which is shorter than its diff:
```python
import jax
import jax.numpy as jnp
from jax import lax
from jax.sharding import PartitionSpec as P

CAP = 12
ALONG_X = 4

route_scale = 2.5


def index_of(z, x):
    return z * ALONG_X + x


def places():
    columns = lax.axis_size("expert") // ALONG_X
    return [(z, x) for z in range(columns) for x in range(ALONG_X)]


def along_z(block, step):
    columns = lax.axis_size("expert") // ALONG_X
    route = [(index_of(z, x), index_of((z + step) % columns, x)) for z, x in places()]
    return lax.ppermute(block, "expert", route)


def to_section(block, section_step, z_step):
    sections, devices = lax.axis_size("pipe"), lax.axis_size("expert")
    columns = devices // ALONG_X
    route = [
        (
            s * devices + index_of(z, x),
            (s + section_step) % sections * devices + index_of((z + z_step) % columns, x),
        )
        for s in range(sections)
        for z, x in places()
    ]
    return lax.ppermute(block, ("pipe", "expert"), route)


def facing(block, z_flip, x_flip):
    route = [(index_of(z, x), index_of(z ^ z_flip, x ^ x_flip)) for z, x in places()]
    return lax.ppermute(block, "expert", route)


def ring_gather(block):
    columns = lax.axis_size("expert") // ALONG_X
    rings = [[index_of(z, x) for x in range(ALONG_X)] for z in range(columns)]
    return lax.all_gather(block, "expert", axis=0, tiled=True, axis_index_groups=rings)


def prepare(x, routes, gain, router, group):
    xf = x.astype(jnp.float32)
    mean_sq = jnp.mean(xf * xf, axis=-1, keepdims=True)
    normed = (xf * lax.rsqrt(mean_sq + 1e-06) * gain).astype(jnp.bfloat16)
    logits = jnp.dot(normed, router, preferred_element_type=jnp.float32)
    affinity = jax.nn.sigmoid(logits)
    experts_n = router.shape[1]
    hits = routes[:, :, None] == jnp.arange(experts_n, dtype=jnp.int32)
    picked = jnp.sum(jnp.where(hits, affinity[:, None, :], 0.0), axis=2)
    weights = picked / jnp.sum(picked, axis=1, keepdims=True) * route_scale
    named = jnp.any(hits, axis=1)
    share = jnp.sum(jnp.where(hits, weights[:, :, None], 0.0), axis=1)
    count = named.astype(jnp.int32)
    before = jnp.cumsum(count, axis=0) - count
    turn = jnp.mod(jnp.arange(experts_n, dtype=jnp.int32) + group, experts_n)
    rolled = turn[:, None] == jnp.arange(experts_n, dtype=jnp.int32)
    pick = lambda v: jnp.sum(jnp.where(rolled, v[:, None, :], jnp.zeros((), v.dtype)), axis=2)
    slot = jnp.where(pick(count) > 0, pick(before), -1)
    chosen = slot[:, :, None] == jnp.arange(CAP, dtype=jnp.int32)
    combine = jnp.where(chosen, pick(share)[:, :, None], 0.0)
    return normed, chosen, combine


def in_terms(value):
    high = value.astype(jnp.bfloat16)
    rest = value - high.astype(jnp.float32)
    middle = rest.astype(jnp.bfloat16)
    low = (rest - middle.astype(jnp.float32)).astype(jnp.bfloat16)
    return [high, middle, low]


def on_device(act_down, act_up, routes_down, routes_up, norm_gain, router_w, w_gate, w_up, w_down):
    experts_n = router_w.shape[2]
    width = act_down.shape[2]
    rows_n = act_down.shape[1]
    slots = experts_n * CAP
    piece = width // 2
    gain = norm_gain[0]
    router = router_w[0]
    hidden_n = w_down.shape[1]
    place = lax.axis_index("expert")
    group = place // ALONG_X // 2
    column = place % ALONG_X

    both_cols = jnp.concatenate([w_gate[0], w_up[0]], axis=1)
    next_cols = facing(both_cols, 0, 1)
    down_rows = ring_gather(w_down[0])

    normed_d, chosen_d, combine_d = prepare(act_down[0], routes_down[0], gain, router, group)
    normed_u, chosen_u, combine_u = prepare(act_up[0], routes_up[0], gain, router, group)
    select = jnp.stack(
        [jnp.pad(chosen_d, ((0, rows_n), (0, 0), (0, 0))), jnp.pad(chosen_u, ((rows_n, 0), (0, 0), (0, 0)))],
        axis=2,
    ).reshape(2 * rows_n, 2 * slots)
    packed = lax.dot_general(
        select.astype(jnp.bfloat16),
        jnp.concatenate([normed_d, normed_u], axis=0),
        (((0,), (0,)), ((), ())),
        preferred_element_type=jnp.float32,
    ).astype(jnp.bfloat16)

    def ahead(x, combine, step):
        terms = in_terms(combine.reshape(rows_n, slots))
        pad = jnp.zeros((rows_n, -(-3 * slots // 128) * 128 - 3 * slots), jnp.bfloat16)
        sent = to_section(jnp.concatenate([x] + terms + [pad], axis=1), step, 0)
        share = sum(sent[:, width + i * slots:width + (i + 1) * slots].astype(jnp.float32) for i in range(3))
        share = share.reshape(1, rows_n, experts_n, 1, CAP) * jnp.eye(2, dtype=jnp.float32).reshape(2, 1, 1, 2, 1)
        return sent[:, :width], share.reshape(2 * rows_n, 2 * slots)

    res_down, mix_down = ahead(act_down[0], combine_d, 1)
    res_up, mix_up = ahead(act_up[0], combine_u, -1)

    chunk = 2 * CAP
    near = [packed[:chunk]] + [
        along_z(packed[s * chunk:(s + 1) * chunk], 2 * s) for s in range(1, experts_n)
    ]
    mine = jnp.concatenate([c[:CAP] for c in near] + [c[CAP:] for c in near], axis=0)
    mine, res_down, res_up = lax.optimization_barrier((mine, res_down, res_up))
    rows = [mine, facing(mine, 1, 0), facing(mine, 0, 3), facing(mine, 1, 3)]

    dot = lambda a, b: jnp.dot(a, b, preferred_element_type=jnp.float32)
    act = lambda joined: (jax.nn.silu(joined[:, :hidden_n]) * joined[:, hidden_n:]).astype(jnp.bfloat16)
    near_rows = jnp.concatenate(rows[:2], axis=0)
    far_rows = jnp.concatenate(rows[2:], axis=0)
    sent = jnp.concatenate([act(dot(far_rows, both_cols)), act(dot(far_rows, next_cols))], axis=1)
    kept = [act(dot(near_rows, both_cols)), act(dot(near_rows, next_cols))]
    sent, down_rows = lax.optimization_barrier((sent, down_rows))
    got = facing(sent, 0, 3)
    blocks = kept + [got[:, hidden_n:], got[:, :hidden_n]]
    for bit in (1, 2):
        flip = (column & bit) > 0
        blocks = [jnp.where(flip, blocks[i ^ bit], blocks[i]) for i in range(ALONG_X)]
    total = dot(jnp.concatenate(blocks, axis=1), down_rows)

    def send_back(own, theirs, step):
        summed = (own + facing(theirs.astype(jnp.bfloat16), 1, 0).astype(jnp.float32)).astype(jnp.bfloat16)
        summed = summed.reshape(experts_n, CAP, 2, piece).transpose(0, 2, 1, 3).reshape(experts_n, chunk, piece)
        return jnp.concatenate([to_section(summed[s], step, -2 * s) for s in range(experts_n)], axis=0)

    back_down = send_back(total[:slots], total[2 * slots:3 * slots], 1)
    back_up = send_back(total[slots:2 * slots], total[3 * slots:], -1)

    def finish(residual, mix, back):
        mixed = jnp.dot(
            mix, back.astype(jnp.float32), precision=lax.Precision.HIGHEST, preferred_element_type=jnp.float32
        )
        mixed = jnp.concatenate([mixed[:rows_n], mixed[rows_n:]], axis=1)
        return (residual.astype(jnp.float32) + mixed).astype(jnp.bfloat16)[None]

    return finish(res_down, mix_down, back_down), finish(res_up, mix_up, back_up)


def solution(mesh):
    placed = (
        P("pipe", "expert", None),
        P("pipe", "expert", None),
        P("pipe", "expert", None),
        P("pipe", "expert", None),
        P("pipe", None),
        P("pipe", None, None),
        P("pipe", None, "expert"),
        P("pipe", None, "expert"),
        P("pipe", "expert", None),
    )
    return jax.shard_map(
        on_device,
        mesh=mesh,
        in_specs=placed,
        out_specs=(P("pipe", "expert", None), P("pipe", "expert", None)),
        check_vma=False,
    )
```

time: 266 us -> 222 us (0.83)
  the two profiles are of different devices: /device:TPU:66 before, /device:TPU:1 now
where the time goes in v2:
time: 222 us; the launch traced here: 221 us
  starting transfers between devices  84 us (38%)
  waiting for transfers between devices  83.6 us (38%)
  local copies, waits for them, and re-layouts  23 us (10%)
  between operations  14.8 us (7%)
  other arithmetic  10.4 us (5%)
  matrix products  5.16 us (2%)
    ppermute x7, waiting for transfers between devices, facing(): return lax.ppermute(block, 'expert', route)  53.3 us
    ppermute x10, starting transfers between devices, to_section(): return lax.ppermute(block, ('pipe', 'expert'), route)  47.1 us
    ppermute x7, starting transfers between devices, facing(): return lax.ppermute(block, 'expert', route)  20.4 us
    ppermute x3, starting transfers between devices, along_z(): return lax.ppermute(block, 'expert', route)  16.5 us
    concatenate x1, local copies, waits for them, and re-layouts, on_device(): jnp.concatenate([c[:CAP] for c in near] + [c[CAP:] for c in near], axis=0)  11.6 us
    ppermute x10, waiting for transfers between devices, to_section(): return lax.ppermute(block, ('pipe', 'expert'), route)  11.3 us
    all_gather x1, waiting for transfers between devices, ring_gather(): lax.all_gather(block, 'expert', axis=0, tiled=True, axis_index_groups=rings)  9.77 us
    ppermute x3, waiting for transfers between devices, along_z(): return lax.ppermute(block, 'expert', route)  9.22 us
  transfers between devices with their start and end apart: 21, of which 9 were waited for; matrix products, arithmetic and copies ran while one was open for 12% of the time, Pallas kernels for 0%

profile of v2, /device:TPU:1, one launch (start us, length us, event | category | flops | bytes accessed | tf_op | source)
XLA Modules:
  0.0 221.0 jit_solution(10729498495321346333)
XLA Ops:
  14.9 12.3 %collective-permute-start.2 = (bf16[24,3584]{1,0:T(8,128)(2,1)}, bf16[24,3584]{1,0:T(8,128)(2,1)}, u32[]{:S(2)}, u32[]{:S(2)}) collective-permute-start(bf16[24,3584]{1,0:T(8,128)(2,1)} %get-tuple-element.35), channel_id=1, source_target_pairs={{0,24},{1,25},{2,26},{3,27},{4,28},{5,29},{6,30},{7,31},{8,0},{9,1... | collective-permute-start | bytes 516104 | tf_op jit(solution)/shard_map/ppermute | solution.py:24
  27.2 1.9 collective-permute-start.1
  29.2 2.2 collective-permute-start
  33.9 4.3 %collective-permute-start.3 = (bf16[16,3840]{1,0:T(8,128)(2,1)}, bf16[16,3840]{1,0:T(8,128)(2,1)S(1)}, u32[]{:S(2)}, u32[]{:S(2)}) collective-permute-start(bf16[16,3840]{1,0:T(8,128)(2,1)} %concatenate.41), channel_id=1, source_target_pairs={{0,32},{1,33},{2,34},{3,35},{4,36},{5,37},{6,38},{7,39},{8,40},{9,... | collective-permute-start | bytes 368648 | tf_op jit(solution)/shard_map/ppermute | solution.py:38
  39.0 1.9 collective-permute-start.4
  41.0 1.5 pad_maximum_fusion
  42.5 3.1 %collective-permute-start.7 = (bf16[3584,256]{1,0:T(8,128)(2,1)}, bf16[3584,256]{1,0:T(8,128)(2,1)S(1)}, u32[]{:S(2)}, u32[]{:S(2)}) collective-permute-start(bf16[3584,256]{1,0:T(8,128)(2,1)} %pad_maximum_fusion), channel_id=1, source_target_pairs={{0,1},{1,0},{2,3},{3,2},{4,5},{5,4},{6,7},{7,6},{8,9},{9,8},{10,11... | collective-permute-start | bytes 5505032 | tf_op jit(solution)/shard_map/ppermute | solution.py:43
  46.8 9.2 %collective-permute-done.1 = bf16[24,3584]{1,0:T(8,128)(2,1)} collective-permute-done((bf16[24,3584]{1,0:T(8,128)(2,1)}, bf16[24,3584]{1,0:T(8,128)(2,1)}, u32[]{:S(2)}, u32[]{:S(2)}) %collective-permute-start.1) | collective-permute-done | bytes 172064 | tf_op jit(solution)/shard_map/ppermute | solution.py:24
  57.1 11.6 %concatenate.40 = bf16[96,3584]{1,0:T(8,128)(2,1)} concatenate(bf16[12,3584]{1,0:T(8,128)(2,1)S(1)} %get-tuple-element.34, bf16[12,3584]{1,0:T(8,128)(2,1)S(1)} %get-tuple-element.58, bf16[12,3584]{1,0:T(8,128)(2,1)S(1)} %get-tuple-element.56, bf16[12,3584]{1,0:T(8,128)(2,1)S(1)} %get-tuple-element.54, bf16[12,3584]{1,0:T(8,128)(2,1)S(1)} %get-tuple-element.33, ...), dimensions={0} | concatenate | bytes 1376256 | tf_op jit(solution)/shard_map/concatenate | solution.py:128
  68.7 4.4 %collective-permute-start.5 = (bf16[96,3584]{1,0:T(8,128)(2,1)}, bf16[96,3584]{1,0:T(8,128)(2,1)}, u32[]{:S(2)}, u32[]{:S(2)}) collective-permute-start(bf16[96,3584]{1,0:T(8,128)(2,1)} %concatenate.40), channel_id=1, source_target_pairs={{0,3},{1,2},{2,1},{3,0},{4,7},{5,6},{6,5},{7,4},{8,11},{9,10},{10,... | collective-permute-start | bytes 2064392 | tf_op jit(solution)/shard_map/ppermute | solution.py:43
  73.4 2.1 collective-permute-start.6
  76.6 3.3 %collective-permute-start.9 = (bf16[96,3584]{1,0:T(8,128)(2,1)}, bf16[96,3584]{1,0:T(8,128)(2,1)S(1)}, u32[]{:S(2)}, u32[]{:S(2)}) collective-permute-start(bf16[96,3584]{1,0:T(8,128)(2,1)} %concatenate.40), channel_id=1, source_target_pairs={{0,4},{1,5},{2,6},{3,7},{4,0},{5,1},{6,2},{7,3},{8,12},{9,13},{10,... | collective-permute-start | bytes 2064392 | tf_op jit(solution)/shard_map/ppermute | solution.py:43
  79.9 38.2 %collective-permute-done.5 = bf16[96,3584]{1,0:T(8,128)(2,1)} collective-permute-done((bf16[96,3584]{1,0:T(8,128)(2,1)}, bf16[96,3584]{1,0:T(8,128)(2,1)}, u32[]{:S(2)}, u32[]{:S(2)}) %collective-permute-start.5) | collective-permute-done | bytes 688160 | tf_op jit(solution)/shard_map/ppermute | solution.py:43
  120.0 1.2 fusion.68
  121.9 9.8 %all-gather.3.cloned.1.call-done = bf16[1,512,3584]{2,1,0:T(8,128)(2,1)} async-done(((bf16[1,128,3584]{2,1,0:T(8,128)(2,1)}), bf16[1,512,3584]{2,1,0:T(8,128)(2,1)}) %all-gather.3.cloned.1.call-update) | async-done | bytes 3670032 | tf_op jit(solution)/shard_map/all_gather | solution.py:49
  131.6 2.2 collective-permute-start.8
  134.3 4.1 %collective-permute-done.8 = bf16[192,256]{1,0:T(8,128)(2,1)S(1)} collective-permute-done((bf16[192,256]{1,0:T(8,128)(2,1)S(1)}, bf16[192,256]{1,0:T(8,128)(2,1)S(1)}, u32[]{:S(2)}, u32[]{:S(2)}) %collective-permute-start.8) | collective-permute-done | bytes 98336 | tf_op jit(solution)/shard_map/ppermute | solution.py:43
  140.4 3.5 %collective-permute-start.10 = (bf16[48,3584]{1,0:T(8,128)(2,1)}, bf16[48,3584]{1,0:T(8,128)(2,1)}, u32[]{:S(2)}, u32[]{:S(2)}) collective-permute-start(bf16[48,3584]{1,0:T(8,128)(2,1)} %get-tuple-element.32), channel_id=1, source_target_pairs={{0,4},{1,5},{2,6},{3,7},{4,0},{5,1},{6,2},{7,3},{8,12},{9,13},{10,... | collective-permute-start | bytes 1032200 | tf_op jit(solution)/shard_map/ppermute | solution.py:43
  144.0 1.9 collective-permute-start.15
  147.1 3.6 %collective-permute-done.10 = bf16[48,3584]{1,0:T(8,128)(2,1)} collective-permute-done((bf16[48,3584]{1,0:T(8,128)(2,1)}, bf16[48,3584]{1,0:T(8,128)(2,1)}, u32[]{:S(2)}, u32[]{:S(2)}) %collective-permute-start.10) | collective-permute-done | bytes 344096 | tf_op jit(solution)/shard_map/ppermute | solution.py:43
  150.7 7.4 %collective-permute-done.15 = bf16[48,3584]{1,0:T(8,128)(2,1)} collective-permute-done((bf16[48,3584]{1,0:T(8,128)(2,1)}, bf16[48,3584]{1,0:T(8,128)(2,1)}, u32[]{:S(2)}, u32[]{:S(2)}) %collective-permute-start.15) | collective-permute-done | bytes 344096 | tf_op jit(solution)/shard_map/ppermute | solution.py:43
  158.1 1.2 fusion.6
  159.5 4.5 %collective-permute-start.16 = (bf16[24,1792]{1,0:T(8,128)(2,1)S(1)}, bf16[24,1792]{1,0:T(8,128)(2,1)S(1)}, u32[]{:S(2)}, u32[]{:S(2)}) collective-permute-start(bf16[24,1792]{1,0:T(8,128)(2,1)S(1)} %squeeze.54), channel_id=1, source_target_pairs={{0,480},{1,481},{2,482},{3,483},{4,484},{5,485},{6,486},{7,487},{8... | collective-permute-start | bytes 258056 | tf_op jit(solution)/shard_map/ppermute | solution.py:38
  164.1 13.0 %collective-permute-start.17 = (bf16[24,1792]{1,0:T(8,128)(2,1)S(1)}, bf16[24,1792]{1,0:T(8,128)(2,1)S(1)}, u32[]{:S(2)}, u32[]{:S(2)}) collective-permute-start(bf16[24,1792]{1,0:T(8,128)(2,1)S(1)} %squeeze.55), channel_id=1, source_target_pairs={{0,504},{1,505},{2,506},{3,507},{4,508},{5,509},{6,510},{7,511},{8... | collective-permute-start | bytes 258056 | tf_op jit(solution)/shard_map/ppermute | solution.py:38
  177.2 4.3 %collective-permute-start.18 = (bf16[24,1792]{1,0:T(8,128)(2,1)S(1)}, bf16[24,1792]{1,0:T(8,128)(2,1)S(1)}, u32[]{:S(2)}, u32[]{:S(2)}) collective-permute-start(bf16[24,1792]{1,0:T(8,128)(2,1)S(1)} %squeeze.56), channel_id=1, source_target_pairs={{0,496},{1,497},{2,498},{3,499},{4,500},{5,501},{6,502},{7,503},{8... | collective-permute-start | bytes 258056 | tf_op jit(solution)/shard_map/ppermute | solution.py:38
  181.5 1.9 collective-permute-start.19
  183.6 3.9 %collective-permute-start.11 = (bf16[24,1792]{1,0:T(8,128)(2,1)S(1)}, bf16[24,1792]{1,0:T(8,128)(2,1)S(1)}, u32[]{:S(2)}, u32[]{:S(2)}) collective-permute-start(bf16[24,1792]{1,0:T(8,128)(2,1)S(1)} %squeeze.50), channel_id=1, source_target_pairs={{0,32},{1,33},{2,34},{3,35},{4,36},{5,37},{6,38},{7,39},{8,40},{9,... | collective-permute-start | bytes 258056 | tf_op jit(solution)/shard_map/ppermute | solution.py:38
  187.7 9.2 %collective-permute-start.12 = (bf16[24,1792]{1,0:T(8,128)(2,1)S(1)}, bf16[24,1792]{1,0:T(8,128)(2,1)S(1)}, u32[]{:S(2)}, u32[]{:S(2)}) collective-permute-start(bf16[24,1792]{1,0:T(8,128)(2,1)S(1)} %squeeze.51), channel_id=1, source_target_pairs={{0,56},{1,57},{2,58},{3,59},{4,60},{5,61},{6,62},{7,63},{8,32},{9,... | collective-permute-start | bytes 258056 | tf_op jit(solution)/shard_map/ppermute | solution.py:38
  196.9 1.9 collective-permute-start.13
  198.8 2.1 collective-permute-start.14
  201.3 7.7 %collective-permute-done.13 = bf16[24,1792]{1,0:T(8,128)(2,1)S(1)} collective-permute-done((bf16[24,1792]{1,0:T(8,128)(2,1)S(1)}, bf16[24,1792]{1,0:T(8,128)(2,1)S(1)}, u32[]{:S(2)}, u32[]{:S(2)}) %collective-permute-start.13) | collective-permute-done | bytes 86048 | tf_op jit(solution)/shard_map/ppermute | solution.py:38
  209.0 3.4 %collective-permute-done.14 = bf16[24,1792]{1,0:T(8,128)(2,1)S(1)} collective-permute-done((bf16[24,1792]{1,0:T(8,128)(2,1)S(1)}, bf16[24,1792]{1,0:T(8,128)(2,1)S(1)}, u32[]{:S(2)}, u32[]{:S(2)}) %collective-permute-start.14) | collective-permute-done | bytes 86048 | tf_op jit(solution)/shard_map/ppermute | solution.py:38
  (156 shorter events, 23.2 us)
Async XLA Ops:
  7.2 24.4 %copy-start = (bf16[1,3584,4]{1,2,0:T(4,128)(2,1)S(1)}, bf16[1,3584,4]{1,2,0:T(4,128)(2,1)}, u32[]{:S(2)}) copy-start(bf16[1,3584,4]{1,2,0:T(4,128)(2,1)} %param.14) | copy-start | bytes 86020
  7.2 24.6 %copy-start.3 = (bf16[1,16,3584]{2,1,0:T(8,128)(2,1)S(1)}, bf16[1,16,3584]{2,1,0:T(8,128)(2,1)}, u32[]{:S(2)}) copy-start(bf16[1,16,3584]{2,1,0:T(8,128)(2,1)} %param.10) | copy-start | bytes 344068
  7.2 124.4 %all-gather.3.cloned.1.call-start = ((), (), s32[]{:S(2)}) async-start(), calls=%async_computation | async-start | bytes 4587520 | tf_op jit(solution)/shard_map/all_gather | solution.py:49
  14.0 26.9 %copy-start.4 = (bf16[1,3584,128]{2,1,0:T(8,128)(2,1)S(1)}, bf16[1,3584,128]{2,1,0:T(8,128)(2,1)}, u32[]{:S(2)}) copy-start(bf16[1,3584,128]{2,1,0:T(8,128)(2,1)} %param.16) | copy-start | bytes 2752516
  14.0 26.9 %copy-start.6 = (bf16[1,3584,128]{2,1,0:T(8,128)(2,1)S(1)}, bf16[1,3584,128]{2,1,0:T(8,128)(2,1)}, u32[]{:S(2)}) copy-start(bf16[1,3584,128]{2,1,0:T(8,128)(2,1)} %param.15) | copy-start | bytes 2752516
  14.9 30.9 %collective-permute-start.2 = (bf16[24,3584]{1,0:T(8,128)(2,1)}, bf16[24,3584]{1,0:T(8,128)(2,1)}, u32[]{:S(2)}, u32[]{:S(2)}) collective-permute-start(bf16[24,3584]{1,0:T(8,128)(2,1)} %get-tuple-element.35), channel_id=1, source_target_pairs={{0,24},{1,25},{2,26},{3,27},{4,28},{5,29},{6,30},{7,31},{8,0},{9,1... | collective-permute-start | bytes 516104 | tf_op jit(solution)/shard_map/ppermute | solution.py:24
  27.2 28.8 %collective-permute-start.1 = (bf16[24,3584]{1,0:T(8,128)(2,1)}, bf16[24,3584]{1,0:T(8,128)(2,1)}, u32[]{:S(2)}, u32[]{:S(2)}) collective-permute-start(bf16[24,3584]{1,0:T(8,128)(2,1)} %get-tuple-element.36), channel_id=1, source_target_pairs={{0,16},{1,17},{2,18},{3,19},{4,20},{5,21},{6,22},{7,23},{8,24},{9,... | collective-permute-start | bytes 516104 | tf_op jit(solution)/shard_map/ppermute | solution.py:24
  29.2 27.9 %collective-permute-start = (bf16[24,3584]{1,0:T(8,128)(2,1)}, bf16[24,3584]{1,0:T(8,128)(2,1)S(1)}, u32[]{:S(2)}, u32[]{:S(2)}) collective-permute-start(bf16[24,3584]{1,0:T(8,128)(2,1)} %get-tuple-element.37), channel_id=1, source_target_pairs={{0,8},{1,9},{2,10},{3,11},{4,12},{5,13},{6,14},{7,15},{8,16},{9,17... | collective-permute-start | bytes 516104 | tf_op jit(solution)/shard_map/ppermute | solution.py:24
  33.9 8.6 %collective-permute-start.3 = (bf16[16,3840]{1,0:T(8,128)(2,1)}, bf16[16,3840]{1,0:T(8,128)(2,1)S(1)}, u32[]{:S(2)}, u32[]{:S(2)}) collective-permute-start(bf16[16,3840]{1,0:T(8,128)(2,1)} %concatenate.41), channel_id=1, source_target_pairs={{0,32},{1,33},{2,34},{3,35},{4,36},{5,37},{6,38},{7,39},{8,40},{9,... | collective-permute-start | bytes 368648 | tf_op jit(solution)/shard_map/ppermute | solution.py:38
  39.0 6.8 %collective-permute-start.4 = (bf16[16,3840]{1,0:T(8,128)(2,1)}, bf16[16,3840]{1,0:T(8,128)(2,1)S(1)}, u32[]{:S(2)}, u32[]{:S(2)}) collective-permute-start(bf16[16,3840]{1,0:T(8,128)(2,1)} %concatenate.42), channel_id=1, source_target_pairs={{0,480},{1,481},{2,482},{3,483},{4,484},{5,485},{6,486},{7,487},{8... | collective-permute-start | bytes 368648 | tf_op jit(solution)/shard_map/ppermute | solution.py:38
  42.5 30.9 %copy-start.8 = (bf16[16,3840]{1,0:T(8,128)(2,1)}, bf16[16,3840]{1,0:T(8,128)(2,1)S(1)}, u32[]{:S(2)}) copy-start(bf16[16,3840]{1,0:T(8,128)(2,1)S(1)} %collective-permute-done.3) | copy-start | bytes 368644
  42.5 78.8 %collective-permute-start.7 = (bf16[3584,256]{1,0:T(8,128)(2,1)}, bf16[3584,256]{1,0:T(8,128)(2,1)S(1)}, u32[]{:S(2)}, u32[]{:S(2)}) collective-permute-start(bf16[3584,256]{1,0:T(8,128)(2,1)} %pad_maximum_fusion), channel_id=1, source_target_pairs={{0,1},{1,0},{2,3},{3,2},{4,5},{5,4},{6,7},{7,6},{8,9},{9,8},{10,11... | collective-permute-start | bytes 5505032 | tf_op jit(solution)/shard_map/ppermute | solution.py:43
  45.8 100.1 %copy-start.9 = (bf16[16,3840]{1,0:T(8,128)(2,1)}, bf16[16,3840]{1,0:T(8,128)(2,1)S(1)}, u32[]{:S(2)}) copy-start(bf16[16,3840]{1,0:T(8,128)(2,1)S(1)} %collective-permute-done.4) | copy-start | bytes 368644
  68.7 49.4 %collective-permute-start.5 = (bf16[96,3584]{1,0:T(8,128)(2,1)}, bf16[96,3584]{1,0:T(8,128)(2,1)}, u32[]{:S(2)}, u32[]{:S(2)}) collective-permute-start(bf16[96,3584]{1,0:T(8,128)(2,1)} %concatenate.40), channel_id=1, source_target_pairs={{0,3},{1,2},{2,1},{3,0},{4,7},{5,6},{6,5},{7,4},{8,11},{9,10},{10,... | collective-permute-start | bytes 2064392 | tf_op jit(solution)/shard_map/ppermute | solution.py:43
  73.4 46.0 %copy-start.5 = (bf16[1,3584,128]{2,1,0:T(8,128)(2,1)S(1)}, bf16[1,3584,128]{2,1,0:T(8,128)(2,1)}, u32[]{:S(2)}) copy-start(bf16[1,3584,128]{2,1,0:T(8,128)(2,1)} %param.16) | copy-start | bytes 2752516
  73.4 46.0 %copy-start.7 = (bf16[1,3584,128]{2,1,0:T(8,128)(2,1)S(1)}, bf16[1,3584,128]{2,1,0:T(8,128)(2,1)}, u32[]{:S(2)}) copy-start(bf16[1,3584,128]{2,1,0:T(8,128)(2,1)} %param.15) | copy-start | bytes 2752516
  73.4 45.9 %collective-permute-start.6 = (bf16[96,3584]{1,0:T(8,128)(2,1)}, bf16[96,3584]{1,0:T(8,128)(2,1)S(1)}, u32[]{:S(2)}, u32[]{:S(2)}) collective-permute-start(bf16[96,3584]{1,0:T(8,128)(2,1)} %concatenate.40), channel_id=1, source_target_pairs={{0,7},{1,6},{2,5},{3,4},{4,3},{5,2},{6,1},{7,0},{8,15},{9,14},{10,... | collective-permute-start | bytes 2064392 | tf_op jit(solution)/shard_map/ppermute | solution.py:43
  76.6 43.3 %collective-permute-start.9 = (bf16[96,3584]{1,0:T(8,128)(2,1)}, bf16[96,3584]{1,0:T(8,128)(2,1)S(1)}, u32[]{:S(2)}, u32[]{:S(2)}) collective-permute-start(bf16[96,3584]{1,0:T(8,128)(2,1)} %concatenate.40), channel_id=1, source_target_pairs={{0,4},{1,5},{2,6},{3,7},{4,0},{5,1},{6,2},{7,3},{8,12},{9,13},{10,... | collective-permute-start | bytes 2064392 | tf_op jit(solution)/shard_map/ppermute | solution.py:43
  131.6 6.8 %collective-permute-start.8 = (bf16[192,256]{1,0:T(8,128)(2,1)S(1)}, bf16[192,256]{1,0:T(8,128)(2,1)S(1)}, u32[]{:S(2)}, u32[]{:S(2)}) collective-permute-start(bf16[192,256]{1,0:T(8,128)(2,1)S(1)} %pad_maximum_fusion.1), channel_id=1, source_target_pairs={{0,3},{1,2},{2,1},{3,0},{4,7},{5,6},{6,5},{7,4},{8,11},{9,10},{10,... | collective-permute-start | bytes 294920 | tf_op jit(solution)/shard_map/ppermute | solution.py:43
  140.4 10.3 %collective-permute-start.10 = (bf16[48,3584]{1,0:T(8,128)(2,1)}, bf16[48,3584]{1,0:T(8,128)(2,1)}, u32[]{:S(2)}, u32[]{:S(2)}) collective-permute-start(bf16[48,3584]{1,0:T(8,128)(2,1)} %get-tuple-element.32), channel_id=1, source_target_pairs={{0,4},{1,5},{2,6},{3,7},{4,0},{5,1},{6,2},{7,3},{8,12},{9,13},{10,... | collective-permute-start | bytes 1032200 | tf_op jit(solution)/shard_map/ppermute | solution.py:43
  144.0 14.1 %collective-permute-start.15 = (bf16[48,3584]{1,0:T(8,128)(2,1)}, bf16[48,3584]{1,0:T(8,128)(2,1)}, u32[]{:S(2)}, u32[]{:S(2)}) collective-permute-start(bf16[48,3584]{1,0:T(8,128)(2,1)} %get-tuple-element.31), channel_id=1, source_target_pairs={{0,4},{1,5},{2,6},{3,7},{4,0},{5,1},{6,2},{7,3},{8,12},{9,13},{10,... | collective-permute-start | bytes 1032200 | tf_op jit(solution)/shard_map/ppermute | solution.py:43
  159.5 28.1 %collective-permute-start.16 = (bf16[24,1792]{1,0:T(8,128)(2,1)S(1)}, bf16[24,1792]{1,0:T(8,128)(2,1)S(1)}, u32[]{:S(2)}, u32[]{:S(2)}) collective-permute-start(bf16[24,1792]{1,0:T(8,128)(2,1)S(1)} %squeeze.54), channel_id=1, source_target_pairs={{0,480},{1,481},{2,482},{3,483},{4,484},{5,485},{6,486},{7,487},{8... | collective-permute-start | bytes 258056 | tf_op jit(solution)/shard_map/ppermute | solution.py:38
  164.1 36.9 %copy-start.11 = (f32[32,96]{0,1:T(8,128)S(1)}, f32[32,96]{0,1:T(8,128)}, u32[]{:S(2)}) copy-start(f32[32,96]{0,1:T(8,128)} %mul.168) | copy-start | bytes 36868
  164.1 32.8 %collective-permute-start.17 = (bf16[24,1792]{1,0:T(8,128)(2,1)S(1)}, bf16[24,1792]{1,0:T(8,128)(2,1)S(1)}, u32[]{:S(2)}, u32[]{:S(2)}) collective-permute-start(bf16[24,1792]{1,0:T(8,128)(2,1)S(1)} %squeeze.55), channel_id=1, source_target_pairs={{0,504},{1,505},{2,506},{3,507},{4,508},{5,509},{6,510},{7,511},{8... | collective-permute-start | bytes 258056 | tf_op jit(solution)/shard_map/ppermute | solution.py:38
  177.2 21.7 %collective-permute-start.18 = (bf16[24,1792]{1,0:T(8,128)(2,1)S(1)}, bf16[24,1792]{1,0:T(8,128)(2,1)S(1)}, u32[]{:S(2)}, u32[]{:S(2)}) collective-permute-start(bf16[24,1792]{1,0:T(8,128)(2,1)S(1)} %squeeze.56), channel_id=1, source_target_pairs={{0,496},{1,497},{2,498},{3,499},{4,500},{5,501},{6,502},{7,503},{8... | collective-permute-start | bytes 258056 | tf_op jit(solution)/shard_map/ppermute | solution.py:38
  181.5 19.4 %collective-permute-start.19 = (bf16[24,1792]{1,0:T(8,128)(2,1)S(1)}, bf16[24,1792]{1,0:T(8,128)(2,1)S(1)}, u32[]{:S(2)}, u32[]{:S(2)}) collective-permute-start(bf16[24,1792]{1,0:T(8,128)(2,1)S(1)} %squeeze.57), channel_id=1, source_target_pairs={{0,488},{1,489},{2,490},{3,491},{4,492},{5,493},{6,494},{7,495},{8... | collective-permute-start | bytes 258056 | tf_op jit(solution)/shard_map/ppermute | solution.py:38
  183.6 17.7 %collective-permute-start.11 = (bf16[24,1792]{1,0:T(8,128)(2,1)S(1)}, bf16[24,1792]{1,0:T(8,128)(2,1)S(1)}, u32[]{:S(2)}, u32[]{:S(2)}) collective-permute-start(bf16[24,1792]{1,0:T(8,128)(2,1)S(1)} %squeeze.50), channel_id=1, source_target_pairs={{0,32},{1,33},{2,34},{3,35},{4,36},{5,37},{6,38},{7,39},{8,40},{9,... | collective-permute-start | bytes 258056 | tf_op jit(solution)/shard_map/ppermute | solution.py:38
  187.6 25.2 %slice-start.1 = ((bf16[16,3840]{1,0:T(8,128)(2,1)}), bf16[16,3584]{1,0:T(8,128)(2,1)S(1)}, s32[]{:S(2)}) async-start(bf16[16,3840]{1,0:T(8,128)(2,1)} %copy-done.9), calls=%async_computation.2 | async-start | bytes 229376 | tf_op jit(solution)/shard_map/slice | solution.py:119
  187.6 25.8 %slice-start = ((bf16[16,3840]{1,0:T(8,128)(2,1)}), bf16[16,3584]{1,0:T(8,128)(2,1)S(1)}, s32[]{:S(2)}) async-start(bf16[16,3840]{1,0:T(8,128)(2,1)} %copy-done.8), calls=%async_computation.1 | async-start | bytes 229376 | tf_op jit(solution)/shard_map/slice | solution.py:119
  187.7 13.6 %collective-permute-start.12 = (bf16[24,1792]{1,0:T(8,128)(2,1)S(1)}, bf16[24,1792]{1,0:T(8,128)(2,1)S(1)}, u32[]{:S(2)}, u32[]{:S(2)}) collective-permute-start(bf16[24,1792]{1,0:T(8,128)(2,1)S(1)} %squeeze.51), channel_id=1, source_target_pairs={{0,56},{1,57},{2,58},{3,59},{4,60},{5,61},{6,62},{7,63},{8,32},{9,... | collective-permute-start | bytes 258056 | tf_op jit(solution)/shard_map/ppermute | solution.py:38
  196.9 12.1 %collective-permute-start.13 = (bf16[24,1792]{1,0:T(8,128)(2,1)S(1)}, bf16[24,1792]{1,0:T(8,128)(2,1)S(1)}, u32[]{:S(2)}, u32[]{:S(2)}) collective-permute-start(bf16[24,1792]{1,0:T(8,128)(2,1)S(1)} %squeeze.52), channel_id=1, source_target_pairs={{0,48},{1,49},{2,50},{3,51},{4,52},{5,53},{6,54},{7,55},{8,56},{9,... | collective-permute-start | bytes 258056 | tf_op jit(solution)/shard_map/ppermute | solution.py:38
  198.8 13.6 %collective-permute-start.14 = (bf16[24,1792]{1,0:T(8,128)(2,1)S(1)}, bf16[24,1792]{1,0:T(8,128)(2,1)S(1)}, u32[]{:S(2)}, u32[]{:S(2)}) collective-permute-start(bf16[24,1792]{1,0:T(8,128)(2,1)S(1)} %squeeze.53), channel_id=1, source_target_pairs={{0,40},{1,41},{2,42},{3,43},{4,44},{5,45},{6,46},{7,47},{8,48},{9,... | collective-permute-start | bytes 258056 | tf_op jit(solution)/shard_map/ppermute | solution.py:38
  (5 other events, 84.3 us)
Sparse Core Ops, SparseCore 0:
  41.0 90.5 all-gather.2

commit v3 on v2

v3 whole, which is shorter than its diff:
```python
import jax
import jax.numpy as jnp
from jax import lax
from jax.sharding import PartitionSpec as P

CAP = 12
ALONG_X = 4

route_scale = 2.5


def index_of(z, x):
    return z * ALONG_X + x


def places():
    columns = lax.axis_size("expert") // ALONG_X
    return [(z, x) for z in range(columns) for x in range(ALONG_X)]


def across_groups(chunks):
    pairs = lax.axis_size("expert") // ALONG_X // 2
    members = [[index_of(2 * j + odd, x) for j in range(pairs)] for odd in range(2) for x in range(ALONG_X)]
    return lax.all_to_all(chunks, "expert", split_axis=0, concat_axis=0, tiled=True, axis_index_groups=members)


def across_sections(chunks):
    sections, devices = lax.axis_size("pipe"), lax.axis_size("expert")
    pairs = devices // ALONG_X // 2
    members = [
        [s * devices + index_of(2 * j + odd, x) for s in ((2 * q - 1) % sections, 2 * q) for j in range(pairs)]
        for q in range(sections // 2)
        for odd in range(2)
        for x in range(ALONG_X)
    ]
    return lax.all_to_all(
        chunks, ("pipe", "expert"), split_axis=0, concat_axis=0, tiled=True, axis_index_groups=members
    )


def neighbour(block):
    sections = lax.axis_size("pipe")
    return lax.ppermute(block, "pipe", [(s, (s + 1 if s % 2 else s - 1) % sections) for s in range(sections)])


def same_chip(block):
    return lax.ppermute(block, "pipe", [(s, s ^ 1) for s in range(lax.axis_size("pipe"))])


def facing(block, z_flip, x_flip):
    route = [(index_of(z, x), index_of(z ^ z_flip, x ^ x_flip)) for z, x in places()]
    return lax.ppermute(block, "expert", route)


def ring_gather(block):
    columns = lax.axis_size("expert") // ALONG_X
    rings = [[index_of(z, x) for x in range(ALONG_X)] for z in range(columns)]
    return lax.all_gather(block, "expert", axis=0, tiled=True, axis_index_groups=rings)


def prepare(x, routes, gain, router):
    xf = x.astype(jnp.float32)
    mean_sq = jnp.mean(xf * xf, axis=-1, keepdims=True)
    normed = (xf * lax.rsqrt(mean_sq + 1e-06) * gain).astype(jnp.bfloat16)
    logits = jnp.dot(normed, router, preferred_element_type=jnp.float32)
    affinity = jax.nn.sigmoid(logits)
    experts_n = router.shape[1]
    hits = routes[:, :, None] == jnp.arange(experts_n, dtype=jnp.int32)
    picked = jnp.sum(jnp.where(hits, affinity[:, None, :], 0.0), axis=2)
    weights = picked / jnp.sum(picked, axis=1, keepdims=True) * route_scale
    named = jnp.any(hits, axis=1)
    share = jnp.sum(jnp.where(hits, weights[:, :, None], 0.0), axis=1)
    count = named.astype(jnp.int32)
    before = jnp.cumsum(count, axis=0) - count
    slot = jnp.where(named, before, -1)
    chosen = slot[:, :, None] == jnp.arange(CAP, dtype=jnp.int32)
    combine = jnp.where(chosen, share[:, :, None], 0.0)
    return normed, chosen, combine


def in_terms(value):
    high = value.astype(jnp.bfloat16)
    rest = value - high.astype(jnp.float32)
    middle = rest.astype(jnp.bfloat16)
    low = (rest - middle.astype(jnp.float32)).astype(jnp.bfloat16)
    return [high, middle, low]


def on_device(act_down, act_up, routes_down, routes_up, norm_gain, router_w, w_gate, w_up, w_down):
    experts_n = router_w.shape[2]
    width = act_down.shape[2]
    rows_n = act_down.shape[1]
    slots = experts_n * CAP
    piece = width // 2
    gain = norm_gain[0]
    router = router_w[0]
    hidden_n = w_down.shape[1]
    place = lax.axis_index("expert")
    odd_section = lax.axis_index("pipe") % 2 == 1
    column = place % ALONG_X

    both_cols = jnp.concatenate([w_gate[0], w_up[0]], axis=1)
    next_cols = facing(both_cols, 0, 1)
    down_rows = ring_gather(w_down[0])
    both_cols, act_down, act_up = lax.optimization_barrier((both_cols, act_down, act_up))

    normed_d, chosen_d, combine_d = prepare(act_down[0], routes_down[0], gain, router)
    normed_u, chosen_u, combine_u = prepare(act_up[0], routes_up[0], gain, router)
    select = jnp.stack(
        [jnp.pad(chosen_d, ((0, rows_n), (0, 0), (0, 0))), jnp.pad(chosen_u, ((rows_n, 0), (0, 0), (0, 0)))],
        axis=2,
    ).reshape(2 * rows_n, 2 * slots)
    packed = lax.dot_general(
        select.astype(jnp.bfloat16),
        jnp.concatenate([normed_d, normed_u], axis=0),
        (((0,), (0,)), ((), ())),
        preferred_element_type=jnp.float32,
    ).astype(jnp.bfloat16)

    chunk = 2 * CAP
    mine = across_groups(packed)
    pair = facing(mine, 1, 0)
    across = facing(mine, 0, 3)
    corner = facing(mine, 1, 3)

    dot = lambda a, b: jnp.dot(a, b, preferred_element_type=jnp.float32)
    exact = lambda a, b: jnp.dot(a, b, precision=lax.Precision.HIGHEST, preferred_element_type=jnp.float32)
    act = lambda joined: (jax.nn.silu(joined[:, :hidden_n]) * joined[:, hidden_n:]).astype(jnp.bfloat16)
    terms_d, terms_u = in_terms(combine_d.reshape(rows_n, slots)), in_terms(combine_u.reshape(rows_n, slots))
    pad = jnp.zeros((rows_n, -(-3 * slots // 128) * 128 - 3 * slots), jnp.bfloat16)
    down_set = jnp.concatenate([act_down[0]] + terms_d + [pad], axis=1)
    up_set = jnp.concatenate([act_up[0]] + terms_u + [pad], axis=1)
    home_set = jnp.where(odd_section, up_set, down_set)
    cross_set, pair = lax.optimization_barrier((jnp.where(odd_section, down_set, up_set), pair))
    cross_set = neighbour(cross_set)
    corner, down_rows = lax.optimization_barrier((corner, down_rows))
    near_rows = jnp.concatenate([mine, pair], axis=0)
    far_rows = jnp.concatenate([across, corner], axis=0)
    sent = jnp.concatenate([act(dot(far_rows, both_cols)), act(dot(far_rows, next_cols))], axis=1)
    kept = [act(dot(near_rows, both_cols)), act(dot(near_rows, next_cols))]
    got = facing(sent, 0, 3)
    got, cross_set = lax.optimization_barrier((got, cross_set))
    blocks = kept + [got[:, hidden_n:], got[:, :hidden_n]]
    for bit in (1, 2):
        flip = (column & bit) > 0
        blocks = [jnp.where(flip, blocks[i ^ bit], blocks[i]) for i in range(ALONG_X)]
    hidden = jnp.concatenate(blocks, axis=1)

    total = dot(hidden, down_rows)
    half = 2 * slots
    summed = total[:half] + facing(total[half:].astype(jnp.bfloat16), 1, 0).astype(jnp.float32)

    number = jnp.arange(2 * slots).reshape(experts_n, 2, CAP).transpose(1, 0, 2)[::-1]
    slot_of = jnp.stack([number, number], axis=2)
    pick = (slot_of.reshape(-1)[:, None] == jnp.arange(2 * slots)).reshape(2, experts_n, 2, CAP, 2 * slots)
    side = jnp.arange(2).reshape(1, 1, 2, 1, 1)
    pick = [(pick & (side == h)).reshape(4 * slots, 2 * slots).astype(jnp.bfloat16) for h in (0, 1)]
    summed = summed.astype(jnp.bfloat16)
    halves = (dot(pick[0], summed[:, :piece]) + dot(pick[1], summed[:, piece:])).astype(jnp.bfloat16)
    back = across_sections(halves)
    from_odd, from_even = back[:2 * slots], back[2 * slots:]
    home_back = jnp.where(odd_section, from_odd, from_even)
    cross_back = jnp.where(odd_section, from_even, from_odd)

    def finish(given, back):
        share = given[:, width:width + 3 * slots].astype(jnp.float32).reshape(rows_n, 3, slots)
        share = (share[:, 0] + share[:, 1] + share[:, 2]).reshape(1, rows_n, experts_n, 1, CAP)
        mix = (share * jnp.eye(2, dtype=jnp.float32).reshape(2, 1, 1, 2, 1)).reshape(2 * rows_n, 2 * slots)
        mixed = exact(mix, back.astype(jnp.float32))
        mixed = jnp.concatenate([mixed[:rows_n], mixed[rows_n:]], axis=1)
        return (given[:, :width].astype(jnp.float32) + mixed).astype(jnp.bfloat16)[None]

    came = same_chip(finish(home_set, home_back))
    crossed = finish(cross_set, cross_back)
    return jnp.where(odd_section, came, crossed), jnp.where(odd_section, crossed, came)


def solution(mesh):
    placed = (
        P("pipe", "expert", None),
        P("pipe", "expert", None),
        P("pipe", "expert", None),
        P("pipe", "expert", None),
        P("pipe", None),
        P("pipe", None, None),
        P("pipe", None, "expert"),
        P("pipe", None, "expert"),
        P("pipe", "expert", None),
    )
    return jax.shard_map(
        on_device,
        mesh=mesh,
        in_specs=placed,
        out_specs=(P("pipe", "expert", None), P("pipe", "expert", None)),
        check_vma=False,
    )
```

time: 222 us -> 196 us (0.88)
  starting transfers between devices: 84 us -> 52.4 us
  waiting for transfers between devices: 83.6 us -> 103 us
  local copies, waits for them, and re-layouts: 23 us -> 5.93 us
  matrix products: 5.16 us -> 11.3 us
  other arithmetic: 10.4 us -> 7.52 us
    all_to_all x0 -> x2, waiting for transfers between devices: none -> 65.6 us  [the longest x1 35.3 us: across_sections(): lax.all_to_all(chunks, ('pipe', 'expert'), split_axis=0, concat_axis=0, t...]
    ppermute x13 -> x2, starting transfers between devices: 63.5 us -> 10.6 us  [the longest x1 8.69 us: neighbour(): lax.ppermute(block, 'pipe', [(s, (s + 1 if s % 2 else s - 1) % sections)...]
    all_to_all x0 -> x2, starting transfers between devices: none -> 23.4 us  [the longest x1 11.7 us: across_groups(): lax.all_to_all(chunks, 'expert', split_axis=0, concat_axis=0, tiled=True,...]
    ppermute x13 -> x2, waiting for transfers between devices: 20.5 us -> 0.93 us  [the longest x1 0.93 us: same_chip(): lax.ppermute(block, 'pipe', [(s, s ^ 1) for s in range(lax.axis_size('pip...]
    ppermute x7 -> x6, waiting for transfers between devices: 53.3 us -> 35.9 us  [facing(): return lax.ppermute(block, 'expert', route)]
    concatenate x5 -> x3, local copies, waits for them, and re-layouts: 13.2 us -> 1.33 us  [the longest x1 1.15 us: on_device(): far_rows = jnp.concatenate([across, corner], axis=0)]
    all_gather x1, waiting for transfers between devices: 9.77 us -> 0.02 us  [ring_gather(): lax.all_gather(block, 'expert', axis=0, tiled=True, axis_index_groups=rings)]
    dot_general x5 -> x7, matrix products: 3.73 us -> 9.02 us  [on_device(): dot = lambda a, b: jnp.dot(a, b, preferred_element_type=jnp.float32)]
  transfers between devices with their start and end apart: 21 -> 11, of which waited for: 9 -> 7; matrix products, arithmetic and copies ran while one was open for 12% -> 10% of each run, Pallas kernels for 0% -> 0%
where the time goes in v3:
time: 196 us; the launch traced here: 195 us
  waiting for transfers between devices  103 us (53%)
  starting transfers between devices  52.4 us (27%)
  between operations  14.6 us (7%)
  matrix products  11.3 us (6%)
  other arithmetic  7.52 us (4%)
  local copies, waits for them, and re-layouts  5.93 us (3%)
    ppermute x6, waiting for transfers between devices, facing(): return lax.ppermute(block, 'expert', route)  35.9 us
    all_to_all x1, waiting for transfers between devices, across_sections(): lax.all_to_all(chunks, ('pipe', 'expert'), split_axis=0, concat_axis=0, t...  35.3 us
    all_to_all x1, waiting for transfers between devices, across_groups(): lax.all_to_all(chunks, 'expert', split_axis=0, concat_axis=0, tiled=True,...  30.2 us
    ppermute x6, starting transfers between devices, facing(): return lax.ppermute(block, 'expert', route)  18.4 us
    all_to_all x1, starting transfers between devices, across_groups(): lax.all_to_all(chunks, 'expert', split_axis=0, concat_axis=0, tiled=True,...  11.7 us
    all_to_all x1, starting transfers between devices, across_sections(): lax.all_to_all(chunks, ('pipe', 'expert'), split_axis=0, concat_axis=0, t...  11.7 us
    dot_general x7, matrix products, on_device(): dot = lambda a, b: jnp.dot(a, b, preferred_element_type=jnp.float32)  9.02 us
    ppermute x1, starting transfers between devices, neighbour(): lax.ppermute(block, 'pipe', [(s, (s + 1 if s % 2 else s - 1) % sections)...  8.69 us
  transfers between devices with their start and end apart: 11, of which 7 were waited for; matrix products, arithmetic and copies ran while one was open for 10% of the time, Pallas kernels for 0%

profile of v3, /device:TPU:1, one launch (start us, length us, event | category | flops | bytes accessed | tf_op | source)
XLA Modules:
  0.0 194.8 jit_solution(322155513786090716)
XLA Ops:
  7.9 0.7 fusion.61
  8.9 0.7 fusion.60
  9.9 1.7 pad_maximum_fusion
  12.2 1.2 convolution_convert_fusion
  13.4 11.7 %all-to-all-start = ((bf16[4,24,3584]{2,1,0:T(8,128)(2,1)}), bf16[4,24,3584]{2,1,0:T(8,128)(2,1)}, u32[]{:S(2)}, u32[]{:S(2)}) async-start(bf16[4,24,3584]{2,1,0:T(8,128)(2,1)} %bitcast.12), calls=%async_computation | async-start | bytes 1376256 | tf_op jit(solution)/shard_map/all_to_all | solution.py:24
  25.1 3.1 %collective-permute-start.2 = (bf16[3584,256]{1,0:T(8,128)(2,1)S(1)}, bf16[3584,256]{1,0:T(8,128)(2,1)}, u32[]{:S(2)}, u32[]{:S(2)}) collective-permute-start(bf16[3584,256]{1,0:T(8,128)(2,1)S(1)} %pad_maximum_fusion), channel_id=1, source_target_pairs={{0,1},{1,0},{2,3},{3,2},{4,5},{5,4},{6,7},{7,6},{8,9},{9,8},{10,11... | collective-permute-start | bytes 5505032 | tf_op jit(solution)/shard_map/ppermute | solution.py:52
  29.8 30.2 %all-to-all-done = bf16[4,24,3584]{2,1,0:T(8,128)(2,1)} async-done(((bf16[4,24,3584]{2,1,0:T(8,128)(2,1)}), bf16[4,24,3584]{2,1,0:T(8,128)(2,1)}, u32[]{:S(2)}, u32[]{:S(2)}) %all-to-all-start) | async-done | bytes 688160 | tf_op jit(solution)/shard_map/all_to_all | solution.py:24
  60.1 4.4 %collective-permute-start = (bf16[96,3584]{1,0:T(8,128)(2,1)}, bf16[96,3584]{1,0:T(8,128)(2,1)}, u32[]{:S(2)}, u32[]{:S(2)}) collective-permute-start(bf16[96,3584]{1,0:T(8,128)(2,1)} %bitcast.13), channel_id=1, source_target_pairs={{0,3},{1,2},{2,1},{3,0},{4,7},{5,6},{6,5},{7,4},{8,11},{9,10},{10,... | collective-permute-start | bytes 2064392 | tf_op jit(solution)/shard_map/ppermute | solution.py:52
  64.4 1.9 collective-permute-start.4
  66.4 0.8 broadcast_select_fusion.2
  67.1 3.3 %collective-permute-start.1 = (bf16[96,3584]{1,0:T(8,128)(2,1)}, bf16[96,3584]{1,0:T(8,128)(2,1)}, u32[]{:S(2)}, u32[]{:S(2)}) collective-permute-start(bf16[96,3584]{1,0:T(8,128)(2,1)} %bitcast.13), channel_id=1, source_target_pairs={{0,7},{1,6},{2,5},{3,4},{4,3},{5,2},{6,1},{7,0},{8,15},{9,14},{10,... | collective-permute-start | bytes 2064392 | tf_op jit(solution)/shard_map/ppermute | solution.py:52
  70.4 11.0 %collective-permute-done.4 = bf16[96,3584]{1,0:T(8,128)(2,1)S(1)} collective-permute-done((bf16[96,3584]{1,0:T(8,128)(2,1)}, bf16[96,3584]{1,0:T(8,128)(2,1)S(1)}, u32[]{:S(2)}, u32[]{:S(2)}) %collective-permute-start.4) | collective-permute-done | bytes 688160 | tf_op jit(solution)/shard_map/ppermute | solution.py:52
  81.5 8.7 %collective-permute-start.5 = (bf16[16,3840]{1,0:T(8,128)(2,1)}, bf16[16,3840]{1,0:T(8,128)(2,1)}, u32[]{:S(2)}, u32[]{:S(2)}) collective-permute-start(bf16[16,3840]{1,0:T(8,128)(2,1)} %get-tuple-element.15), channel_id=1, source_target_pairs={{0,480},{32,64},{64,32},{96,128},{128,96},{160,192},{192,160},{224... | collective-permute-start | bytes 368648 | tf_op jit(solution)/shard_map/ppermute | solution.py:43
  90.1 1.6 fusion.8
  91.8 10.2 %collective-permute-done = bf16[96,3584]{1,0:T(8,128)(2,1)} collective-permute-done((bf16[96,3584]{1,0:T(8,128)(2,1)}, bf16[96,3584]{1,0:T(8,128)(2,1)}, u32[]{:S(2)}, u32[]{:S(2)}) %collective-permute-start) | collective-permute-done | bytes 688160 | tf_op jit(solution)/shard_map/ppermute | solution.py:52
  102.0 1.1 constant_dynamic-update-slice_fusion.1
  103.2 1.1 constant_dynamic-update-slice_fusion
  104.9 2.1 %fusion.71 = f32[192,256]{1,0:T(8,128)S(1)} fusion(bf16[192,3584]{1,0:T(8,128)(2,1)S(1)} %constant_dynamic-update-slice_fusion, bf16[3584,256]{1,0:T(8,128)(2,1)} %collective-permute-done.2), kind=kOutput, calls=%fused_computation.142 | convolution fusion | flops 352321536 | bytes 3407872 | tf_op jit(solution)/shard_map/dot_general | solution.py:126
  107.1 2.2 %collective-permute-start.3 = (bf16[192,256]{1,0:T(8,128)(2,1)S(1)}, bf16[192,256]{1,0:T(8,128)(2,1)S(1)}, u32[]{:S(2)}, u32[]{:S(2)}) collective-permute-start(bf16[192,256]{1,0:T(8,128)(2,1)S(1)} %pad_maximum_fusion.4), channel_id=1, source_target_pairs={{0,3},{1,2},{2,1},{3,0},{4,7},{5,6},{6,5},{7,4},{8,11},{9,10},{10,... | collective-permute-start | bytes 294920 | tf_op jit(solution)/shard_map/ppermute | solution.py:52
  109.3 2.2 %fusion.9 = f32[192,256]{1,0:T(8,128)S(1)} fusion(bf16[3584,256]{1,0:T(8,128)(2,1)} %collective-permute-done.2, bf16[96,3584]{1,0:T(8,128)(2,1)S(1)} %copy-done.9, bf16[96,3584]{1,0:T(8,128)(2,1)} %bitcast.13), kind=kOutput, calls=%fused_computation.17 | convolution fusion | flops 355074048 | bytes 3407872 | tf_op jit(solution)/shard_map/dot_general | solution.py:126
  111.6 2.4 %collective-permute-done.3 = bf16[192,256]{1,0:T(8,128)(2,1)S(1)} collective-permute-done((bf16[192,256]{1,0:T(8,128)(2,1)S(1)}, bf16[192,256]{1,0:T(8,128)(2,1)S(1)}, u32[]{:S(2)}, u32[]{:S(2)}) %collective-permute-start.3) | collective-permute-done | bytes 98336 | tf_op jit(solution)/shard_map/ppermute | solution.py:52
  114.0 0.9 fusion.24
  114.9 0.9 slice.219
  115.9 3.6 %collective-permute-start.6 = (bf16[96,3584]{1,0:T(8,128)(2,1)}, bf16[96,3584]{1,0:T(8,128)(2,1)S(1)}, u32[]{:S(2)}, u32[]{:S(2)}) collective-permute-start(bf16[96,3584]{1,0:T(8,128)(2,1)} %slice.219), channel_id=1, source_target_pairs={{0,4},{1,5},{2,6},{3,7},{4,0},{5,1},{6,2},{7,3},{8,12},{9,13},{10,... | collective-permute-start | bytes 2064392 | tf_op jit(solution)/shard_map/ppermute | solution.py:52
  120.0 12.2 %collective-permute-done.6 = bf16[96,3584]{1,0:T(8,128)(2,1)S(1)} collective-permute-done((bf16[96,3584]{1,0:T(8,128)(2,1)}, bf16[96,3584]{1,0:T(8,128)(2,1)S(1)}, u32[]{:S(2)}, u32[]{:S(2)}) %collective-permute-start.6) | collective-permute-done | bytes 688160 | tf_op jit(solution)/shard_map/ppermute | solution.py:52
  132.7 1.2 fusion
  134.0 11.7 %all-to-all-start.1 = ((bf16[8,24,1792]{2,1,0:T(8,128)(2,1)}), bf16[8,24,1792]{2,1,0:T(8,128)(2,1)S(1)}, u32[]{:S(2)}, u32[]{:S(2)}) async-start(bf16[8,24,1792]{2,1,0:T(8,128)(2,1)} %bitcast.15), calls=%async_computation.1 | async-start | bytes 1376256 | tf_op jit(solution)/shard_map/all_to_all | solution.py:36
  145.7 0.7 slice_convert_fusion.2
  147.4 35.3 %all-to-all-done.1 = bf16[8,24,1792]{2,1,0:T(8,128)(2,1)S(1)} async-done(((bf16[8,24,1792]{2,1,0:T(8,128)(2,1)}), bf16[8,24,1792]{2,1,0:T(8,128)(2,1)S(1)}, u32[]{:S(2)}, u32[]{:S(2)}) %all-to-all-start.1) | async-done | bytes 688160 | tf_op jit(solution)/shard_map/all_to_all | solution.py:36
  183.1 1.9 collective-permute-start.7
  185.4 0.9 collective-permute-done.7
  186.3 1.6 broadcast_select_fusion.4
  (113 shorter events, 6.8 us)
Async XLA Ops:
  7.2 21.1 %copy-start = (bf16[1,3584,4]{1,2,0:T(4,128)(2,1)S(1)}, bf16[1,3584,4]{1,2,0:T(4,128)(2,1)}, u32[]{:S(2)}) copy-start(bf16[1,3584,4]{1,2,0:T(4,128)(2,1)} %param.14) | copy-start | bytes 86020
  7.2 96.0 %all-gather.3.cloned.1.call-start = ((), (), s32[]{:S(2)}) async-start(), calls=%async_computation.2 | async-start | bytes 4587520 | tf_op jit(solution)/shard_map/all_gather | solution.py:58
  9.9 1.8 copy-start.5
  9.9 1.8 copy-start.2
  9.9 2.0 %copy-start.3 = (bf16[1,16,3584]{2,1,0:T(8,128)(2,1)S(1)}, bf16[1,16,3584]{2,1,0:T(8,128)(2,1)}, u32[]{:S(2)}) copy-start(bf16[1,16,3584]{2,1,0:T(8,128)(2,1)} %param.10) | copy-start | bytes 344068
  11.6 16.8 %copy-start.6 = (s32[1,16,2]{1,2,0:T(2,128)S(1)}, s32[1,16,2]{1,2,0:T(2,128)}, u32[]{:S(2)}) copy-start(s32[1,16,2]{1,2,0:T(2,128)} %param.11) | copy-start | bytes 388
  11.9 17.3 %copy-start.7 = (s32[1,16,2]{1,2,0:T(2,128)S(1)}, s32[1,16,2]{1,2,0:T(2,128)}, u32[]{:S(2)}) copy-start(s32[1,16,2]{1,2,0:T(2,128)} %param.12) | copy-start | bytes 388
  13.4 46.7 %all-to-all-start = ((bf16[4,24,3584]{2,1,0:T(8,128)(2,1)}), bf16[4,24,3584]{2,1,0:T(8,128)(2,1)}, u32[]{:S(2)}, u32[]{:S(2)}) async-start(bf16[4,24,3584]{2,1,0:T(8,128)(2,1)} %bitcast.12), calls=%async_computation | async-start | bytes 1376256 | tf_op jit(solution)/shard_map/all_to_all | solution.py:24
  25.1 79.8 %collective-permute-start.2 = (bf16[3584,256]{1,0:T(8,128)(2,1)S(1)}, bf16[3584,256]{1,0:T(8,128)(2,1)}, u32[]{:S(2)}, u32[]{:S(2)}) collective-permute-start(bf16[3584,256]{1,0:T(8,128)(2,1)S(1)} %pad_maximum_fusion), channel_id=1, source_target_pairs={{0,1},{1,0},{2,3},{3,2},{4,5},{5,4},{6,7},{7,6},{8,9},{9,8},{10,11... | collective-permute-start | bytes 5505032 | tf_op jit(solution)/shard_map/ppermute | solution.py:52
  60.1 41.9 %collective-permute-start = (bf16[96,3584]{1,0:T(8,128)(2,1)}, bf16[96,3584]{1,0:T(8,128)(2,1)}, u32[]{:S(2)}, u32[]{:S(2)}) collective-permute-start(bf16[96,3584]{1,0:T(8,128)(2,1)} %bitcast.13), channel_id=1, source_target_pairs={{0,3},{1,2},{2,1},{3,0},{4,7},{5,6},{6,5},{7,4},{8,11},{9,10},{10,... | collective-permute-start | bytes 2064392 | tf_op jit(solution)/shard_map/ppermute | solution.py:52
  64.4 17.0 %collective-permute-start.4 = (bf16[96,3584]{1,0:T(8,128)(2,1)}, bf16[96,3584]{1,0:T(8,128)(2,1)S(1)}, u32[]{:S(2)}, u32[]{:S(2)}) collective-permute-start(bf16[96,3584]{1,0:T(8,128)(2,1)} %bitcast.13), channel_id=1, source_target_pairs={{0,4},{1,5},{2,6},{3,7},{4,0},{5,1},{6,2},{7,3},{8,12},{9,13},{10,... | collective-permute-start | bytes 2064392 | tf_op jit(solution)/shard_map/ppermute | solution.py:52
  67.1 36.0 %collective-permute-start.1 = (bf16[96,3584]{1,0:T(8,128)(2,1)}, bf16[96,3584]{1,0:T(8,128)(2,1)}, u32[]{:S(2)}, u32[]{:S(2)}) collective-permute-start(bf16[96,3584]{1,0:T(8,128)(2,1)} %bitcast.13), channel_id=1, source_target_pairs={{0,7},{1,6},{2,5},{3,4},{4,3},{5,2},{6,1},{7,0},{8,15},{9,14},{10,... | collective-permute-start | bytes 2064392 | tf_op jit(solution)/shard_map/ppermute | solution.py:52
  81.5 10.3 %copy-start.8 = (bf16[96,3584]{1,0:T(8,128)(2,1)}, bf16[96,3584]{1,0:T(8,128)(2,1)S(1)}, u32[]{:S(2)}) copy-start(bf16[96,3584]{1,0:T(8,128)(2,1)S(1)} %collective-permute-done.4) | copy-start | bytes 2064388
  81.5 30.1 %collective-permute-start.5 = (bf16[16,3840]{1,0:T(8,128)(2,1)}, bf16[16,3840]{1,0:T(8,128)(2,1)}, u32[]{:S(2)}, u32[]{:S(2)}) collective-permute-start(bf16[16,3840]{1,0:T(8,128)(2,1)} %get-tuple-element.15), channel_id=1, source_target_pairs={{0,480},{32,64},{64,32},{96,128},{128,96},{160,192},{192,160},{224... | collective-permute-start | bytes 368648 | tf_op jit(solution)/shard_map/ppermute | solution.py:43
  104.8 4.4 %copy-start.9 = (bf16[96,3584]{1,0:T(8,128)(2,1)S(1)}, bf16[96,3584]{1,0:T(8,128)(2,1)}, u32[]{:S(2)}) copy-start(bf16[96,3584]{1,0:T(8,128)(2,1)} %copy-done.8) | copy-start | bytes 2064388
  107.1 7.0 %copy-start.1 = (bf16[1,512,3584]{2,1,0:T(8,128)(2,1)S(1)}, bf16[1,512,3584]{2,1,0:T(8,128)(2,1)}, u32[]{:S(2)}) copy-start(bf16[1,512,3584]{2,1,0:T(8,128)(2,1)} %all-gather.3.cloned.1.call-done) | copy-start | bytes 11010052
  107.1 6.8 %collective-permute-start.3 = (bf16[192,256]{1,0:T(8,128)(2,1)S(1)}, bf16[192,256]{1,0:T(8,128)(2,1)S(1)}, u32[]{:S(2)}, u32[]{:S(2)}) collective-permute-start(bf16[192,256]{1,0:T(8,128)(2,1)S(1)} %pad_maximum_fusion.4), channel_id=1, source_target_pairs={{0,3},{1,2},{2,1},{3,0},{4,7},{5,6},{6,5},{7,4},{8,11},{9,10},{10,... | collective-permute-start | bytes 294920 | tf_op jit(solution)/shard_map/ppermute | solution.py:52
  115.9 16.3 %collective-permute-start.6 = (bf16[96,3584]{1,0:T(8,128)(2,1)}, bf16[96,3584]{1,0:T(8,128)(2,1)S(1)}, u32[]{:S(2)}, u32[]{:S(2)}) collective-permute-start(bf16[96,3584]{1,0:T(8,128)(2,1)} %slice.219), channel_id=1, source_target_pairs={{0,4},{1,5},{2,6},{3,7},{4,0},{5,1},{6,2},{7,3},{8,12},{9,13},{10,... | collective-permute-start | bytes 2064392 | tf_op jit(solution)/shard_map/ppermute | solution.py:52
  132.7 12.9 %copy-start.4 = (bf16[16,3840]{1,0:T(8,128)(2,1)S(1)}, bf16[16,3840]{1,0:T(8,128)(2,1)}, u32[]{:S(2)}) copy-start(bf16[16,3840]{1,0:T(8,128)(2,1)} %get-tuple-element.36) | copy-start | bytes 368644
  134.0 48.7 %all-to-all-start.1 = ((bf16[8,24,1792]{2,1,0:T(8,128)(2,1)}), bf16[8,24,1792]{2,1,0:T(8,128)(2,1)S(1)}, u32[]{:S(2)}, u32[]{:S(2)}) async-start(bf16[8,24,1792]{2,1,0:T(8,128)(2,1)} %bitcast.15), calls=%async_computation.1 | async-start | bytes 1376256 | tf_op jit(solution)/shard_map/all_to_all | solution.py:36
  183.1 3.2 %collective-permute-start.7 = (bf16[1,16,3584]{2,1,0:T(8,128)(2,1)S(1)}, bf16[1,16,3584]{2,1,0:T(8,128)(2,1)S(1)}, u32[]{:S(2)}, u32[]{:S(2)}) collective-permute-start(bf16[1,16,3584]{2,1,0:T(8,128)(2,1)S(1)} %fusion.37), channel_id=1, source_target_pairs={{0,32},{32,0},{64,96},{96,64},{128,160},{160,128},{192,224},{224,1... | collective-permute-start | bytes 344072 | tf_op jit(solution)/shard_map/ppermute | solution.py:47
Sparse Core Ops, SparseCore 0:
  10.1 86.0 all-gather.2

commit v4 on v3

--- a/solution.py
+++ b/solution.py
@@ -43,13 +43,24 @@
     return lax.ppermute(block, "pipe", [(s, (s + 1 if s % 2 else s - 1) % sections) for s in range(sections)])
 
 
-def same_chip(block):
-    return lax.ppermute(block, "pipe", [(s, s ^ 1) for s in range(lax.axis_size("pipe"))])
-
-
-def facing(block, z_flip, x_flip):
-    route = [(index_of(z, x), index_of(z ^ z_flip, x ^ x_flip)) for z, x in places()]
-    return lax.ppermute(block, "expert", route)
+def facing(block, z_flip, even, odd):
+    devices = lax.axis_size("expert")
+    route = [
+        (s * devices + index_of(z, x), s * devices + index_of(z ^ z_flip, x ^ (odd if s % 2 else even)))
+        for s in range(lax.axis_size("pipe"))
+        for z, x in places()
+    ]
+    return lax.ppermute(block, ("pipe", "expert"), route)
+
+
+def other_core(block, z_flip):
+    devices = lax.axis_size("expert")
+    route = [
+        (s * devices + index_of(z, x), (s ^ 1) * devices + index_of(z ^ z_flip, x))
+        for s in range(lax.axis_size("pipe"))
+        for z, x in places()
+    ]
+    return lax.ppermute(block, ("pipe", "expert"), route)
 
 
 def ring_gather(block):
@@ -100,7 +111,7 @@
     column = place % ALONG_X
 
     both_cols = jnp.concatenate([w_gate[0], w_up[0]], axis=1)
-    next_cols = facing(both_cols, 0, 1)
+    next_cols = facing(both_cols, 0, 1, 3)
     down_rows = ring_gather(w_down[0])
     both_cols, act_down, act_up = lax.optimization_barrier((both_cols, act_down, act_up))
 
@@ -118,49 +129,57 @@
     ).astype(jnp.bfloat16)
 
     chunk = 2 * CAP
-    mine = across_groups(packed)
-    pair = facing(mine, 1, 0)
-    across = facing(mine, 0, 3)
-    corner = facing(mine, 1, 3)
-
-    dot = lambda a, b: jnp.dot(a, b, preferred_element_type=jnp.float32)
-    exact = lambda a, b: jnp.dot(a, b, precision=lax.Precision.HIGHEST, preferred_element_type=jnp.float32)
-    act = lambda joined: (jax.nn.silu(joined[:, :hidden_n]) * joined[:, hidden_n:]).astype(jnp.bfloat16)
     terms_d, terms_u = in_terms(combine_d.reshape(rows_n, slots)), in_terms(combine_u.reshape(rows_n, slots))
     pad = jnp.zeros((rows_n, -(-3 * slots // 128) * 128 - 3 * slots), jnp.bfloat16)
     down_set = jnp.concatenate([act_down[0]] + terms_d + [pad], axis=1)
     up_set = jnp.concatenate([act_up[0]] + terms_u + [pad], axis=1)
-    home_set = jnp.where(odd_section, up_set, down_set)
-    cross_set, pair = lax.optimization_barrier((jnp.where(odd_section, down_set, up_set), pair))
+    home_set, cross_set = jnp.where(odd_section, up_set, down_set), jnp.where(odd_section, down_set, up_set)
+    home_set = other_core(home_set, 0)
+    mine = across_groups(packed)
+    mine, home_set = lax.optimization_barrier((mine, home_set))
+    pair = facing(mine, 1, 0, 0)
+    across = facing(mine, 0, 3, 1)
+    corner = facing(mine, 1, 3, 1)
+
+    dot = lambda a, b: jnp.dot(a, b, preferred_element_type=jnp.float32)
+    exact = lambda a, b: jnp.dot(a, b, precision=lax.Precision.HIGHEST, preferred_element_type=jnp.float32)
+    act = lambda joined: (jax.nn.silu(joined[:, :hidden_n]) * joined[:, hidden_n:]).astype(jnp.bfloat16)
+    cross_set, pair = lax.optimization_barrier((cross_set, pair))
     cross_set = neighbour(cross_set)
     corner, down_rows = lax.optimization_barrier((corner, down_rows))
     near_rows = jnp.concatenate([mine, pair], axis=0)
     far_rows = jnp.concatenate([across, corner], axis=0)
     sent = jnp.concatenate([act(dot(far_rows, both_cols)), act(dot(far_rows, next_cols))], axis=1)
     kept = [act(dot(near_rows, both_cols)), act(dot(near_rows, next_cols))]
-    got = facing(sent, 0, 3)
+    got = facing(sent, 0, 3, 1)
     got, cross_set = lax.optimization_barrier((got, cross_set))
-    blocks = kept + [got[:, hidden_n:], got[:, :hidden_n]]
+    first, second = got[:, :hidden_n], got[:, hidden_n:]
+    one, three = jnp.where(odd_section, first, kept[1]), jnp.where(odd_section, kept[1], first)
+    blocks = [kept[0], one, second, three]
     for bit in (1, 2):
         flip = (column & bit) > 0
         blocks = [jnp.where(flip, blocks[i ^ bit], blocks[i]) for i in range(ALONG_X)]
     hidden = jnp.concatenate(blocks, axis=1)
 
-    total = dot(hidden, down_rows)
-    half = 2 * slots
-    summed = total[:half] + facing(total[half:].astype(jnp.bfloat16), 1, 0).astype(jnp.float32)
-
-    number = jnp.arange(2 * slots).reshape(experts_n, 2, CAP).transpose(1, 0, 2)[::-1]
-    slot_of = jnp.stack([number, number], axis=2)
-    pick = (slot_of.reshape(-1)[:, None] == jnp.arange(2 * slots)).reshape(2, experts_n, 2, CAP, 2 * slots)
+    batch = jnp.arange(2).reshape(1, 2, 1, 1) ^ odd_section.astype(jnp.int32)
+    row_of = lambda owner: (owner * experts_n + jnp.arange(experts_n).reshape(1, 1, -1, 1)) * chunk
+    row_of = row_of(jnp.arange(2).reshape(2, 1, 1, 1)[::-1]) + batch * CAP + jnp.arange(CAP)
+    order = (row_of.reshape(-1)[:, None] == jnp.arange(4 * slots)).astype(jnp.bfloat16)
+    hidden = dot(order, hidden).astype(jnp.bfloat16)
+    away = dot(hidden[:2 * slots], down_rows).astype(jnp.bfloat16)
+    home, cross = other_core(away[:slots], 1), facing(away[slots:], 1, 0, 0)
+    stays = dot(hidden[2 * slots:], down_rows)
+    home = home.astype(jnp.float32) + other_core(stays[:slots].astype(jnp.bfloat16), 0).astype(jnp.float32)
+    cross = cross.astype(jnp.float32) + stays[slots:]
+    summed = jnp.concatenate([home, cross], axis=0).astype(jnp.bfloat16)
+
+    source = jnp.arange(2).reshape(2, 1, 1, 1, 1) ^ 1 ^ odd_section.astype(jnp.int32)
+    slot_of = source * slots + jnp.arange(experts_n).reshape(1, -1, 1, 1, 1) * CAP
+    slot_of = slot_of + jnp.arange(CAP).reshape(1, 1, 1, CAP, 1) == jnp.arange(2 * slots)
     side = jnp.arange(2).reshape(1, 1, 2, 1, 1)
-    pick = [(pick & (side == h)).reshape(4 * slots, 2 * slots).astype(jnp.bfloat16) for h in (0, 1)]
-    summed = summed.astype(jnp.bfloat16)
+    pick = [(slot_of & (side == h)).reshape(4 * slots, 2 * slots).astype(jnp.bfloat16) for h in (0, 1)]
     halves = (dot(pick[0], summed[:, :piece]) + dot(pick[1], summed[:, piece:])).astype(jnp.bfloat16)
     back = across_sections(halves)
-    from_odd, from_even = back[:2 * slots], back[2 * slots:]
-    home_back = jnp.where(odd_section, from_odd, from_even)
-    cross_back = jnp.where(odd_section, from_even, from_odd)
 
     def finish(given, back):
         share = given[:, width:width + 3 * slots].astype(jnp.float32).reshape(rows_n, 3, slots)
@@ -170,9 +189,8 @@
         mixed = jnp.concatenate([mixed[:rows_n], mixed[rows_n:]], axis=1)
         return (given[:, :width].astype(jnp.float32) + mixed).astype(jnp.bfloat16)[None]
 
-    came = same_chip(finish(home_set, home_back))
-    crossed = finish(cross_set, cross_back)
-    return jnp.where(odd_section, came, crossed), jnp.where(odd_section, crossed, came)
+    down_set, up_set = jnp.where(odd_section, home_set, cross_set), jnp.where(odd_section, cross_set, home_set)
+    return finish(down_set, back[:2 * slots]), finish(up_set, back[2 * slots:])
 
 
 def solution(mesh):

time: 196 us -> 189 us (0.964)
  the two profiles are of different devices: /device:TPU:1 before, /device:TPU:17 now
where the time goes in v4:
time: 189 us; the launch traced here: 188 us
  waiting for transfers between devices  89.3 us (47%)
  starting transfers between devices  56.9 us (30%)
  between operations  14.7 us (8%)
  matrix products  12.4 us (7%)
  local copies, waits for them, and re-layouts  8.85 us (5%)
  other arithmetic  6.33 us (3%)
    all_to_all x1, waiting for transfers between devices, across_sections(): lax.all_to_all(chunks, ('pipe', 'expert'), split_axis=0, concat_axis=0, t...  35.4 us
    all_to_all x1, waiting for transfers between devices, across_groups(): lax.all_to_all(chunks, 'expert', split_axis=0, concat_axis=0, tiled=True,...  30.4 us
    ppermute x6, starting transfers between devices, facing(): return lax.ppermute(block, ('pipe', 'expert'), route)  18.9 us
    ppermute x6, waiting for transfers between devices, facing(): return lax.ppermute(block, ('pipe', 'expert'), route)  14.1 us
    all_to_all x1, starting transfers between devices, across_groups(): lax.all_to_all(chunks, 'expert', split_axis=0, concat_axis=0, tiled=True,...  10.9 us
    ppermute x3, starting transfers between devices, other_core(): return lax.ppermute(block, ('pipe', 'expert'), route)  10.8 us
    all_to_all x1, starting transfers between devices, across_sections(): lax.all_to_all(chunks, ('pipe', 'expert'), split_axis=0, concat_axis=0, t...  10.6 us
    dot_general x9, matrix products, on_device(): dot = lambda a, b: jnp.dot(a, b, preferred_element_type=jnp.float32)  10.1 us
  transfers between devices with their start and end apart: 13, of which 6 were waited for; matrix products, arithmetic and copies ran while one was open for 12% of the time, Pallas kernels for 0%

profile of v4, /device:TPU:17, one launch (start us, length us, event | category | flops | bytes accessed | tf_op | source)
XLA Modules:
  0.0 188.4 jit_solution(8161515582836306400)
XLA Ops:
  7.2 0.7 all-gather.3.cloned.1.call-update
  8.4 1.6 pad_maximum_fusion
  10.0 4.4 %collective-permute-start.3 = (bf16[3584,256]{1,0:T(8,128)(2,1)S(1)}, bf16[3584,256]{1,0:T(8,128)(2,1)}, u32[]{:S(2)}, u32[]{:S(2)}) collective-permute-start(bf16[3584,256]{1,0:T(8,128)(2,1)S(1)} %pad_maximum_fusion), channel_id=1, source_target_pairs={{0,1},{1,0},{2,3},{3,2},{4,5},{5,4},{6,7},{7,6},{8,9},{9,8},{10,11... | collective-permute-start | bytes 5505032 | tf_op jit(solution)/shard_map/ppermute | solution.py:53
  15.6 1.2 convolution_convert_fusion.1
  16.8 10.9 %all-to-all-start = ((bf16[4,24,3584]{2,1,0:T(8,128)(2,1)}), bf16[4,24,3584]{2,1,0:T(8,128)(2,1)}, u32[]{:S(2)}, u32[]{:S(2)}) async-start(bf16[4,24,3584]{2,1,0:T(8,128)(2,1)} %bitcast.8), calls=%async_computation | async-start | bytes 1376256 | tf_op jit(solution)/shard_map/all_to_all | solution.py:24
  29.4 0.7 broadcast_select_fusion.2
  30.1 1.9 %collective-permute-start = (bf16[16,3840]{1,0:T(8,128)(2,1)S(1)}, bf16[16,3840]{1,0:T(8,128)(2,1)S(1)}, u32[]{:S(2)}, u32[]{:S(2)}) collective-permute-start(bf16[16,3840]{1,0:T(8,128)(2,1)S(1)} %get-tuple-element.46), channel_id=1, source_target_pairs={{0,32},{1,33},{2,34},{3,35},{4,36},{5,37},{6,38},{7,39},{8,40},{9,... | collective-permute-start | bytes 368648 | tf_op jit(solution)/shard_map/ppermute | solution.py:63
  33.3 30.4 %all-to-all-done = bf16[4,24,3584]{2,1,0:T(8,128)(2,1)} async-done(((bf16[4,24,3584]{2,1,0:T(8,128)(2,1)}), bf16[4,24,3584]{2,1,0:T(8,128)(2,1)}, u32[]{:S(2)}, u32[]{:S(2)}) %all-to-all-start) | async-done | bytes 688160 | tf_op jit(solution)/shard_map/all_to_all | solution.py:24
  63.8 1.9 %collective-permute-start.5 = (bf16[96,3584]{1,0:T(8,128)(2,1)}, bf16[96,3584]{1,0:T(8,128)(2,1)}, u32[]{:S(2)}, u32[]{:S(2)}) collective-permute-start(bf16[96,3584]{1,0:T(8,128)(2,1)} %bitcast.9), channel_id=1, source_target_pairs={{0,4},{1,5},{2,6},{3,7},{4,0},{5,1},{6,2},{7,3},{8,12},{9,13},{10,... | collective-permute-start | bytes 2064392 | tf_op jit(solution)/shard_map/ppermute | solution.py:53
  65.8 2.7 %collective-permute-start.2 = (bf16[96,3584]{1,0:T(8,128)(2,1)}, bf16[96,3584]{1,0:T(8,128)(2,1)}, u32[]{:S(2)}, u32[]{:S(2)}) collective-permute-start(bf16[96,3584]{1,0:T(8,128)(2,1)} %bitcast.9), channel_id=1, source_target_pairs={{0,7},{1,6},{2,5},{3,4},{4,3},{5,2},{6,1},{7,0},{8,15},{9,14},{10,... | collective-permute-start | bytes 2064392 | tf_op jit(solution)/shard_map/ppermute | solution.py:53
  68.5 3.8 %collective-permute-start.1 = (bf16[96,3584]{1,0:T(8,128)(2,1)}, bf16[96,3584]{1,0:T(8,128)(2,1)S(1)}, u32[]{:S(2)}, u32[]{:S(2)}) collective-permute-start(bf16[96,3584]{1,0:T(8,128)(2,1)} %bitcast.9), channel_id=1, source_target_pairs={{0,3},{1,2},{2,1},{3,0},{4,7},{5,6},{6,5},{7,4},{8,11},{9,10},{10,... | collective-permute-start | bytes 2064392 | tf_op jit(solution)/shard_map/ppermute | solution.py:53
  72.3 1.2 constant_dynamic-update-slice_fusion.3
  73.5 8.7 %collective-permute-done.5 = bf16[96,3584]{1,0:T(8,128)(2,1)} collective-permute-done((bf16[96,3584]{1,0:T(8,128)(2,1)}, bf16[96,3584]{1,0:T(8,128)(2,1)}, u32[]{:S(2)}, u32[]{:S(2)}) %collective-permute-start.5) | collective-permute-done | bytes 688160 | tf_op jit(solution)/shard_map/ppermute | solution.py:53
  82.2 5.6 %collective-permute-start.6 = (bf16[16,3840]{1,0:T(8,128)(2,1)}, bf16[16,3840]{1,0:T(8,128)(2,1)}, u32[]{:S(2)}, u32[]{:S(2)}) collective-permute-start(bf16[16,3840]{1,0:T(8,128)(2,1)} %get-tuple-element.19), channel_id=1, source_target_pairs={{0,480},{32,64},{64,32},{96,128},{128,96},{160,192},{192,160},{224... | collective-permute-start | bytes 368648 | tf_op jit(solution)/shard_map/ppermute | solution.py:43
  87.8 1.1 constant_dynamic-update-slice_fusion.2
  89.5 0.9 constant_dynamic-update-slice_fusion.1
  90.5 5.4 %collective-permute-done.2 = bf16[96,3584]{1,0:T(8,128)(2,1)} collective-permute-done((bf16[96,3584]{1,0:T(8,128)(2,1)}, bf16[96,3584]{1,0:T(8,128)(2,1)}, u32[]{:S(2)}, u32[]{:S(2)}) %collective-permute-start.2) | collective-permute-done | bytes 688160 | tf_op jit(solution)/shard_map/ppermute | solution.py:53
  95.9 2.0 %constant_dynamic-update-slice_fusion = bf16[192,3584]{1,0:T(8,128)(2,1)} fusion(bf16[192,3584]{1,0:T(8,128)(2,1)} %constant_dynamic-update-slice_fusion.1, bf16[96,3584]{1,0:T(8,128)(2,1)} %collective-permute-done.2), kind=kLoop, calls=%fused_computation.100 | loop fusion | bytes 1376256 | tf_op jit(solution)/shard_map/concatenate | solution.py:151
  97.9 2.0 %fusion.69 = f32[192,256]{1,0:T(8,128)S(1)} fusion(bf16[192,3584]{1,0:T(8,128)(2,1)} %constant_dynamic-update-slice_fusion, bf16[3584,256]{1,0:T(8,128)(2,1)S(1)} %pad_maximum_fusion), kind=kOutput, calls=%fused_computation.156 | convolution fusion | flops 352321536 | bytes 3407872 | tf_op jit(solution)/shard_map/dot_general | solution.py:144
  99.9 2.0 %fusion.70 = f32[192,256]{1,0:T(8,128)S(1)} fusion(bf16[192,3584]{1,0:T(8,128)(2,1)S(1)} %copy-done.2, bf16[3584,256]{1,0:T(8,128)(2,1)} %collective-permute-done.3), kind=kOutput, calls=%fused_computation.157 | convolution fusion | flops 352321536 | bytes 3407872 | tf_op jit(solution)/shard_map/dot_general | solution.py:144
  102.0 3.9 %collective-permute-start.4 = (bf16[192,256]{1,0:T(8,128)(2,1)S(1)}, bf16[192,256]{1,0:T(8,128)(2,1)S(1)}, u32[]{:S(2)}, u32[]{:S(2)}) collective-permute-start(bf16[192,256]{1,0:T(8,128)(2,1)S(1)} %pad_maximum_fusion.3), channel_id=1, source_target_pairs={{0,3},{1,2},{2,1},{3,0},{4,7},{5,6},{6,5},{7,4},{8,11},{9,10},{10,... | collective-permute-start | bytes 294920 | tf_op jit(solution)/shard_map/ppermute | solution.py:53
  105.9 2.2 %fusion.71 = f32[192,256]{1,0:T(8,128)S(1)} fusion(bf16[192,3584]{1,0:T(8,128)(2,1)S(1)} %constant_dynamic-update-slice_fusion.2, bf16[3584,256]{1,0:T(8,128)(2,1)} %collective-permute-done.3), kind=kOutput, calls=%fused_computation.158 | convolution fusion | flops 352321536 | bytes 3407872 | tf_op jit(solution)/shard_map/dot_general | solution.py:144
  108.5 0.7 convolution_convert_fusion
  109.3 2.2 %collective-permute-start.9 = (bf16[48,3584]{1,0:T(8,128)(2,1)S(1)}, bf16[48,3584]{1,0:T(8,128)(2,1)S(1)}, u32[]{:S(2)}, u32[]{:S(2)}) collective-permute-start(bf16[48,3584]{1,0:T(8,128)(2,1)S(1)} %get-tuple-element.38), channel_id=1, source_target_pairs={{0,4},{1,5},{2,6},{3,7},{4,0},{5,1},{6,2},{7,3},{8,12},{9,13},{10,... | collective-permute-start | bytes 1032200 | tf_op jit(solution)/shard_map/ppermute | solution.py:53
  111.6 0.7 fusion.40
  112.4 5.6 %collective-permute-start.8 = (bf16[48,3584]{1,0:T(8,128)(2,1)S(1)}, bf16[48,3584]{1,0:T(8,128)(2,1)S(1)}, u32[]{:S(2)}, u32[]{:S(2)}) collective-permute-start(bf16[48,3584]{1,0:T(8,128)(2,1)S(1)} %slice.239), channel_id=1, source_target_pairs={{0,32},{1,33},{2,34},{3,35},{4,36},{5,37},{6,38},{7,39},{8,40},{9,... | collective-permute-start | bytes 1032200 | tf_op jit(solution)/shard_map/ppermute | solution.py:63
  118.0 3.3 %collective-permute-start.7 = (bf16[48,3584]{1,0:T(8,128)(2,1)S(1)}, bf16[48,3584]{1,0:T(8,128)(2,1)S(1)}, u32[]{:S(2)}, u32[]{:S(2)}) collective-permute-start(bf16[48,3584]{1,0:T(8,128)(2,1)S(1)} %get-tuple-element.39), channel_id=1, source_target_pairs={{0,36},{1,37},{2,38},{3,39},{4,32},{5,33},{6,34},{7,35},{8,44},{9,... | collective-permute-start | bytes 1032200 | tf_op jit(solution)/shard_map/ppermute | solution.py:63
  121.4 8.3 %collective-permute-done.7 = bf16[48,3584]{1,0:T(8,128)(2,1)S(1)} collective-permute-done((bf16[48,3584]{1,0:T(8,128)(2,1)S(1)}, bf16[48,3584]{1,0:T(8,128)(2,1)S(1)}, u32[]{:S(2)}, u32[]{:S(2)}) %collective-permute-start.7) | collective-permute-done | bytes 344096 | tf_op jit(solution)/shard_map/ppermute | solution.py:63
  130.2 1.2 fusion
  131.4 10.6 %all-to-all-start.1 = ((bf16[8,24,1792]{2,1,0:T(8,128)(2,1)}), bf16[8,24,1792]{2,1,0:T(8,128)(2,1)S(1)}, u32[]{:S(2)}, u32[]{:S(2)}) async-start(bf16[8,24,1792]{2,1,0:T(8,128)(2,1)} %bitcast.15), calls=%async_computation.1 | async-start | bytes 1376256 | tf_op jit(solution)/shard_map/all_to_all | solution.py:36
  142.1 0.9 broadcast_select_fusion
  144.0 35.4 %all-to-all-done.1 = bf16[8,24,1792]{2,1,0:T(8,128)(2,1)S(1)} async-done(((bf16[8,24,1792]{2,1,0:T(8,128)(2,1)}), bf16[8,24,1792]{2,1,0:T(8,128)(2,1)S(1)}, u32[]{:S(2)}, u32[]{:S(2)}) %all-to-all-start.1) | async-done | bytes 688160 | tf_op jit(solution)/shard_map/all_to_all | solution.py:36
  (134 shorter events, 9.4 us)
Async XLA Ops:
  7.2 20.5 %copy-start = (bf16[1,3584,4]{1,2,0:T(4,128)(2,1)S(1)}, bf16[1,3584,4]{1,2,0:T(4,128)(2,1)}, u32[]{:S(2)}) copy-start(bf16[1,3584,4]{1,2,0:T(4,128)(2,1)} %param.14) | copy-start | bytes 86020
  7.2 1.2 copy-start.5
  7.2 88.7 %all-gather.3.cloned.1.call-start = ((), (), s32[]{:S(2)}) async-start(), calls=%async_computation.2 | async-start | bytes 4587520 | tf_op jit(solution)/shard_map/all_gather | solution.py:69
  8.4 6.0 %copy-start.9 = (s32[1,16,2]{1,2,0:T(2,128)S(1)}, s32[1,16,2]{1,2,0:T(2,128)}, u32[]{:S(2)}) copy-start(s32[1,16,2]{1,2,0:T(2,128)} %param.11) | copy-start | bytes 388
  8.4 6.0 %copy-start.10 = (s32[1,16,2]{1,2,0:T(2,128)S(1)}, s32[1,16,2]{1,2,0:T(2,128)}, u32[]{:S(2)}) copy-start(s32[1,16,2]{1,2,0:T(2,128)} %param.12) | copy-start | bytes 388
  8.4 6.7 %copy-start.4 = (bf16[1,16,3584]{2,1,0:T(8,128)(2,1)S(1)}, bf16[1,16,3584]{2,1,0:T(8,128)(2,1)}, u32[]{:S(2)}) copy-start(bf16[1,16,3584]{2,1,0:T(8,128)(2,1)} %param.9) | copy-start | bytes 344068
  8.4 6.9 %copy-start.3 = (bf16[1,16,3584]{2,1,0:T(8,128)(2,1)S(1)}, bf16[1,16,3584]{2,1,0:T(8,128)(2,1)}, u32[]{:S(2)}) copy-start(bf16[1,16,3584]{2,1,0:T(8,128)(2,1)} %param.10) | copy-start | bytes 344068
  8.4 7.1 %copy-start.8 = (f32[1,3584]{1,0:T(1,128)S(1)}, f32[1,3584]{1,0:T(1,128)}, u32[]{:S(2)}) copy-start(f32[1,3584]{1,0:T(1,128)} %param.13) | copy-start | bytes 43012
  10.0 89.9 %collective-permute-start.3 = (bf16[3584,256]{1,0:T(8,128)(2,1)S(1)}, bf16[3584,256]{1,0:T(8,128)(2,1)}, u32[]{:S(2)}, u32[]{:S(2)}) collective-permute-start(bf16[3584,256]{1,0:T(8,128)(2,1)S(1)} %pad_maximum_fusion), channel_id=1, source_target_pairs={{0,1},{1,0},{2,3},{3,2},{4,5},{5,4},{6,7},{7,6},{8,9},{9,8},{10,11... | collective-permute-start | bytes 5505032 | tf_op jit(solution)/shard_map/ppermute | solution.py:53
  16.8 47.0 %all-to-all-start = ((bf16[4,24,3584]{2,1,0:T(8,128)(2,1)}), bf16[4,24,3584]{2,1,0:T(8,128)(2,1)}, u32[]{:S(2)}, u32[]{:S(2)}) async-start(bf16[4,24,3584]{2,1,0:T(8,128)(2,1)} %bitcast.8), calls=%async_computation | async-start | bytes 1376256 | tf_op jit(solution)/shard_map/all_to_all | solution.py:24
  30.1 3.2 %collective-permute-start = (bf16[16,3840]{1,0:T(8,128)(2,1)S(1)}, bf16[16,3840]{1,0:T(8,128)(2,1)S(1)}, u32[]{:S(2)}, u32[]{:S(2)}) collective-permute-start(bf16[16,3840]{1,0:T(8,128)(2,1)S(1)} %get-tuple-element.46), channel_id=1, source_target_pairs={{0,32},{1,33},{2,34},{3,35},{4,36},{5,37},{6,38},{7,39},{8,40},{9,... | collective-permute-start | bytes 368648 | tf_op jit(solution)/shard_map/ppermute | solution.py:63
  33.3 32.4 %copy-start.6 = (bf16[16,3840]{1,0:T(8,128)(2,1)}, bf16[16,3840]{1,0:T(8,128)(2,1)S(1)}, u32[]{:S(2)}) copy-start(bf16[16,3840]{1,0:T(8,128)(2,1)S(1)} %collective-permute-done) | copy-start | bytes 368644
  63.8 18.4 %collective-permute-start.5 = (bf16[96,3584]{1,0:T(8,128)(2,1)}, bf16[96,3584]{1,0:T(8,128)(2,1)}, u32[]{:S(2)}, u32[]{:S(2)}) collective-permute-start(bf16[96,3584]{1,0:T(8,128)(2,1)} %bitcast.9), channel_id=1, source_target_pairs={{0,4},{1,5},{2,6},{3,7},{4,0},{5,1},{6,2},{7,3},{8,12},{9,13},{10,... | collective-permute-start | bytes 2064392 | tf_op jit(solution)/shard_map/ppermute | solution.py:53
  65.8 30.0 %collective-permute-start.2 = (bf16[96,3584]{1,0:T(8,128)(2,1)}, bf16[96,3584]{1,0:T(8,128)(2,1)}, u32[]{:S(2)}, u32[]{:S(2)}) collective-permute-start(bf16[96,3584]{1,0:T(8,128)(2,1)} %bitcast.9), channel_id=1, source_target_pairs={{0,7},{1,6},{2,5},{3,4},{4,3},{5,2},{6,1},{7,0},{8,15},{9,14},{10,... | collective-permute-start | bytes 2064392 | tf_op jit(solution)/shard_map/ppermute | solution.py:53
  68.5 21.0 %collective-permute-start.1 = (bf16[96,3584]{1,0:T(8,128)(2,1)}, bf16[96,3584]{1,0:T(8,128)(2,1)S(1)}, u32[]{:S(2)}, u32[]{:S(2)}) collective-permute-start(bf16[96,3584]{1,0:T(8,128)(2,1)} %bitcast.9), channel_id=1, source_target_pairs={{0,3},{1,2},{2,1},{3,0},{4,7},{5,6},{6,5},{7,4},{8,11},{9,10},{10,... | collective-permute-start | bytes 2064392 | tf_op jit(solution)/shard_map/ppermute | solution.py:53
  82.2 25.9 %collective-permute-start.6 = (bf16[16,3840]{1,0:T(8,128)(2,1)}, bf16[16,3840]{1,0:T(8,128)(2,1)}, u32[]{:S(2)}, u32[]{:S(2)}) collective-permute-start(bf16[16,3840]{1,0:T(8,128)(2,1)} %get-tuple-element.19), channel_id=1, source_target_pairs={{0,480},{32,64},{64,32},{96,128},{128,96},{160,192},{192,160},{224... | collective-permute-start | bytes 368648 | tf_op jit(solution)/shard_map/ppermute | solution.py:43
  97.9 2.0 %copy-start.2 = (bf16[192,3584]{1,0:T(8,128)(2,1)S(1)}, bf16[192,3584]{1,0:T(8,128)(2,1)}, u32[]{:S(2)}) copy-start(bf16[192,3584]{1,0:T(8,128)(2,1)} %constant_dynamic-update-slice_fusion) | copy-start | bytes 4128772
  102.0 6.1 %collective-permute-start.4 = (bf16[192,256]{1,0:T(8,128)(2,1)S(1)}, bf16[192,256]{1,0:T(8,128)(2,1)S(1)}, u32[]{:S(2)}, u32[]{:S(2)}) collective-permute-start(bf16[192,256]{1,0:T(8,128)(2,1)S(1)} %pad_maximum_fusion.3), channel_id=1, source_target_pairs={{0,3},{1,2},{2,1},{3,0},{4,7},{5,6},{6,5},{7,4},{8,11},{9,10},{10,... | collective-permute-start | bytes 294920 | tf_op jit(solution)/shard_map/ppermute | solution.py:53
  105.9 2.6 %copy-start.1 = (bf16[1,512,3584]{2,1,0:T(8,128)(2,1)S(1)}, bf16[1,512,3584]{2,1,0:T(8,128)(2,1)}, u32[]{:S(2)}) copy-start(bf16[1,512,3584]{2,1,0:T(8,128)(2,1)} %all-gather.3.cloned.1.call-done) | copy-start | bytes 11010052
  109.3 11.9 %collective-permute-start.9 = (bf16[48,3584]{1,0:T(8,128)(2,1)S(1)}, bf16[48,3584]{1,0:T(8,128)(2,1)S(1)}, u32[]{:S(2)}, u32[]{:S(2)}) collective-permute-start(bf16[48,3584]{1,0:T(8,128)(2,1)S(1)} %get-tuple-element.38), channel_id=1, source_target_pairs={{0,4},{1,5},{2,6},{3,7},{4,0},{5,1},{6,2},{7,3},{8,12},{9,13},{10,... | collective-permute-start | bytes 1032200 | tf_op jit(solution)/shard_map/ppermute | solution.py:53
  112.4 9.0 %collective-permute-start.8 = (bf16[48,3584]{1,0:T(8,128)(2,1)S(1)}, bf16[48,3584]{1,0:T(8,128)(2,1)S(1)}, u32[]{:S(2)}, u32[]{:S(2)}) collective-permute-start(bf16[48,3584]{1,0:T(8,128)(2,1)S(1)} %slice.239), channel_id=1, source_target_pairs={{0,32},{1,33},{2,34},{3,35},{4,36},{5,37},{6,38},{7,39},{8,40},{9,... | collective-permute-start | bytes 1032200 | tf_op jit(solution)/shard_map/ppermute | solution.py:63
  118.0 11.7 %collective-permute-start.7 = (bf16[48,3584]{1,0:T(8,128)(2,1)S(1)}, bf16[48,3584]{1,0:T(8,128)(2,1)S(1)}, u32[]{:S(2)}, u32[]{:S(2)}) collective-permute-start(bf16[48,3584]{1,0:T(8,128)(2,1)S(1)} %get-tuple-element.39), channel_id=1, source_target_pairs={{0,36},{1,37},{2,38},{3,39},{4,32},{5,33},{6,34},{7,35},{8,44},{9,... | collective-permute-start | bytes 1032200 | tf_op jit(solution)/shard_map/ppermute | solution.py:63
  131.4 10.7 %copy-start.7 = (bf16[16,3840]{1,0:T(8,128)(2,1)S(1)}, bf16[16,3840]{1,0:T(8,128)(2,1)}, u32[]{:S(2)}) copy-start(bf16[16,3840]{1,0:T(8,128)(2,1)} %copy-done.6) | copy-start | bytes 368644
  131.4 48.0 %all-to-all-start.1 = ((bf16[8,24,1792]{2,1,0:T(8,128)(2,1)}), bf16[8,24,1792]{2,1,0:T(8,128)(2,1)S(1)}, u32[]{:S(2)}, u32[]{:S(2)}) async-start(bf16[8,24,1792]{2,1,0:T(8,128)(2,1)} %bitcast.15), calls=%async_computation.1 | async-start | bytes 1376256 | tf_op jit(solution)/shard_map/all_to_all | solution.py:36
Sparse Core Ops, SparseCore 0:
  10.1 55.8 all-gather.2

commit v5 on v4

--- a/solution.py
+++ b/solution.py
@@ -143,14 +143,19 @@
 
     dot = lambda a, b: jnp.dot(a, b, preferred_element_type=jnp.float32)
     exact = lambda a, b: jnp.dot(a, b, precision=lax.Precision.HIGHEST, preferred_element_type=jnp.float32)
-    act = lambda joined: (jax.nn.silu(joined[:, :hidden_n]) * joined[:, hidden_n:]).astype(jnp.bfloat16)
-    cross_set, pair = lax.optimization_barrier((cross_set, pair))
+    all_cols = jnp.concatenate([both_cols, next_cols], axis=1)
+    cross_set, all_cols, pair = lax.optimization_barrier((cross_set, all_cols, pair))
     cross_set = neighbour(cross_set)
     corner, down_rows = lax.optimization_barrier((corner, down_rows))
     near_rows = jnp.concatenate([mine, pair], axis=0)
     far_rows = jnp.concatenate([across, corner], axis=0)
-    sent = jnp.concatenate([act(dot(far_rows, both_cols)), act(dot(far_rows, next_cols))], axis=1)
-    kept = [act(dot(near_rows, both_cols)), act(dot(near_rows, next_cols))]
+    def units(rows):
+        joined = dot(rows, all_cols).reshape(rows.shape[0], 2, 2 * hidden_n)
+        return (jax.nn.silu(joined[:, :, :hidden_n]) * joined[:, :, hidden_n:]).astype(jnp.bfloat16)
+
+    sent = units(far_rows).reshape(4 * slots, 2 * hidden_n)
+    kept = units(near_rows)
+    kept = [kept[:, 0], kept[:, 1]]
     got = facing(sent, 0, 3, 1)
     got, cross_set = lax.optimization_barrier((got, cross_set))
     first, second = got[:, :hidden_n], got[:, hidden_n:]

time: 189 us -> 184 us (0.974)
  the two profiles are of different devices: /device:TPU:17 before, /device:TPU:1 now
where the time goes in v5:
time: 184 us
  waiting for transfers between devices  92.8 us (50%)
  starting transfers between devices  52.5 us (29%)
  between operations  14.7 us (8%)
  matrix products  13.1 us (7%)
  other arithmetic  6.67 us (4%)
  local copies, waits for them, and re-layouts  3.93 us (2%)
    all_to_all x1, waiting for transfers between devices, across_sections(): lax.all_to_all(chunks, ('pipe', 'expert'), split_axis=0, concat_axis=0, t...  35.9 us
    all_to_all x1, waiting for transfers between devices, across_groups(): lax.all_to_all(chunks, 'expert', split_axis=0, concat_axis=0, tiled=True,...  30.2 us
    ppermute x6, starting transfers between devices, facing(): return lax.ppermute(block, ('pipe', 'expert'), route)  19.4 us
    ppermute x6, waiting for transfers between devices, facing(): return lax.ppermute(block, ('pipe', 'expert'), route)  17.7 us
    ppermute x3, starting transfers between devices, other_core(): return lax.ppermute(block, ('pipe', 'expert'), route)  11.6 us
    all_to_all x1, starting transfers between devices, across_groups(): lax.all_to_all(chunks, 'expert', split_axis=0, concat_axis=0, tiled=True,...  10.9 us
    dot_general x7, matrix products, on_device(): dot = lambda a, b: jnp.dot(a, b, preferred_element_type=jnp.float32)  10.8 us
    ppermute x3, waiting for transfers between devices, other_core(): return lax.ppermute(block, ('pipe', 'expert'), route)  8.29 us
  transfers between devices with their start and end apart: 13, of which 7 were waited for; matrix products, arithmetic and copies ran while one was open for 8% of the time, Pallas kernels for 0%

profile of v5, /device:TPU:1, one launch (start us, length us, event | category | flops | bytes accessed | tf_op | source)
XLA Modules:
  0.0 183.7 jit_solution(14046453648363982889)
XLA Ops:
  7.2 1.8 pad_maximum_fusion.1
  9.0 5.2 %collective-permute-start.3 = (bf16[3584,256]{1,0:T(8,128)(2,1)S(1)}, bf16[3584,256]{1,0:T(8,128)(2,1)}, u32[]{:S(2)}, u32[]{:S(2)}) collective-permute-start(bf16[3584,256]{1,0:T(8,128)(2,1)S(1)} %pad_maximum_fusion.1), channel_id=1, source_target_pairs={{0,1},{1,0},{2,3},{3,2},{4,5},{5,4},{6,7},{7,6},{8,9},{9,8},{10,11... | collective-permute-start | bytes 5505032 | tf_op jit(solution)/shard_map/ppermute | solution.py:53
  15.5 1.2 convolution_convert_fusion.1
  16.7 10.9 %all-to-all-start = ((bf16[4,24,3584]{2,1,0:T(8,128)(2,1)}), bf16[4,24,3584]{2,1,0:T(8,128)(2,1)S(1)}, u32[]{:S(2)}, u32[]{:S(2)}) async-start(bf16[4,24,3584]{2,1,0:T(8,128)(2,1)} %bitcast.8), calls=%async_computation | async-start | bytes 1376256 | tf_op jit(solution)/shard_map/all_to_all | solution.py:24
  27.5 0.7 all-gather.3.cloned.1.call-update
  30.1 1.9 %collective-permute-start = (bf16[16,3840]{1,0:T(8,128)(2,1)S(1)}, bf16[16,3840]{1,0:T(8,128)(2,1)S(1)}, u32[]{:S(2)}, u32[]{:S(2)}) collective-permute-start(bf16[16,3840]{1,0:T(8,128)(2,1)S(1)} %get-tuple-element.51), channel_id=1, source_target_pairs={{0,32},{1,33},{2,34},{3,35},{4,36},{5,37},{6,38},{7,39},{8,40},{9,... | collective-permute-start | bytes 368648 | tf_op jit(solution)/shard_map/ppermute | solution.py:63
  32.6 0.7 collective-permute-done
  33.3 30.2 %all-to-all-done = bf16[4,24,3584]{2,1,0:T(8,128)(2,1)S(1)} async-done(((bf16[4,24,3584]{2,1,0:T(8,128)(2,1)}), bf16[4,24,3584]{2,1,0:T(8,128)(2,1)S(1)}, u32[]{:S(2)}, u32[]{:S(2)}) %all-to-all-start) | async-done | bytes 688160 | tf_op jit(solution)/shard_map/all_to_all | solution.py:24
  63.5 1.9 %collective-permute-start.4 = (bf16[96,3584]{1,0:T(8,128)(2,1)S(1)}, bf16[96,3584]{1,0:T(8,128)(2,1)}, u32[]{:S(2)}, u32[]{:S(2)}) collective-permute-start(bf16[96,3584]{1,0:T(8,128)(2,1)S(1)} %bitcast.87), channel_id=1, source_target_pairs={{0,4},{1,5},{2,6},{3,7},{4,0},{5,1},{6,2},{7,3},{8,12},{9,13},{10,... | collective-permute-start | bytes 2064392 | tf_op jit(solution)/shard_map/ppermute | solution.py:53
  66.0 2.7 %collective-permute-start.2 = (bf16[96,3584]{1,0:T(8,128)(2,1)S(1)}, bf16[96,3584]{1,0:T(8,128)(2,1)}, u32[]{:S(2)}, u32[]{:S(2)}) collective-permute-start(bf16[96,3584]{1,0:T(8,128)(2,1)S(1)} %bitcast.88), channel_id=1, source_target_pairs={{0,7},{1,6},{2,5},{3,4},{4,3},{5,2},{6,1},{7,0},{8,15},{9,14},{10,... | collective-permute-start | bytes 2064392 | tf_op jit(solution)/shard_map/ppermute | solution.py:53
  68.6 3.8 %collective-permute-start.1 = (bf16[96,3584]{1,0:T(8,128)(2,1)S(1)}, bf16[96,3584]{1,0:T(8,128)(2,1)}, u32[]{:S(2)}, u32[]{:S(2)}) collective-permute-start(bf16[96,3584]{1,0:T(8,128)(2,1)S(1)} %bitcast.89), channel_id=1, source_target_pairs={{0,3},{1,2},{2,1},{3,0},{4,7},{5,6},{6,5},{7,4},{8,11},{9,10},{10,... | collective-permute-start | bytes 2064392 | tf_op jit(solution)/shard_map/ppermute | solution.py:53
  72.5 1.8 pad_maximum_fusion
  74.2 7.5 %collective-permute-done.4 = bf16[96,3584]{1,0:T(8,128)(2,1)} collective-permute-done((bf16[96,3584]{1,0:T(8,128)(2,1)S(1)}, bf16[96,3584]{1,0:T(8,128)(2,1)}, u32[]{:S(2)}, u32[]{:S(2)}) %collective-permute-start.4) | collective-permute-done | bytes 688160 | tf_op jit(solution)/shard_map/ppermute | solution.py:53
  81.7 2.0 %fusion.5 = f32[192,512]{1,0:T(8,128)S(1)} fusion(bf16[3584,512]{1,0:T(8,128)(2,1)S(1)} %pad_maximum_fusion, bf16[96,3584]{1,0:T(8,128)(2,1)} %collective-permute-done.4, bf16[96,3584]{1,0:T(8,128)(2,1)S(1)} %bitcast.90), kind=kOutput, calls=%fused_computation.10 | convolution fusion | flops 707395584 | bytes 5439488 | tf_op jit(solution)/shard_map/dot_general | solution.py:144
  84.0 5.9 %collective-permute-start.6 = (bf16[16,3840]{1,0:T(8,128)(2,1)S(1)}, bf16[16,3840]{1,0:T(8,128)(2,1)S(1)}, u32[]{:S(2)}, u32[]{:S(2)}) collective-permute-start(bf16[16,3840]{1,0:T(8,128)(2,1)S(1)} %get-tuple-element.21), channel_id=1, source_target_pairs={{0,480},{32,64},{64,32},{96,128},{128,96},{160,192},{192,160},{224... | collective-permute-start | bytes 368648 | tf_op jit(solution)/shard_map/ppermute | solution.py:43
  90.1 8.0 %collective-permute-done.2 = bf16[96,3584]{1,0:T(8,128)(2,1)} collective-permute-done((bf16[96,3584]{1,0:T(8,128)(2,1)S(1)}, bf16[96,3584]{1,0:T(8,128)(2,1)}, u32[]{:S(2)}, u32[]{:S(2)}) %collective-permute-start.2) | collective-permute-done | bytes 688160 | tf_op jit(solution)/shard_map/ppermute | solution.py:53
  98.0 3.3 %fusion.1 = f32[192,512]{1,0:T(8,128)S(1)} fusion(bf16[3584,512]{1,0:T(8,128)(2,1)} %copy-done.2, bf16[96,3584]{1,0:T(8,128)(2,1)} %collective-permute-done.2, bf16[96,3584]{1,0:T(8,128)(2,1)} %collective-permute-done.1), kind=kOutput, calls=%fused_computation.6 | convolution fusion | flops 707395584 | bytes 5439488 | tf_op jit(solution)/shard_map/dot_general | solution.py:144
  101.8 3.9 %collective-permute-start.5 = (bf16[192,256]{1,0:T(8,128)(2,1)S(1)}, bf16[192,256]{1,0:T(8,128)(2,1)S(1)}, u32[]{:S(2)}, u32[]{:S(2)}) collective-permute-start(bf16[192,256]{1,0:T(8,128)(2,1)S(1)} %copy_bitcast_fusion), channel_id=1, source_target_pairs={{0,3},{1,2},{2,1},{3,0},{4,7},{5,6},{6,5},{7,4},{8,11},{9,10},{10,... | collective-permute-start | bytes 294920 | tf_op jit(solution)/shard_map/ppermute | solution.py:53
  105.8 2.2 %collective-permute-done.5 = bf16[192,256]{1,0:T(8,128)(2,1)S(1)} collective-permute-done((bf16[192,256]{1,0:T(8,128)(2,1)S(1)}, bf16[192,256]{1,0:T(8,128)(2,1)S(1)}, u32[]{:S(2)}, u32[]{:S(2)}) %collective-permute-start.5) | collective-permute-done | bytes 98336 | tf_op jit(solution)/shard_map/ppermute | solution.py:53
  108.3 2.9 %convolution_convert_fusion = bf16[96,3584]{1,0:T(8,128)(2,1)S(1)} fusion(bf16[512,3584]{1,0:T(8,128)(2,1)} %bitcast.79, bf16[192,512]{1,0:T(8,128)(2,1)S(1)} %convolution_convert_fusion.2), kind=kOutput, calls=%fused_computation | convolution fusion | flops 352665600 | bytes 4456448 | tf_op jit(solution)/shard_map/dot_general | solution.py:144
  111.3 1.9 %collective-permute-start.9 = (bf16[48,3584]{1,0:T(8,128)(2,1)S(1)}, bf16[48,3584]{1,0:T(8,128)(2,1)S(1)}, u32[]{:S(2)}, u32[]{:S(2)}) collective-permute-start(bf16[48,3584]{1,0:T(8,128)(2,1)S(1)} %get-tuple-element.39), channel_id=1, source_target_pairs={{0,4},{1,5},{2,6},{3,7},{4,0},{5,1},{6,2},{7,3},{8,12},{9,13},{10,... | collective-permute-start | bytes 1032200 | tf_op jit(solution)/shard_map/ppermute | solution.py:53
  113.2 7.7 %collective-permute-start.7 = (bf16[48,3584]{1,0:T(8,128)(2,1)S(1)}, bf16[48,3584]{1,0:T(8,128)(2,1)S(1)}, u32[]{:S(2)}, u32[]{:S(2)}) collective-permute-start(bf16[48,3584]{1,0:T(8,128)(2,1)S(1)} %get-tuple-element.40), channel_id=1, source_target_pairs={{0,36},{1,37},{2,38},{3,39},{4,32},{5,33},{6,34},{7,35},{8,44},{9,... | collective-permute-start | bytes 1032200 | tf_op jit(solution)/shard_map/ppermute | solution.py:63
  121.0 0.7 fusion.50
  121.8 1.9 %collective-permute-start.8 = (bf16[48,3584]{1,0:T(8,128)(2,1)S(1)}, bf16[48,3584]{1,0:T(8,128)(2,1)S(1)}, u32[]{:S(2)}, u32[]{:S(2)}) collective-permute-start(bf16[48,3584]{1,0:T(8,128)(2,1)S(1)} %slice.231), channel_id=1, source_target_pairs={{0,32},{1,33},{2,34},{3,35},{4,36},{5,37},{6,38},{7,39},{8,40},{9,... | collective-permute-start | bytes 1032200 | tf_op jit(solution)/shard_map/ppermute | solution.py:63
  123.8 7.6 %collective-permute-done.7 = bf16[48,3584]{1,0:T(8,128)(2,1)S(1)} collective-permute-done((bf16[48,3584]{1,0:T(8,128)(2,1)S(1)}, bf16[48,3584]{1,0:T(8,128)(2,1)S(1)}, u32[]{:S(2)}, u32[]{:S(2)}) %collective-permute-start.7) | collective-permute-done | bytes 344096 | tf_op jit(solution)/shard_map/ppermute | solution.py:63
  131.4 0.4 fusion.17
  131.8 1.2 fusion
  133.1 4.7 %all-to-all-start.1 = ((bf16[8,24,1792]{2,1,0:T(8,128)(2,1)}), bf16[8,24,1792]{2,1,0:T(8,128)(2,1)S(1)}, u32[]{:S(2)}, u32[]{:S(2)}) async-start(bf16[8,24,1792]{2,1,0:T(8,128)(2,1)} %bitcast.17), calls=%async_computation.1 | async-start | bytes 1376256 | tf_op jit(solution)/shard_map/all_to_all | solution.py:36
  138.9 35.9 %all-to-all-done.1 = bf16[8,24,1792]{2,1,0:T(8,128)(2,1)S(1)} async-done(((bf16[8,24,1792]{2,1,0:T(8,128)(2,1)}), bf16[8,24,1792]{2,1,0:T(8,128)(2,1)S(1)}, u32[]{:S(2)}, u32[]{:S(2)}) %all-to-all-start.1) | async-done | bytes 688160 | tf_op jit(solution)/shard_map/all_to_all | solution.py:36
  175.2 0.3 fusion.79
  175.5 0.7 fusion.44
  176.2 0.7 fusion.45
  (126 shorter events, 6.8 us)
Async XLA Ops:
  7.2 21.1 %copy-start = (bf16[1,3584,4]{1,2,0:T(4,128)(2,1)S(1)}, bf16[1,3584,4]{1,2,0:T(4,128)(2,1)}, u32[]{:S(2)}) copy-start(bf16[1,3584,4]{1,2,0:T(4,128)(2,1)} %param.14) | copy-start | bytes 86020
  7.2 7.0 %copy-start.3 = (bf16[1,16,3584]{2,1,0:T(8,128)(2,1)S(1)}, bf16[1,16,3584]{2,1,0:T(8,128)(2,1)}, u32[]{:S(2)}) copy-start(bf16[1,16,3584]{2,1,0:T(8,128)(2,1)} %param.10) | copy-start | bytes 344068
  7.2 7.2 %copy-start.4 = (bf16[1,16,3584]{2,1,0:T(8,128)(2,1)S(1)}, bf16[1,16,3584]{2,1,0:T(8,128)(2,1)}, u32[]{:S(2)}) copy-start(bf16[1,16,3584]{2,1,0:T(8,128)(2,1)} %param.9) | copy-start | bytes 344068
  7.2 7.3 %copy-start.6 = (s32[1,16,2]{1,2,0:T(2,128)S(1)}, s32[1,16,2]{1,2,0:T(2,128)}, u32[]{:S(2)}) copy-start(s32[1,16,2]{1,2,0:T(2,128)} %param.12) | copy-start | bytes 388
  7.2 7.5 %copy-start.7 = (s32[1,16,2]{1,2,0:T(2,128)S(1)}, s32[1,16,2]{1,2,0:T(2,128)}, u32[]{:S(2)}) copy-start(s32[1,16,2]{1,2,0:T(2,128)} %param.11) | copy-start | bytes 388
  7.2 8.1 %copy-start.5 = (f32[1,3584]{1,0:T(1,128)S(1)}, f32[1,3584]{1,0:T(1,128)}, u32[]{:S(2)}) copy-start(f32[1,3584]{1,0:T(1,128)} %param.13) | copy-start | bytes 43012
  9.0 63.4 %collective-permute-start.3 = (bf16[3584,256]{1,0:T(8,128)(2,1)S(1)}, bf16[3584,256]{1,0:T(8,128)(2,1)}, u32[]{:S(2)}, u32[]{:S(2)}) collective-permute-start(bf16[3584,256]{1,0:T(8,128)(2,1)S(1)} %pad_maximum_fusion.1), channel_id=1, source_target_pairs={{0,1},{1,0},{2,3},{3,2},{4,5},{5,4},{6,7},{7,6},{8,9},{9,8},{10,11... | collective-permute-start | bytes 5505032 | tf_op jit(solution)/shard_map/ppermute | solution.py:53
  16.7 46.9 %all-to-all-start = ((bf16[4,24,3584]{2,1,0:T(8,128)(2,1)}), bf16[4,24,3584]{2,1,0:T(8,128)(2,1)S(1)}, u32[]{:S(2)}, u32[]{:S(2)}) async-start(bf16[4,24,3584]{2,1,0:T(8,128)(2,1)} %bitcast.8), calls=%async_computation | async-start | bytes 1376256 | tf_op jit(solution)/shard_map/all_to_all | solution.py:24
  27.5 70.5 %all-gather.3.cloned.1.call-start = ((), (), s32[]{:S(2)}) async-start(), calls=%async_computation.2 | async-start | bytes 4587520 | tf_op jit(solution)/shard_map/all_gather | solution.py:69
  30.1 3.2 %collective-permute-start = (bf16[16,3840]{1,0:T(8,128)(2,1)S(1)}, bf16[16,3840]{1,0:T(8,128)(2,1)S(1)}, u32[]{:S(2)}, u32[]{:S(2)}) collective-permute-start(bf16[16,3840]{1,0:T(8,128)(2,1)S(1)} %get-tuple-element.51), channel_id=1, source_target_pairs={{0,32},{1,33},{2,34},{3,35},{4,36},{5,37},{6,38},{7,39},{8,40},{9,... | collective-permute-start | bytes 368648 | tf_op jit(solution)/shard_map/ppermute | solution.py:63
  63.5 18.2 %collective-permute-start.4 = (bf16[96,3584]{1,0:T(8,128)(2,1)S(1)}, bf16[96,3584]{1,0:T(8,128)(2,1)}, u32[]{:S(2)}, u32[]{:S(2)}) collective-permute-start(bf16[96,3584]{1,0:T(8,128)(2,1)S(1)} %bitcast.87), channel_id=1, source_target_pairs={{0,4},{1,5},{2,6},{3,7},{4,0},{5,1},{6,2},{7,3},{8,12},{9,13},{10,... | collective-permute-start | bytes 2064392 | tf_op jit(solution)/shard_map/ppermute | solution.py:53
  66.0 32.0 %collective-permute-start.2 = (bf16[96,3584]{1,0:T(8,128)(2,1)S(1)}, bf16[96,3584]{1,0:T(8,128)(2,1)}, u32[]{:S(2)}, u32[]{:S(2)}) collective-permute-start(bf16[96,3584]{1,0:T(8,128)(2,1)S(1)} %bitcast.88), channel_id=1, source_target_pairs={{0,7},{1,6},{2,5},{3,4},{4,3},{5,2},{6,1},{7,0},{8,15},{9,14},{10,... | collective-permute-start | bytes 2064392 | tf_op jit(solution)/shard_map/ppermute | solution.py:53
  68.6 29.4 %collective-permute-start.1 = (bf16[96,3584]{1,0:T(8,128)(2,1)S(1)}, bf16[96,3584]{1,0:T(8,128)(2,1)}, u32[]{:S(2)}, u32[]{:S(2)}) collective-permute-start(bf16[96,3584]{1,0:T(8,128)(2,1)S(1)} %bitcast.89), channel_id=1, source_target_pairs={{0,3},{1,2},{2,1},{3,0},{4,7},{5,6},{6,5},{7,4},{8,11},{9,10},{10,... | collective-permute-start | bytes 2064392 | tf_op jit(solution)/shard_map/ppermute | solution.py:53
  74.2 7.5 %copy-start.2 = (bf16[3584,512]{1,0:T(8,128)(2,1)}, bf16[3584,512]{1,0:T(8,128)(2,1)S(1)}, u32[]{:S(2)}) copy-start(bf16[3584,512]{1,0:T(8,128)(2,1)S(1)} %pad_maximum_fusion) | copy-start | bytes 11010052
  84.0 21.8 %collective-permute-start.6 = (bf16[16,3840]{1,0:T(8,128)(2,1)S(1)}, bf16[16,3840]{1,0:T(8,128)(2,1)S(1)}, u32[]{:S(2)}, u32[]{:S(2)}) collective-permute-start(bf16[16,3840]{1,0:T(8,128)(2,1)S(1)} %get-tuple-element.21), channel_id=1, source_target_pairs={{0,480},{32,64},{64,32},{96,128},{128,96},{160,192},{192,160},{224... | collective-permute-start | bytes 368648 | tf_op jit(solution)/shard_map/ppermute | solution.py:43
  101.8 6.2 %collective-permute-start.5 = (bf16[192,256]{1,0:T(8,128)(2,1)S(1)}, bf16[192,256]{1,0:T(8,128)(2,1)S(1)}, u32[]{:S(2)}, u32[]{:S(2)}) collective-permute-start(bf16[192,256]{1,0:T(8,128)(2,1)S(1)} %copy_bitcast_fusion), channel_id=1, source_target_pairs={{0,3},{1,2},{2,1},{3,0},{4,7},{5,6},{6,5},{7,4},{8,11},{9,10},{10,... | collective-permute-start | bytes 294920 | tf_op jit(solution)/shard_map/ppermute | solution.py:53
  108.3 12.6 %copy-start.1 = (bf16[1,512,3584]{2,1,0:T(8,128)(2,1)S(1)}, bf16[1,512,3584]{2,1,0:T(8,128)(2,1)}, u32[]{:S(2)}) copy-start(bf16[1,512,3584]{2,1,0:T(8,128)(2,1)} %all-gather.3.cloned.1.call-done) | copy-start | bytes 11010052
  111.3 12.4 %collective-permute-start.9 = (bf16[48,3584]{1,0:T(8,128)(2,1)S(1)}, bf16[48,3584]{1,0:T(8,128)(2,1)S(1)}, u32[]{:S(2)}, u32[]{:S(2)}) collective-permute-start(bf16[48,3584]{1,0:T(8,128)(2,1)S(1)} %get-tuple-element.39), channel_id=1, source_target_pairs={{0,4},{1,5},{2,6},{3,7},{4,0},{5,1},{6,2},{7,3},{8,12},{9,13},{10,... | collective-permute-start | bytes 1032200 | tf_op jit(solution)/shard_map/ppermute | solution.py:53
  113.2 18.1 %collective-permute-start.7 = (bf16[48,3584]{1,0:T(8,128)(2,1)S(1)}, bf16[48,3584]{1,0:T(8,128)(2,1)S(1)}, u32[]{:S(2)}, u32[]{:S(2)}) collective-permute-start(bf16[48,3584]{1,0:T(8,128)(2,1)S(1)} %get-tuple-element.40), channel_id=1, source_target_pairs={{0,36},{1,37},{2,38},{3,39},{4,32},{5,33},{6,34},{7,35},{8,44},{9,... | collective-permute-start | bytes 1032200 | tf_op jit(solution)/shard_map/ppermute | solution.py:63
  121.8 9.6 %collective-permute-start.8 = (bf16[48,3584]{1,0:T(8,128)(2,1)S(1)}, bf16[48,3584]{1,0:T(8,128)(2,1)S(1)}, u32[]{:S(2)}, u32[]{:S(2)}) collective-permute-start(bf16[48,3584]{1,0:T(8,128)(2,1)S(1)} %slice.231), channel_id=1, source_target_pairs={{0,32},{1,33},{2,34},{3,35},{4,36},{5,37},{6,38},{7,39},{8,40},{9,... | collective-permute-start | bytes 1032200 | tf_op jit(solution)/shard_map/ppermute | solution.py:63
  133.1 41.7 %all-to-all-start.1 = ((bf16[8,24,1792]{2,1,0:T(8,128)(2,1)}), bf16[8,24,1792]{2,1,0:T(8,128)(2,1)S(1)}, u32[]{:S(2)}, u32[]{:S(2)}) async-start(bf16[8,24,1792]{2,1,0:T(8,128)(2,1)} %bitcast.17), calls=%async_computation.1 | async-start | bytes 1376256 | tf_op jit(solution)/shard_map/all_to_all | solution.py:36
Sparse Core Ops, SparseCore 0:
  30.5 54.9 all-gather.2

commit v6 on v5

--- a/solution.py
+++ b/solution.py
@@ -90,11 +90,11 @@
 
 
 def in_terms(value):
-    high = value.astype(jnp.bfloat16)
-    rest = value - high.astype(jnp.float32)
-    middle = rest.astype(jnp.bfloat16)
-    low = (rest - middle.astype(jnp.float32)).astype(jnp.bfloat16)
-    return [high, middle, low]
+    rounded = lambda v: lax.reduce_precision(v, exponent_bits=8, mantissa_bits=7)
+    high = rounded(value)
+    middle = rounded(value - high)
+    low = rounded(value - high - middle)
+    return [term.astype(jnp.bfloat16) for term in (high, middle, low)]
 
 
 def on_device(act_down, act_up, routes_down, routes_up, norm_gain, router_w, w_gate, w_up, w_down):

time: 184 us -> 184 us (level)
  no operation moved by 1% of the time
where the time goes in v6:
time: 184 us
  waiting for transfers between devices  92.8 us (50%)
  starting transfers between devices  52.5 us (29%)
  between operations  14.7 us (8%)
  matrix products  13.1 us (7%)
  other arithmetic  6.67 us (4%)
  local copies, waits for them, and re-layouts  3.93 us (2%)
    all_to_all x1, waiting for transfers between devices, across_sections(): lax.all_to_all(chunks, ('pipe', 'expert'), split_axis=0, concat_axis=0, t...  35.9 us
    all_to_all x1, waiting for transfers between devices, across_groups(): lax.all_to_all(chunks, 'expert', split_axis=0, concat_axis=0, tiled=True,...  30.2 us
    ppermute x6, starting transfers between devices, facing(): return lax.ppermute(block, ('pipe', 'expert'), route)  19.4 us
    ppermute x6, waiting for transfers between devices, facing(): return lax.ppermute(block, ('pipe', 'expert'), route)  17.7 us
    ppermute x3, starting transfers between devices, other_core(): return lax.ppermute(block, ('pipe', 'expert'), route)  11.6 us
    all_to_all x1, starting transfers between devices, across_groups(): lax.all_to_all(chunks, 'expert', split_axis=0, concat_axis=0, tiled=True,...  10.9 us
    dot_general x7, matrix products, on_device(): dot = lambda a, b: jnp.dot(a, b, preferred_element_type=jnp.float32)  10.8 us
    ppermute x3, waiting for transfers between devices, other_core(): return lax.ppermute(block, ('pipe', 'expert'), route)  8.29 us
  transfers between devices with their start and end apart: 13, of which 7 were waited for; matrix products, arithmetic and copies ran while one was open for 8% of the time, Pallas kernels for 0%

profile of v6, /device:TPU:1, one launch (start us, length us, event | category | flops | bytes accessed | tf_op | source)
XLA Modules:
  0.0 183.7 jit_solution(43703334508135001)
XLA Ops:
  7.2 1.8 pad_maximum_fusion.1
  9.0 5.2 %collective-permute-start.3 = (bf16[3584,256]{1,0:T(8,128)(2,1)S(1)}, bf16[3584,256]{1,0:T(8,128)(2,1)}, u32[]{:S(2)}, u32[]{:S(2)}) collective-permute-start(bf16[3584,256]{1,0:T(8,128)(2,1)S(1)} %pad_maximum_fusion.1), channel_id=1, source_target_pairs={{0,1},{1,0},{2,3},{3,2},{4,5},{5,4},{6,7},{7,6},{8,9},{9,8},{10,11... | collective-permute-start | bytes 5505032 | tf_op jit(solution)/shard_map/ppermute | solution.py:53
  15.5 1.2 convolution_convert_fusion.1
  16.7 10.9 %all-to-all-start = ((bf16[4,24,3584]{2,1,0:T(8,128)(2,1)}), bf16[4,24,3584]{2,1,0:T(8,128)(2,1)S(1)}, u32[]{:S(2)}, u32[]{:S(2)}) async-start(bf16[4,24,3584]{2,1,0:T(8,128)(2,1)} %bitcast.8), calls=%async_computation | async-start | bytes 1376256 | tf_op jit(solution)/shard_map/all_to_all | solution.py:24
  27.5 0.7 all-gather.3.cloned.1.call-update
  30.1 1.9 %collective-permute-start = (bf16[16,3840]{1,0:T(8,128)(2,1)S(1)}, bf16[16,3840]{1,0:T(8,128)(2,1)S(1)}, u32[]{:S(2)}, u32[]{:S(2)}) collective-permute-start(bf16[16,3840]{1,0:T(8,128)(2,1)S(1)} %get-tuple-element.51), channel_id=1, source_target_pairs={{0,32},{1,33},{2,34},{3,35},{4,36},{5,37},{6,38},{7,39},{8,40},{9,... | collective-permute-start | bytes 368648 | tf_op jit(solution)/shard_map/ppermute | solution.py:63
  32.6 0.7 collective-permute-done
  33.3 30.2 %all-to-all-done = bf16[4,24,3584]{2,1,0:T(8,128)(2,1)S(1)} async-done(((bf16[4,24,3584]{2,1,0:T(8,128)(2,1)}), bf16[4,24,3584]{2,1,0:T(8,128)(2,1)S(1)}, u32[]{:S(2)}, u32[]{:S(2)}) %all-to-all-start) | async-done | bytes 688160 | tf_op jit(solution)/shard_map/all_to_all | solution.py:24
  63.5 1.9 %collective-permute-start.4 = (bf16[96,3584]{1,0:T(8,128)(2,1)S(1)}, bf16[96,3584]{1,0:T(8,128)(2,1)}, u32[]{:S(2)}, u32[]{:S(2)}) collective-permute-start(bf16[96,3584]{1,0:T(8,128)(2,1)S(1)} %bitcast.87), channel_id=1, source_target_pairs={{0,4},{1,5},{2,6},{3,7},{4,0},{5,1},{6,2},{7,3},{8,12},{9,13},{10,... | collective-permute-start | bytes 2064392 | tf_op jit(solution)/shard_map/ppermute | solution.py:53
  66.0 2.7 %collective-permute-start.2 = (bf16[96,3584]{1,0:T(8,128)(2,1)S(1)}, bf16[96,3584]{1,0:T(8,128)(2,1)}, u32[]{:S(2)}, u32[]{:S(2)}) collective-permute-start(bf16[96,3584]{1,0:T(8,128)(2,1)S(1)} %bitcast.88), channel_id=1, source_target_pairs={{0,7},{1,6},{2,5},{3,4},{4,3},{5,2},{6,1},{7,0},{8,15},{9,14},{10,... | collective-permute-start | bytes 2064392 | tf_op jit(solution)/shard_map/ppermute | solution.py:53
  68.6 3.8 %collective-permute-start.1 = (bf16[96,3584]{1,0:T(8,128)(2,1)S(1)}, bf16[96,3584]{1,0:T(8,128)(2,1)}, u32[]{:S(2)}, u32[]{:S(2)}) collective-permute-start(bf16[96,3584]{1,0:T(8,128)(2,1)S(1)} %bitcast.89), channel_id=1, source_target_pairs={{0,3},{1,2},{2,1},{3,0},{4,7},{5,6},{6,5},{7,4},{8,11},{9,10},{10,... | collective-permute-start | bytes 2064392 | tf_op jit(solution)/shard_map/ppermute | solution.py:53
  72.5 1.8 pad_maximum_fusion
  74.2 7.5 %collective-permute-done.4 = bf16[96,3584]{1,0:T(8,128)(2,1)} collective-permute-done((bf16[96,3584]{1,0:T(8,128)(2,1)S(1)}, bf16[96,3584]{1,0:T(8,128)(2,1)}, u32[]{:S(2)}, u32[]{:S(2)}) %collective-permute-start.4) | collective-permute-done | bytes 688160 | tf_op jit(solution)/shard_map/ppermute | solution.py:53
  81.7 2.0 %fusion.5 = f32[192,512]{1,0:T(8,128)S(1)} fusion(bf16[3584,512]{1,0:T(8,128)(2,1)S(1)} %pad_maximum_fusion, bf16[96,3584]{1,0:T(8,128)(2,1)} %collective-permute-done.4, bf16[96,3584]{1,0:T(8,128)(2,1)S(1)} %bitcast.90), kind=kOutput, calls=%fused_computation.10 | convolution fusion | flops 707395584 | bytes 5439488 | tf_op jit(solution)/shard_map/dot_general | solution.py:144
  84.0 5.9 %collective-permute-start.6 = (bf16[16,3840]{1,0:T(8,128)(2,1)S(1)}, bf16[16,3840]{1,0:T(8,128)(2,1)S(1)}, u32[]{:S(2)}, u32[]{:S(2)}) collective-permute-start(bf16[16,3840]{1,0:T(8,128)(2,1)S(1)} %get-tuple-element.21), channel_id=1, source_target_pairs={{0,480},{32,64},{64,32},{96,128},{128,96},{160,192},{192,160},{224... | collective-permute-start | bytes 368648 | tf_op jit(solution)/shard_map/ppermute | solution.py:43
  90.1 8.0 %collective-permute-done.2 = bf16[96,3584]{1,0:T(8,128)(2,1)} collective-permute-done((bf16[96,3584]{1,0:T(8,128)(2,1)S(1)}, bf16[96,3584]{1,0:T(8,128)(2,1)}, u32[]{:S(2)}, u32[]{:S(2)}) %collective-permute-start.2) | collective-permute-done | bytes 688160 | tf_op jit(solution)/shard_map/ppermute | solution.py:53
  98.0 3.3 %fusion.1 = f32[192,512]{1,0:T(8,128)S(1)} fusion(bf16[3584,512]{1,0:T(8,128)(2,1)} %copy-done.2, bf16[96,3584]{1,0:T(8,128)(2,1)} %collective-permute-done.2, bf16[96,3584]{1,0:T(8,128)(2,1)} %collective-permute-done.1), kind=kOutput, calls=%fused_computation.6 | convolution fusion | flops 707395584 | bytes 5439488 | tf_op jit(solution)/shard_map/dot_general | solution.py:144
  101.8 3.9 %collective-permute-start.5 = (bf16[192,256]{1,0:T(8,128)(2,1)S(1)}, bf16[192,256]{1,0:T(8,128)(2,1)S(1)}, u32[]{:S(2)}, u32[]{:S(2)}) collective-permute-start(bf16[192,256]{1,0:T(8,128)(2,1)S(1)} %copy_bitcast_fusion), channel_id=1, source_target_pairs={{0,3},{1,2},{2,1},{3,0},{4,7},{5,6},{6,5},{7,4},{8,11},{9,10},{10,... | collective-permute-start | bytes 294920 | tf_op jit(solution)/shard_map/ppermute | solution.py:53
  105.8 2.2 %collective-permute-done.5 = bf16[192,256]{1,0:T(8,128)(2,1)S(1)} collective-permute-done((bf16[192,256]{1,0:T(8,128)(2,1)S(1)}, bf16[192,256]{1,0:T(8,128)(2,1)S(1)}, u32[]{:S(2)}, u32[]{:S(2)}) %collective-permute-start.5) | collective-permute-done | bytes 98336 | tf_op jit(solution)/shard_map/ppermute | solution.py:53
  108.3 2.9 %convolution_convert_fusion = bf16[96,3584]{1,0:T(8,128)(2,1)S(1)} fusion(bf16[512,3584]{1,0:T(8,128)(2,1)} %bitcast.79, bf16[192,512]{1,0:T(8,128)(2,1)S(1)} %convolution_convert_fusion.2), kind=kOutput, calls=%fused_computation | convolution fusion | flops 352665600 | bytes 4456448 | tf_op jit(solution)/shard_map/dot_general | solution.py:144
  111.3 1.9 %collective-permute-start.9 = (bf16[48,3584]{1,0:T(8,128)(2,1)S(1)}, bf16[48,3584]{1,0:T(8,128)(2,1)S(1)}, u32[]{:S(2)}, u32[]{:S(2)}) collective-permute-start(bf16[48,3584]{1,0:T(8,128)(2,1)S(1)} %get-tuple-element.39), channel_id=1, source_target_pairs={{0,4},{1,5},{2,6},{3,7},{4,0},{5,1},{6,2},{7,3},{8,12},{9,13},{10,... | collective-permute-start | bytes 1032200 | tf_op jit(solution)/shard_map/ppermute | solution.py:53
  113.2 7.7 %collective-permute-start.7 = (bf16[48,3584]{1,0:T(8,128)(2,1)S(1)}, bf16[48,3584]{1,0:T(8,128)(2,1)S(1)}, u32[]{:S(2)}, u32[]{:S(2)}) collective-permute-start(bf16[48,3584]{1,0:T(8,128)(2,1)S(1)} %get-tuple-element.40), channel_id=1, source_target_pairs={{0,36},{1,37},{2,38},{3,39},{4,32},{5,33},{6,34},{7,35},{8,44},{9,... | collective-permute-start | bytes 1032200 | tf_op jit(solution)/shard_map/ppermute | solution.py:63
  121.0 0.7 fusion.50
  121.8 1.9 %collective-permute-start.8 = (bf16[48,3584]{1,0:T(8,128)(2,1)S(1)}, bf16[48,3584]{1,0:T(8,128)(2,1)S(1)}, u32[]{:S(2)}, u32[]{:S(2)}) collective-permute-start(bf16[48,3584]{1,0:T(8,128)(2,1)S(1)} %slice.231), channel_id=1, source_target_pairs={{0,32},{1,33},{2,34},{3,35},{4,36},{5,37},{6,38},{7,39},{8,40},{9,... | collective-permute-start | bytes 1032200 | tf_op jit(solution)/shard_map/ppermute | solution.py:63
  123.8 7.6 %collective-permute-done.7 = bf16[48,3584]{1,0:T(8,128)(2,1)S(1)} collective-permute-done((bf16[48,3584]{1,0:T(8,128)(2,1)S(1)}, bf16[48,3584]{1,0:T(8,128)(2,1)S(1)}, u32[]{:S(2)}, u32[]{:S(2)}) %collective-permute-start.7) | collective-permute-done | bytes 344096 | tf_op jit(solution)/shard_map/ppermute | solution.py:63
  131.4 0.4 fusion.17
  131.8 1.2 fusion
  133.1 4.7 %all-to-all-start.1 = ((bf16[8,24,1792]{2,1,0:T(8,128)(2,1)}), bf16[8,24,1792]{2,1,0:T(8,128)(2,1)S(1)}, u32[]{:S(2)}, u32[]{:S(2)}) async-start(bf16[8,24,1792]{2,1,0:T(8,128)(2,1)} %bitcast.17), calls=%async_computation.1 | async-start | bytes 1376256 | tf_op jit(solution)/shard_map/all_to_all | solution.py:36
  138.9 35.9 %all-to-all-done.1 = bf16[8,24,1792]{2,1,0:T(8,128)(2,1)S(1)} async-done(((bf16[8,24,1792]{2,1,0:T(8,128)(2,1)}), bf16[8,24,1792]{2,1,0:T(8,128)(2,1)S(1)}, u32[]{:S(2)}, u32[]{:S(2)}) %all-to-all-start.1) | async-done | bytes 688160 | tf_op jit(solution)/shard_map/all_to_all | solution.py:36
  175.2 0.3 fusion.81
  175.5 0.7 fusion.44
  176.2 0.7 fusion.45
  (126 shorter events, 6.8 us)
Async XLA Ops:
  7.2 21.1 %copy-start = (bf16[1,3584,4]{1,2,0:T(4,128)(2,1)S(1)}, bf16[1,3584,4]{1,2,0:T(4,128)(2,1)}, u32[]{:S(2)}) copy-start(bf16[1,3584,4]{1,2,0:T(4,128)(2,1)} %param.14) | copy-start | bytes 86020
  7.2 7.0 %copy-start.3 = (bf16[1,16,3584]{2,1,0:T(8,128)(2,1)S(1)}, bf16[1,16,3584]{2,1,0:T(8,128)(2,1)}, u32[]{:S(2)}) copy-start(bf16[1,16,3584]{2,1,0:T(8,128)(2,1)} %param.10) | copy-start | bytes 344068
  7.2 7.2 %copy-start.4 = (bf16[1,16,3584]{2,1,0:T(8,128)(2,1)S(1)}, bf16[1,16,3584]{2,1,0:T(8,128)(2,1)}, u32[]{:S(2)}) copy-start(bf16[1,16,3584]{2,1,0:T(8,128)(2,1)} %param.9) | copy-start | bytes 344068
  7.2 7.3 %copy-start.6 = (s32[1,16,2]{1,2,0:T(2,128)S(1)}, s32[1,16,2]{1,2,0:T(2,128)}, u32[]{:S(2)}) copy-start(s32[1,16,2]{1,2,0:T(2,128)} %param.12) | copy-start | bytes 388
  7.2 7.5 %copy-start.7 = (s32[1,16,2]{1,2,0:T(2,128)S(1)}, s32[1,16,2]{1,2,0:T(2,128)}, u32[]{:S(2)}) copy-start(s32[1,16,2]{1,2,0:T(2,128)} %param.11) | copy-start | bytes 388
  7.2 8.1 %copy-start.5 = (f32[1,3584]{1,0:T(1,128)S(1)}, f32[1,3584]{1,0:T(1,128)}, u32[]{:S(2)}) copy-start(f32[1,3584]{1,0:T(1,128)} %param.13) | copy-start | bytes 43012
  9.0 63.4 %collective-permute-start.3 = (bf16[3584,256]{1,0:T(8,128)(2,1)S(1)}, bf16[3584,256]{1,0:T(8,128)(2,1)}, u32[]{:S(2)}, u32[]{:S(2)}) collective-permute-start(bf16[3584,256]{1,0:T(8,128)(2,1)S(1)} %pad_maximum_fusion.1), channel_id=1, source_target_pairs={{0,1},{1,0},{2,3},{3,2},{4,5},{5,4},{6,7},{7,6},{8,9},{9,8},{10,11... | collective-permute-start | bytes 5505032 | tf_op jit(solution)/shard_map/ppermute | solution.py:53
  16.7 46.9 %all-to-all-start = ((bf16[4,24,3584]{2,1,0:T(8,128)(2,1)}), bf16[4,24,3584]{2,1,0:T(8,128)(2,1)S(1)}, u32[]{:S(2)}, u32[]{:S(2)}) async-start(bf16[4,24,3584]{2,1,0:T(8,128)(2,1)} %bitcast.8), calls=%async_computation | async-start | bytes 1376256 | tf_op jit(solution)/shard_map/all_to_all | solution.py:24
  27.5 70.5 %all-gather.3.cloned.1.call-start = ((), (), s32[]{:S(2)}) async-start(), calls=%async_computation.2 | async-start | bytes 4587520 | tf_op jit(solution)/shard_map/all_gather | solution.py:69
  30.1 3.2 %collective-permute-start = (bf16[16,3840]{1,0:T(8,128)(2,1)S(1)}, bf16[16,3840]{1,0:T(8,128)(2,1)S(1)}, u32[]{:S(2)}, u32[]{:S(2)}) collective-permute-start(bf16[16,3840]{1,0:T(8,128)(2,1)S(1)} %get-tuple-element.51), channel_id=1, source_target_pairs={{0,32},{1,33},{2,34},{3,35},{4,36},{5,37},{6,38},{7,39},{8,40},{9,... | collective-permute-start | bytes 368648 | tf_op jit(solution)/shard_map/ppermute | solution.py:63
  63.5 18.2 %collective-permute-start.4 = (bf16[96,3584]{1,0:T(8,128)(2,1)S(1)}, bf16[96,3584]{1,0:T(8,128)(2,1)}, u32[]{:S(2)}, u32[]{:S(2)}) collective-permute-start(bf16[96,3584]{1,0:T(8,128)(2,1)S(1)} %bitcast.87), channel_id=1, source_target_pairs={{0,4},{1,5},{2,6},{3,7},{4,0},{5,1},{6,2},{7,3},{8,12},{9,13},{10,... | collective-permute-start | bytes 2064392 | tf_op jit(solution)/shard_map/ppermute | solution.py:53
  66.0 32.0 %collective-permute-start.2 = (bf16[96,3584]{1,0:T(8,128)(2,1)S(1)}, bf16[96,3584]{1,0:T(8,128)(2,1)}, u32[]{:S(2)}, u32[]{:S(2)}) collective-permute-start(bf16[96,3584]{1,0:T(8,128)(2,1)S(1)} %bitcast.88), channel_id=1, source_target_pairs={{0,7},{1,6},{2,5},{3,4},{4,3},{5,2},{6,1},{7,0},{8,15},{9,14},{10,... | collective-permute-start | bytes 2064392 | tf_op jit(solution)/shard_map/ppermute | solution.py:53
  68.6 29.4 %collective-permute-start.1 = (bf16[96,3584]{1,0:T(8,128)(2,1)S(1)}, bf16[96,3584]{1,0:T(8,128)(2,1)}, u32[]{:S(2)}, u32[]{:S(2)}) collective-permute-start(bf16[96,3584]{1,0:T(8,128)(2,1)S(1)} %bitcast.89), channel_id=1, source_target_pairs={{0,3},{1,2},{2,1},{3,0},{4,7},{5,6},{6,5},{7,4},{8,11},{9,10},{10,... | collective-permute-start | bytes 2064392 | tf_op jit(solution)/shard_map/ppermute | solution.py:53
  74.2 7.5 %copy-start.2 = (bf16[3584,512]{1,0:T(8,128)(2,1)}, bf16[3584,512]{1,0:T(8,128)(2,1)S(1)}, u32[]{:S(2)}) copy-start(bf16[3584,512]{1,0:T(8,128)(2,1)S(1)} %pad_maximum_fusion) | copy-start | bytes 11010052
  84.0 21.8 %collective-permute-start.6 = (bf16[16,3840]{1,0:T(8,128)(2,1)S(1)}, bf16[16,3840]{1,0:T(8,128)(2,1)S(1)}, u32[]{:S(2)}, u32[]{:S(2)}) collective-permute-start(bf16[16,3840]{1,0:T(8,128)(2,1)S(1)} %get-tuple-element.21), channel_id=1, source_target_pairs={{0,480},{32,64},{64,32},{96,128},{128,96},{160,192},{192,160},{224... | collective-permute-start | bytes 368648 | tf_op jit(solution)/shard_map/ppermute | solution.py:43
  101.8 6.2 %collective-permute-start.5 = (bf16[192,256]{1,0:T(8,128)(2,1)S(1)}, bf16[192,256]{1,0:T(8,128)(2,1)S(1)}, u32[]{:S(2)}, u32[]{:S(2)}) collective-permute-start(bf16[192,256]{1,0:T(8,128)(2,1)S(1)} %copy_bitcast_fusion), channel_id=1, source_target_pairs={{0,3},{1,2},{2,1},{3,0},{4,7},{5,6},{6,5},{7,4},{8,11},{9,10},{10,... | collective-permute-start | bytes 294920 | tf_op jit(solution)/shard_map/ppermute | solution.py:53
  108.3 12.6 %copy-start.1 = (bf16[1,512,3584]{2,1,0:T(8,128)(2,1)S(1)}, bf16[1,512,3584]{2,1,0:T(8,128)(2,1)}, u32[]{:S(2)}) copy-start(bf16[1,512,3584]{2,1,0:T(8,128)(2,1)} %all-gather.3.cloned.1.call-done) | copy-start | bytes 11010052
  111.3 12.4 %collective-permute-start.9 = (bf16[48,3584]{1,0:T(8,128)(2,1)S(1)}, bf16[48,3584]{1,0:T(8,128)(2,1)S(1)}, u32[]{:S(2)}, u32[]{:S(2)}) collective-permute-start(bf16[48,3584]{1,0:T(8,128)(2,1)S(1)} %get-tuple-element.39), channel_id=1, source_target_pairs={{0,4},{1,5},{2,6},{3,7},{4,0},{5,1},{6,2},{7,3},{8,12},{9,13},{10,... | collective-permute-start | bytes 1032200 | tf_op jit(solution)/shard_map/ppermute | solution.py:53
  113.2 18.1 %collective-permute-start.7 = (bf16[48,3584]{1,0:T(8,128)(2,1)S(1)}, bf16[48,3584]{1,0:T(8,128)(2,1)S(1)}, u32[]{:S(2)}, u32[]{:S(2)}) collective-permute-start(bf16[48,3584]{1,0:T(8,128)(2,1)S(1)} %get-tuple-element.40), channel_id=1, source_target_pairs={{0,36},{1,37},{2,38},{3,39},{4,32},{5,33},{6,34},{7,35},{8,44},{9,... | collective-permute-start | bytes 1032200 | tf_op jit(solution)/shard_map/ppermute | solution.py:63
  121.8 9.6 %collective-permute-start.8 = (bf16[48,3584]{1,0:T(8,128)(2,1)S(1)}, bf16[48,3584]{1,0:T(8,128)(2,1)S(1)}, u32[]{:S(2)}, u32[]{:S(2)}) collective-permute-start(bf16[48,3584]{1,0:T(8,128)(2,1)S(1)} %slice.231), channel_id=1, source_target_pairs={{0,32},{1,33},{2,34},{3,35},{4,36},{5,37},{6,38},{7,39},{8,40},{9,... | collective-permute-start | bytes 1032200 | tf_op jit(solution)/shard_map/ppermute | solution.py:63
  133.1 41.7 %all-to-all-start.1 = ((bf16[8,24,1792]{2,1,0:T(8,128)(2,1)}), bf16[8,24,1792]{2,1,0:T(8,128)(2,1)S(1)}, u32[]{:S(2)}, u32[]{:S(2)}) async-start(bf16[8,24,1792]{2,1,0:T(8,128)(2,1)} %bitcast.17), calls=%async_computation.1 | async-start | bytes 1376256 | tf_op jit(solution)/shard_map/all_to_all | solution.py:36
Sparse Core Ops, SparseCore 0:
  30.5 54.9 all-gather.2
